TPU v7x, 32 devices: a whole 2x2x4 slice. The times are simulated.
32 devices in a mesh: ckpt: 8 (over z, core), rows: 4 (over y, x).
Axes of the slice: x: 2, y: 2, z: 4, core: 2. Of those that a mesh axis runs over, the one named last changes fastest.
Arguments:
- deltas: bfloat16 [8, 4096, 14336], P('ckpt', 'rows'), may hold values from -24 to 24
- start_basis: bfloat16 [8, 14336, 64], P('ckpt', 'rows'), may hold values from -6 to 6
- edit_order: int32 [8], replicated, may hold values from 0 to 7, each once
Outputs:
- merged: bfloat16 [4096, 14336], P('rows', 'ckpt')
Inputs may be any that keep to these rules, and one draw needn't show every extreme that they name: `edit_order`: a permutation: each of 0 to 7 appears once.
All inputs are finite; a program needn't handle non-finite values.
Results may differ from a plain program's by a relative error of at most 0.034.
Values may be sent and summed in bfloat16 or wider, within the bound.
No kernel may reach another device: no remote copies, remote signals or barrier semaphores. Data moves between devices by JAX's collectives and lax.ppermute only.
A program may use at most 128 MiB of HBM per device.

v0:
```python
import functools
import math

import jax
import jax.numpy as jnp
from jax import lax
from jax.experimental import pallas as pl
from jax.experimental.pallas import tpu as pltpu
from jax.sharding import PartitionSpec as P

NS_ITERS = 4
LIFT = 2.0**60
VMEM_BYTES = 24 * 1024 * 1024
DELTA_VMEM_BYTES = 22 * 1024 * 1024
SHORT = pl.CostEstimate(flops=1024, bytes_accessed=1024, transcendentals=0)
F32 = jnp.float32
BF16 = jnp.bfloat16
NN = (((1,), (0,)), ((), ()))
NT = (((1,), (1,)), ((), ()))
TN = (((0,), (0,)), ((), ()))


def dot(a, b, dims=NN):
    return lax.dot_general(a, b, dims, preferred_element_type=F32)


def halves(x):
    high = x.astype(BF16)
    return high, (x - high.astype(F32)).astype(BF16)


def dot_wide(a, b, dims=NN):
    a_high, a_low = halves(a)
    b_high, b_low = halves(b)
    return dot(a_high, b_high, dims) + (dot(a_high, b_low, dims) + dot(a_low, b_high, dims))


def power_scale(peak, root=False):
    scale = jnp.ones_like(peak)
    full = jnp.ones_like(peak)
    for exponent in (64, 32, 16, 8, 4, 2, 1):
        big = peak * full >= 2.0**exponent
        full = jnp.where(big, full * 2.0**-exponent, full)
        scale = jnp.where(big, scale * 2.0 ** -(exponent // 2), scale)
    for exponent in (64, 32, 16, 8, 4, 2, 1):
        small = peak * full * 2.0**exponent < 2.0
        full = jnp.where(small, full * 2.0**exponent, full)
        scale = jnp.where(small, scale * 2.0 ** (exponent // 2), scale)
    return scale if root else full


def inverse_factor(gram, work):
    rank = gram.shape[0]
    index = lax.broadcasted_iota(jnp.int32, (rank, 1), 0)
    lane = lax.broadcasted_iota(jnp.int32, (rank, 2 * rank), 1)
    work[:, :rank] = (lax.broadcasted_iota(jnp.int32, (rank, rank), 1) == index).astype(F32)
    work[:, rank:] = gram
    tiles = [work[at:at + 8, :] for at in range(0, rank, 8)]
    below = lax.broadcasted_iota(jnp.int32, (8, 1), 0)
    for k in range(rank - 1):
        at = rank + k
        first, inner = divmod(k, 8)
        row = tiles[first][inner:inner + 1, :]
        row = row * (1.0 / row[:, at:at + 1])
        for number in range(first, len(tiles)):
            column = tiles[number][:, at:at + 1]
            if number == first:
                column = jnp.where(below > inner, column, 0.0)
            tiles[number] = tiles[number] - column * row
    table = jnp.concatenate(tiles, axis=0)
    pivots = jnp.sum(jnp.where(lane == index + rank, table, 0.0), axis=1, keepdims=True)
    work[...] = table * lax.rsqrt(pivots)
    return work[:, :rank]


def slot_columns(place, gap, width):
    return pl.ds(pl.multiple_of((place ^ gap) * width, 128), width)


def add_products(place, gaps, pieces, delta, part):
    rows = delta.shape[0]
    block = min(256, rows)
    for start in range(0, rows, block):
        total = part[:, start:start + block]
        for gap, piece in zip(gaps, pieces):
            columns = slot_columns(place, gap, piece.shape[1])
            total += dot(piece[...], delta[start:start + block, columns], NT)
        part[:, start:start + block] = total


def part_kernel(gaps, fresh, place_ref, delta, *refs):
    pieces, refs = refs[:len(gaps)], refs[len(gaps):]
    out = refs[-1]
    out[...] = jnp.zeros_like(out) if fresh else refs[0][...]
    add_products(place_ref[0], gaps, pieces, delta, out)


def biggest(pieces):
    peak = None
    for piece in pieces:
        most = jnp.max(jnp.abs(piece[...]).astype(F32), keepdims=True)
        peak = most if peak is None else jnp.maximum(peak, most)
    return peak


def first_kernel(gaps, count, place_ref, delta, *refs):
    pieces, refs = refs[:count], refs[count:]
    before, out, part = refs
    part[...] = before[...]
    scale = power_scale(biggest(pieces)) * LIFT
    add_products(place_ref[0], gaps, [pieces[gap] for gap in gaps], delta, part)
    out[...] = (part[...] * scale).astype(BF16)


def second_kernel(gaps, count, place_ref, delta, *refs):
    pieces, refs = refs[:count], refs[count:]
    before, out, gram, part, work = refs
    part[...] = before[...]
    peak = biggest(pieces)
    scale = power_scale(peak)
    second = power_scale(peak * (1.0 / LIFT), root=True)
    right_gram = None
    for piece in pieces:
        scaled = (piece[...].astype(F32) * scale).astype(BF16)
        term = dot(scaled, scaled, NT)
        right_gram = term if right_gram is None else right_gram + term
    inverse = inverse_factor(right_gram, work) * second
    add_products(place_ref[0], gaps, [pieces[gap] for gap in gaps], delta, part)
    left = dot_wide(inverse, part[...] * scale).astype(BF16)
    out[...] = left
    gram[...] = dot(left, left, NT)


def delta_call(kernel, place, delta, args, out_shape, scratch, name):
    vmem = pl.BlockSpec(memory_space=pltpu.VMEM)
    return pl.pallas_call(
        kernel,
        in_specs=[pl.BlockSpec(memory_space=pltpu.SMEM)] + [vmem] * (1 + len(args)),
        out_specs=[vmem] * len(out_shape),
        out_shape=out_shape,
        scratch_shapes=scratch,
        compiler_params=pltpu.CompilerParams(vmem_limit_bytes=DELTA_VMEM_BYTES),
        name=name,
        cost_estimate=SHORT,
    )(place, pltpu.with_memory_space_constraint(delta, pltpu.VMEM), *args)


def left_sweep(kernel, place, delta, own, early, out_shape, scratch, name):
    rank, width = own.shape
    rows = delta.shape[0]
    count = lax.axis_size("rows")
    near = tuple(gap for gap in range(1, count) if not gap & (gap - 1))
    far = tuple(gap for gap in range(1, count) if gap & (gap - 1))

    def add(gaps, args):
        return delta_call(
            functools.partial(part_kernel, gaps, gaps[0] == 0), place, delta, args,
            [jax.ShapeDtypeStruct((rank, rows), F32)], [], name + "_part",
        )[0]

    arrived = [permute(own, "rows", gap) for gap in near]
    if early:
        part = add((0,), [own])
        part, *arrived = together(part, *arrived)
    pieces = [own] + [None] * (count - 1)
    for gap, piece in zip(near, arrived):
        pieces[gap] = piece
    forward(pieces, "rows")
    part = add(near, [*arrived, part]) if early else add((0, *near), [own, *arrived])
    return delta_call(
        functools.partial(kernel, far, count), place, delta, [*pieces, part], out_shape,
        [pltpu.VMEM((rank, rows), F32)] + scratch, name,
    )


def right_kernel_first(gap, place_ref, delta, left, out):
    width = out.shape[1]
    step = 1792 if width % 1792 == 0 else width
    for start in range(0, width, step):
        at = pl.ds(pl.multiple_of((place_ref[0] ^ gap) * width + start, 128), step)
        out[:, start:start + step] = dot(left[...], delta[:, at]).astype(BF16)


def right_kernel_second(gap, real, place_ref, delta, left, out):
    groups, _, size = out.shape
    slot = place_ref[0] ^ gap
    start = slot_start(slot, size, real)
    inside = lax.broadcasted_iota(jnp.int32, (1, size), 1) + start >= slot * size
    for group in range(groups):
        at = pl.ds(pl.multiple_of(group * real + start, 128), size)
        value = dot(left[...], delta[:, at])
        out[group] = jnp.where(inside, value, 0.0).astype(BF16)


def own_kernel_second(count, real, place_ref, delta, left, *refs):
    grams, (out, unit, inverse, work) = refs[:count], refs[count:]
    right_kernel_second(0, real, place_ref, delta, left, out)
    total = grams[0][...]
    for gram in grams[1:]:
        total = total + gram[...]
    factor = inverse_factor(total, work)
    inverse[...] = factor
    high_part, low_part = halves(factor)
    unit[...] = (dot(high_part, left[...]) + dot(low_part, left[...])).astype(BF16)


def slot_start(slot, size, real):
    return jnp.minimum(slot * size, real - size)


def small_call(kernel, out_shape, args, scratch=(), name=None, scalars=0):
    spec = lambda i: pl.BlockSpec(memory_space=pltpu.SMEM if i < scalars else pltpu.VMEM)
    return pl.pallas_call(
        kernel,
        in_specs=[spec(i) for i in range(len(args))],
        out_specs=[pl.BlockSpec(memory_space=pltpu.VMEM)] * len(out_shape),
        out_shape=out_shape,
        scratch_shapes=list(scratch),
        compiler_params=pltpu.CompilerParams(vmem_limit_bytes=VMEM_BYTES),
        name=name,
        cost_estimate=SHORT,
    )(*args)


def right_sum_kernel(count, *refs):
    parts, (total, gram) = refs[:count], refs[count:]
    result = None
    for group in range(total.shape[0]):
        value = parts[0][group].astype(F32)
        for part in parts[1:]:
            value = value + part[group].astype(F32)
        total[group] = value
        term = dot_wide(value, value, NT)
        result = term if result is None else result + term
    gram[...] = result


def right_kernel(count, groups, place_ref, weight_ref, total, left_inverse, *refs):
    grams, outs, (work,) = refs[:count], refs[count:count + groups], refs[count + groups:]
    gram = grams[0][...]
    for other in grams[1:]:
        gram = gram + other[...]
    factor = inverse_factor(gram, work)
    middle_high, middle_low = halves(weight_ref[0] * dot_wide(left_inverse[...], dot_wide(gram, factor, NT)))
    high, low = halves(factor)
    rank, size = total.shape[1:]
    for gap, out in enumerate(outs):
        value_high, value_low = halves(total[place_ref[0] ^ gap])
        out[:, :size] = (dot(high, value_high) + (dot(high, value_low) + dot(low, value_high))).astype(BF16)
        out[:, size:size + rank] = middle_high
        out[:, size + rank:] = middle_low


def grams_kernel(groups, place_ref, left_stack, *refs):
    pieces, (stack, middles, home, away, *slabs) = refs[:groups], refs[groups:]
    left_rows = slabs[0].shape[0]
    for gap, slab in enumerate(slabs):
        at = pl.multiple_of((place_ref[1] ^ gap) * left_rows, left_rows)
        slab[...] = dot(left_stack[pl.ds(at, left_rows), :], left_stack[...], NT).astype(BF16)
    rank = pieces[0].shape[0]
    size = stack.shape[1]
    place = place_ref[0]
    for gap, piece in enumerate(pieces):
        owner = place ^ gap
        stack[pl.ds(pl.multiple_of(owner * rank, rank), rank), :] = piece[:, :size]
        middles[owner] = piece[:, size:size + rank].astype(F32) + piece[:, size + rank:].astype(F32)
    for number in range(groups // 2):
        for out, gap in ((home, 2 * number), (away, 2 * number + 1)):
            at = pl.multiple_of((place ^ gap) * rank, rank)
            out[number] = dot(stack[pl.ds(at, rank), :], stack[...], NT).astype(BF16)


def fill_gram(place, pairs, gram):
    rank = pairs[0].shape[1]
    for number, pair in enumerate(pairs):
        for side in range(2):
            at = pl.multiple_of((place ^ (2 * number + side)) * rank, rank)
            gram[pl.ds(at, rank), :] = pair[side].astype(F32)


def polish(count, gram, product, spare, side):
    size = gram.shape[0]
    strip = min(512, size)
    eye = (
        lax.broadcasted_iota(jnp.int32, (size, size), 0) == lax.broadcasted_iota(jnp.int32, (size, size), 1)
    ).astype(F32)
    lead, tail = 1.5 / math.sqrt(count), -0.5 / (count * math.sqrt(count))
    product[...] = lead * eye + tail * gram[...]

    def multiply(a_ref, c_ref, lead, tail):
        def one(index, _):
            rows = pl.ds(pl.multiple_of(index * strip, strip), strip)
            a = a_ref[rows, :]
            c_ref[rows, :] = lead * a + tail * dot(a.astype(BF16), side[...])
            return 0

        lax.fori_loop(0, size // strip, one, 0)

    def step(index, _):
        first = index == 1
        before = jnp.where(first, lead, 1.5)
        after = jnp.where(first, tail, -0.5)
        side[...] = gram[...].astype(BF16)
        multiply(gram, spare, before, after)
        multiply(spare, gram, before, after)
        side[...] = gram[...].astype(BF16)
        multiply(product, product, 1.5, -0.5)
        return 0

    lax.fori_loop(1, NS_ITERS, step, 0)


def left_mix_kernel(count, ckpt_count, place_ref, *refs):
    slabs, (stack, middle, out, gram, product, spare, side) = refs[:count], refs[count:]
    slab_rows = slabs[0].shape[0]
    for gap, slab in enumerate(slabs):
        at = pl.multiple_of((place_ref[0] ^ gap) * slab_rows, slab_rows)
        gram[pl.ds(at, slab_rows), :] = slab[...].astype(F32)
    polish(ckpt_count, gram, product, spare, side)
    rank = middle.shape[1]
    for index in range(ckpt_count):
        rows = pl.ds(index * rank, rank)
        spare[rows, :] = dot_wide(jnp.transpose(middle[index]), product[rows, :])
    side[...] = spare[...].astype(BF16)
    out[...] = dot(side[...], stack[...]).astype(BF16)


def merge_kernel(count, ckpt_count, places_ref, mixed, *refs):
    pairs, refs = refs[:ckpt_count // 2], refs[ckpt_count // 2:]
    pieces, (out, gram, product, spare, side, wide) = refs[:count], refs[count:]
    real = out.shape[1]

    @pl.when(pl.program_id(0) == 0)
    def _():
        fill_gram(places_ref[0], pairs, gram)
        size = pieces[0].shape[1]
        wide[...] = jnp.zeros_like(wide)
        for gap, piece in enumerate(pieces):
            start = pl.multiple_of(slot_start(places_ref[1] ^ gap, size, real), 128)
            wide[:, pl.ds(start, size)] += piece[...]
        polish(ckpt_count, gram, product, spare, side)
        side[...] = product[...].astype(BF16)

    turned = jnp.transpose(dot(side[...], mixed[...])).astype(BF16)
    out[...] = dot(turned, wide[...]).astype(BF16)


def permute(value, axis, gap):
    count = lax.axis_size(axis)
    return lax.ppermute(value, axis, [(source, source ^ gap) for source in range(count)])


def spread(value, axis):
    return [value] + [permute(value, axis, gap) for gap in range(1, lax.axis_size(axis))]


def forward(got, axis):
    half = got[0].shape[0] // 2
    for gap in sorted(range(1, len(got)), key=lambda gap: bin(gap).count("1")):
        low, high = gap & -gap, 1 << (gap.bit_length() - 1)
        if low != high:
            got[gap] = jnp.concatenate([
                permute(got[gap ^ low][:half], axis, low), permute(got[gap ^ high][half:], axis, high)
            ])
    return got


def swap(values, axis):
    return [values[0]] + [permute(value, axis, gap) for gap, value in enumerate(values) if gap]


def right_sweep(call, left, count, small=()):
    parts = [None] * count
    for gap in range(count - 1, 0, -1):
        piece, left = together(call(gap, left), left)
        if small:
            left, *small = together(left, *small)
        parts[gap] = permute(piece, "rows", gap)
    if count > 2:
        left, parts[count - 1] = together(left, parts[count - 1])
    parts[0] = call(0, left, *small)
    return parts


def together(*values):
    return lax.optimization_barrier(values)


def add_up(values):
    return sum(value.astype(F32) for value in values)


def body(deltas, start_basis, edit_order):
    changes = deltas[0]
    start = jnp.transpose(start_basis[0])
    rank, width = start.shape
    rows, cols = changes.shape
    count = lax.axis_size("rows")
    groups = lax.axis_size("ckpt")
    row_place = lax.axis_index("rows").astype(jnp.int32)
    ckpt_place = lax.axis_index("ckpt").astype(jnp.int32)
    at_row = row_place[None]
    at_ckpt = ckpt_place[None]
    at_both = jnp.stack([ckpt_place, row_place])
    shape = jax.ShapeDtypeStruct
    square = shape((rank, rank), F32)
    work = pltpu.VMEM((rank, 2 * rank), F32)
    (left,) = left_sweep(
        first_kernel, at_row, changes, start, True, [shape((rank, rows), BF16)], [], "first_left"
    )
    parts = right_sweep(
        lambda gap, left: delta_call(
            functools.partial(right_kernel_first, gap), at_row, changes, [left], [shape((rank, width), BF16)], [],
            "first_right",
        )[0],
        left, count,
    )
    right = add_up(parts).astype(BF16)

    block = cols // groups
    padded = -(-block // (count * 128)) * 128
    left, left_gram = left_sweep(
        second_kernel, at_row, changes, right, True, [shape((rank, rows), BF16), square], [work], "second_left"
    )
    left_grams = spread(left_gram, "rows")

    def right_piece(gap, left, *grams):
        if gap:
            return delta_call(
                functools.partial(right_kernel_second, gap, block), at_row, changes, [left],
                [shape((groups, rank, padded), BF16)], [], "second_right",
            )[0]
        return delta_call(
            functools.partial(own_kernel_second, count, block), at_row, changes, [left, *grams],
            [shape((groups, rank, padded), BF16), shape((rank, rows), BF16), square], [work], "second_own",
        )

    parts = right_sweep(right_piece, left, count, left_grams)
    parts[0], left_unit, left_inverse = parts[0]
    left_unit, *arrived = together(left_unit, *parts[1:])
    parts[1:] = arrived
    left_stack = lax.all_gather(left_unit, "ckpt", axis=0, tiled=True)
    total, right_gram = small_call(
        functools.partial(right_sum_kernel, count), [shape((groups, rank, padded), F32), square], parts,
        name="right_sum",
    )
    position = jnp.sum(jnp.where(jnp.arange(groups) == ckpt_place, edit_order, 0))
    weight = (1 + position).astype(F32)[None] / groups
    leaving = small_call(
        functools.partial(right_kernel, count, groups), [shape((rank, padded + 2 * rank), BF16)] * groups,
        [at_ckpt, weight, total, left_inverse] + spread(right_gram, "rows"), [work], "right_unit", scalars=2,
    )
    pieces = swap(leaving, "ckpt")
    size = groups * rank
    table = pltpu.VMEM((size, size), F32)
    tables = [table, table, table, pltpu.VMEM((size, size), BF16)]
    slabs = shape((groups // 2, rank, size), BF16)
    right_stack, middles, home, away, *left_slabs = small_call(
        functools.partial(grams_kernel, groups),
        [shape((size, padded), BF16), shape((groups, rank, rank), F32), slabs, slabs]
        + [shape((size // count, size), BF16)] * count,
        [at_both, left_stack] + pieces, name="grams", scalars=1,
    )
    near = [permute(right_stack, "rows", gap) for gap in range(1, count) if not gap & (gap - 1)]
    pair_sum = add_up([home, permute(away, "ckpt", 1)]).astype(BF16)
    own = add_up([pair_sum[0]] + [permute(pair_sum[n], "ckpt", 2 * n) for n in range(1, groups // 2)]).astype(BF16)
    own, *held = together(own, *near, *left_slabs)
    near, left_slabs = held[:len(near)], held[len(near):]
    right_rows = add_up(spread(own, "rows")).astype(BF16)
    left_slab = add_up(swap(left_slabs, "rows")).astype(BF16)
    right_rows, left_slab = together(right_rows, left_slab)
    pair = jnp.stack([right_rows, permute(right_rows, "ckpt", 1)])
    pair, left_slab, *near = together(pair, left_slab, *near)
    right_pairs = [pair] + [permute(pair, "ckpt", gap) for gap in range(2, groups, 2)]
    left_slabs = spread(left_slab, "rows")
    right_all = [right_stack] + [None if gap & (gap - 1) else near.pop(0) for gap in range(1, count)]
    forward(right_all, "rows")

    (mixed,) = small_call(
        functools.partial(left_mix_kernel, count, groups), [shape((size, rows), BF16)],
        [at_row] + left_slabs + [left_stack, middles], tables, "left_mix", scalars=1,
    )
    step = min(512, rows)
    full = lambda value: pl.BlockSpec(value.shape, lambda i: (0,) * value.ndim)
    return pl.pallas_call(
        functools.partial(merge_kernel, count, groups),
        grid=(rows // step,),
        in_specs=[pl.BlockSpec(memory_space=pltpu.SMEM), pl.BlockSpec((size, step), lambda i: (0, i))]
        + [full(value) for value in right_pairs + right_all],
        out_specs=pl.BlockSpec((step, block), lambda i: (i, 0)),
        out_shape=shape((rows, block), BF16),
        scratch_shapes=tables + [pltpu.VMEM((size, block), BF16)],
        compiler_params=pltpu.CompilerParams(vmem_limit_bytes=VMEM_BYTES),
        name="merge",
        cost_estimate=SHORT,
    )(at_both, mixed, *right_pairs, *right_all)


def solution(mesh):
    return jax.shard_map(
        body,
        mesh=mesh,
        in_specs=(P("ckpt", "rows", None), P("ckpt", "rows", None), P()),
        out_specs=P("rows", "ckpt"),
        check_vma=False,
    )
```

profile of v0, /device:TPU:0, one launch (start us, length us, event | category | flops | bytes accessed | tf_op | source)
XLA Modules:
  0.0 224.1 jit_solution(1085413180797269830)
XLA Ops:
  6.5 3.0 %collective-permute-start.1 = (bf16[64,3584]{1,0:T(8,128)(2,1)}, bf16[64,3584]{1,0:T(8,128)(2,1)S(1)}, u32[]{:S(2)}, u32[]{:S(2)}) collective-permute-start(bf16[64,3584]{1,0:T(8,128)(2,1)} %bitcast.34), channel_id=1, source_target_pairs={{0,2},{1,3},{2,0},{3,1},{4,6},{5,7},{6,4},{7,5},{8,10},{9,11},{10,... | collective-permute-start | bytes 1376264 | tf_op jit(solution)/shard_map/ppermute | solution.py:350
  11.0 9.3 %copy-done = bf16[1,1024,14336]{2,1,0:T(8,128)(2,1)S(1)} copy-done((bf16[1,1024,14336]{2,1,0:T(8,128)(2,1)S(1)}, bf16[1,1024,14336]{2,1,0:T(8,128)(2,1)}, u32[]{:S(2)}) %copy-start) | copy-done | bytes 29360152
  24.4 4.5 %first_left_part.3.refs_4_ = f32[64,1024]{1,0:T(8,128)S(1)} custom-call(s32[1]{0:T(128)} %bitcast.1.place_ref, bf16[1024,14336]{1,0:T(8,128)(2,1)S(1)} %bitcast.21, bf16[64,3584]{1,0:T(8,128)(2,1)S(1)} %collective-permute-done.refs_0_.refs_1_, bf16[64,3584]{1,0:T(8,128)(2,1)S(1)} %collective-permute-done.1.refs_1_.refs_2_, f32[64,1024]{1,0:T(8,128)S(1)} %first_left_part.2.refs_2_), custom_call_target="tpu_custom_call" | custom-call | flops 1024 | bytes 1024 | tf_op jit(solution)/shard_map/first_left_part/pallas_call | solution.py:136
  30.9 2.4 %first_left.1.left = bf16[64,1024]{1,0:T(8,128)(2,1)S(1)} custom-call(s32[1]{0:T(128)} %bitcast.1.place_ref, bf16[1024,14336]{1,0:T(8,128)(2,1)S(1)} %bitcast.22, bf16[64,3584]{1,0:T(8,128)(2,1)S(1)} %bitcast.37, bf16[64,3584]{1,0:T(8,128)(2,1)S(1)} %collective-permute-done.refs_0_.refs_1_, bf16[64,3584]{1,0:T(8,128)(2,1)S(1)} %collective-permute-done.1.refs_1_.refs_2_, ...), custom_call_target="tpu_custom_call" | custom-call | flops 1024 | bytes 1024 | tf_op jit(solution)/shard_map/first_left/pallas_call | solution.py:136
  41.1 9.5 %collective-permute-done.4 = bf16[64,3584]{1,0:T(8,128)(2,1)S(1)} collective-permute-done((bf16[64,3584]{1,0:T(8,128)(2,1)S(1)}, bf16[64,3584]{1,0:T(8,128)(2,1)S(1)}, u32[]{:S(2)}, u32[]{:S(2)}) %collective-permute-start.4) | collective-permute-done | bytes 458784 | tf_op jit(solution)/shard_map/ppermute | solution.py:350
  51.9 4.8 %collective-permute-done.5 = bf16[64,3584]{1,0:T(8,128)(2,1)S(1)} collective-permute-done((bf16[64,3584]{1,0:T(8,128)(2,1)S(1)}, bf16[64,3584]{1,0:T(8,128)(2,1)S(1)}, u32[]{:S(2)}, u32[]{:S(2)}) %collective-permute-start.5) | collective-permute-done | bytes 458784 | tf_op jit(solution)/shard_map/ppermute | solution.py:350
  59.9 2.3 %second_left_part.2.refs_2_ = f32[64,1024]{1,0:T(8,128)S(1)} custom-call(s32[1]{0:T(128)} %bitcast.1.place_ref, bf16[1024,14336]{1,0:T(8,128)(2,1)S(1)} %bitcast.27, bf16[64,3584]{1,0:T(8,128)(2,1)S(1)} %add_convert_fusion.refs_0_), custom_call_target="tpu_custom_call" | custom-call | flops 1024 | bytes 1024 | tf_op jit(solution)/shard_map/second_left_part/pallas_call | solution.py:136
  62.2 7.9 %collective-permute-done.8.refs_1_.refs_2_ = bf16[64,3584]{1,0:T(8,128)(2,1)S(1)} collective-permute-done((bf16[64,3584]{1,0:T(8,128)(2,1)S(1)}, bf16[64,3584]{1,0:T(8,128)(2,1)S(1)}, u32[]{:S(2)}, u32[]{:S(2)}) %collective-permute-start.8) | collective-permute-done | bytes 458784 | tf_op jit(solution)/shard_map/ppermute | solution.py:350
  73.4 4.7 %second_left_part.3.refs_4_ = f32[64,1024]{1,0:T(8,128)S(1)} custom-call(s32[1]{0:T(128)} %bitcast.1.place_ref, bf16[1024,14336]{1,0:T(8,128)(2,1)S(1)} %bitcast.28, bf16[64,3584]{1,0:T(8,128)(2,1)S(1)} %collective-permute-done.7.refs_0_.refs_1_, bf16[64,3584]{1,0:T(8,128)(2,1)S(1)} %collective-permute-done.8.refs_1_.refs_2_, ...), custom_call_target="tpu_custom_call" | custom-call | flops 1024 | bytes 1024 | tf_op jit(solution)/shard_map/second_left_part/pallas_call | solution.py:136
  78.3 7.6 %second_left.1 = (bf16[64,1024]{1,0:T(8,128)(2,1)S(1)}, f32[64,64]{1,0:T(8,128)S(1)}) custom-call(s32[1]{0:T(128)} %bitcast.1.place_ref, bf16[1024,14336]{1,0:T(8,128)(2,1)S(1)} %bitcast.29, bf16[64,3584]{1,0:T(8,128)(2,1)S(1)} %add_convert_fusion.refs_0_, bf16[64,3584]{1,0:T(8,128)(2,1)S(1)} %collective-permute-done.7.refs_0_.refs_1_, ...), custom_call_target="tpu_custom_call" | custom-call | flops 1024 | bytes 1024 | tf_op jit(solution)/shard_map/second_left/pallas_call | solution.py:136
  98.2 8.6 %collective-permute-done.14.refs_3_ = bf16[8,64,512]{2,1,0:T(8,128)(2,1)S(1)} collective-permute-done((bf16[8,64,512]{2,1,0:T(8,128)(2,1)S(1)}, bf16[8,64,512]{2,1,0:T(8,128)(2,1)S(1)}, u32[]{:S(2)}, u32[]{:S(2)}) %collective-permute-start.14) | collective-permute-done | bytes 524320 | tf_op jit(solution)/shard_map/ppermute | solution.py:350
  106.8 6.5 %second_own.1 = (bf16[8,64,512]{2,1,0:T(8,128)(2,1)S(1)}, bf16[64,1024]{1,0:T(8,128)(2,1)}, f32[64,64]{1,0:T(8,128)S(1)}) custom-call(s32[1]{0:T(128)} %bitcast.1.place_ref, bf16[1024,14336]{1,0:T(8,128)(2,1)S(1)} %bitcast.33, bf16[64,1024]{1,0:T(8,128)(2,1)S(1)} %get-tuple-element.113.left, f32[64,64]{1,0:T(8,128)S(1)} %get-tuple-element.114.refs_0_, ...), custom_call_target="tpu_custom_call" | custom-call | flops 1024 | bytes 1024 | tf_op jit(solution)/shard_map/second_own/pallas_call | solution.py:136
  121.3 6.2 %right_unit.1 = (bf16[64,640]{1,0:T(8,128)(2,1)S(1)}, bf16[64,640]{1,0:T(8,128)(2,1)S(1)}, bf16[64,640]{1,0:T(8,128)(2,1)S(1)}, bf16[64,640]{1,0:T(8,128)(2,1)S(...) custom-call(s32[1]{0:T(128)} %bitcast.place_ref, ...), custom_call_target="tpu_custom_call" | custom-call | flops 1024 | bytes 1024 | tf_op jit(solution)/shard_map/right_unit/pallas_call | solution.py:213
  129.5 2.6 %collective-permute-start.23 = (bf16[64,640]{1,0:T(8,128)(2,1)S(1)}, bf16[64,640]{1,0:T(8,128)(2,1)S(1)}, u32[]{:S(2)}, u32[]{:S(2)}) collective-permute-start(bf16[64,640]{1,0:T(8,128)(2,1)S(1)} %get-tuple-element.134), channel_id=1, source_target_pairs={{0,16},{4,20},{8,24},{12,28},{16,0},{20,4},{24,8},{28,12},{1,17},{... | collective-permute-start | bytes 245768 | tf_op jit(solution)/shard_map/ppermute | solution.py:350
  132.1 3.6 %collective-permute-start.25 = (bf16[64,640]{1,0:T(8,128)(2,1)S(1)}, bf16[64,640]{1,0:T(8,128)(2,1)S(1)}, u32[]{:S(2)}, u32[]{:S(2)}) collective-permute-start(bf16[64,640]{1,0:T(8,128)(2,1)S(1)} %get-tuple-element.136), channel_id=1, source_target_pairs={{0,24},{4,28},{8,16},{12,20},{16,8},{20,12},{24,0},{28,4},{1,25},{... | collective-permute-start | bytes 245768 | tf_op jit(solution)/shard_map/ppermute | solution.py:350
  135.7 3.8 %collective-permute-done.21.refs_2_ = bf16[64,640]{1,0:T(8,128)(2,1)S(1)} collective-permute-done((bf16[64,640]{1,0:T(8,128)(2,1)S(1)}, bf16[64,640]{1,0:T(8,128)(2,1)S(1)}, u32[]{:S(2)}, u32[]{:S(2)}) %collective-permute-start.21) | collective-permute-done | bytes 81952 | tf_op jit(solution)/shard_map/ppermute | solution.py:350
  147.1 3.3 %grams.1 = (bf16[512,512]{1,0:T(8,128)(2,1)S(1)}, f32[8,64,64]{2,1,0:T(8,128)S(1)}, bf16[4,64,512]{2,1,0:T(8,128)(2,1)S(1)}, bf16[4,64,512]{2,1,0:T(8,128)(2,1)S...) custom-call(s32[2]{0:T(128)S(1)} %pad_add_fusion.place_ref.places_re, ...), custom_call_target="tpu_custom_call" | custom-call | flops 1024 | bytes 1024 | tf_op jit(solution)/shard_map/grams/pallas_call | solution.py:213
  152.8 3.0 %collective-permute-start.31 = (bf16[512,512]{1,0:T(8,128)(2,1)S(1)}, bf16[512,512]{1,0:T(8,128)(2,1)S(1)}, u32[]{:S(2)}, u32[]{:S(2)}) collective-permute-start(bf16[512,512]{1,0:T(8,128)(2,1)S(1)} %get-tuple-element.140.refs_4_), channel_id=1, source_target_pairs={{0,1},{1,0},{2,3},{3,2},{4,5},{5,4},{6,7},{7,6},{8,9},{9,8},{10,11... | collective-permute-start | bytes 1572872 | tf_op jit(solution)/shard_map/ppermute | solution.py:350
  155.9 2.9 %collective-permute-start.28 = (bf16[64,512]{1,0:T(8,128)(2,1)S(1)}, bf16[64,512]{1,0:T(8,128)(2,1)S(1)}, u32[]{:S(2)}, u32[]{:S(2)}) collective-permute-start(bf16[64,512]{1,0:T(8,128)(2,1)S(1)} %get-tuple-element.159), channel_id=1, source_target_pairs={{0,8},{4,12},{8,0},{12,4},{16,24},{20,28},{24,16},{28,20},{1,9},{5... | collective-permute-start | bytes 196616 | tf_op jit(solution)/shard_map/ppermute | solution.py:350
  161.0 4.1 %collective-permute-done.30 = bf16[64,512]{1,0:T(8,128)(2,1)S(1)} collective-permute-done((bf16[64,512]{1,0:T(8,128)(2,1)S(1)}, bf16[64,512]{1,0:T(8,128)(2,1)S(1)}, u32[]{:S(2)}, u32[]{:S(2)}) %collective-permute-start.30) | collective-permute-done | bytes 65568 | tf_op jit(solution)/shard_map/ppermute | solution.py:350
  187.0 7.0 %collective-permute-done.42.refs_3_ = bf16[128,512]{1,0:T(8,128)(2,1)S(1)} collective-permute-done((bf16[128,512]{1,0:T(8,128)(2,1)S(1)}, bf16[128,512]{1,0:T(8,128)(2,1)S(1)}, u32[]{:S(2)}, u32[]{:S(2)}) %collective-permute-start.42) | collective-permute-done | bytes 131104 | tf_op jit(solution)/shard_map/ppermute | solution.py:350
  196.6 3.3 %collective-permute-start.44 = (bf16[2,64,512]{2,1,0:T(8,128)(2,1)S(1)}, bf16[2,64,512]{2,1,0:T(8,128)(2,1)S(1)}, u32[]{:S(2)}, u32[]{:S(2)}) collective-permute-start(bf16[2,64,512]{2,1,0:T(8,128)(2,1)S(1)} %pad_maximum_fusion.3.refs_0_), channel_id=1, source_target_pairs={{0,16},{4,20},{8,24},{12,28},{16,0},{20,4},{24,8},{28,12},{1,17},{... | collective-permute-start | bytes 393224 | tf_op jit(solution)/shard_map/ppermute | solution.py:350
  201.2 4.6 %left_mix.1.mixed = bf16[512,1024]{1,0:T(8,128)(2,1)S(1)} custom-call(s32[1]{0:T(128)} %bitcast.1.place_ref, bf16[128,512]{1,0:T(8,128)(2,1)S(1)} %add_convert_fusion.2.refs_0_, bf16[128,512]{1,0:T(8,128)(2,1)S(1)} %collective-permute-done.40.refs_1_, bf16[128,512]{1,0:T(8,128)(2,1)S(1)} %collective-permute-done.41.refs_2_, ...), custom_call_target="tpu_custom_call" | custom-call | flops 1024 | bytes 1024 | tf_op jit(solution)/shard_map/left_mix/pallas_call | solution.py:213
  208.2 9.1 %merge.1 = bf16[1024,1792]{1,0:T(8,128)(2,1)} custom-call(s32[2]{0:T(128)S(1)} %pad_add_fusion.place_ref.places_ref, bf16[512,1024]{1,0:T(8,128)(2,1)S(1)} %left_mix.1.mixed, bf16[2,64,512]{2,1,0:T(8,128)(2,1)S(1)} %pad_maximum_fusion.3.refs_0_, bf16[2,64,512]{2,1,0:T(8,128)(2,1)S(1)} %collective-permute-done.43.refs_1_, ...), custom_call_target="tpu_custom_call" | custom-call | flops 1024 | bytes 1024 | tf_op jit(solution)/shard_map/merge/pallas_call | solution.py:485
  (124 shorter events, 85.3 us)
Async XLA Ops:
  6.5 139.3 %all-gather.2.cloned.1.call-start = ((), (), s32[]{:S(2)}) async-start(), calls=%async_computation | async-start | bytes 1179648 | tf_op jit(solution)/shard_map/all_gather | solution.py:442
  6.5 17.2 %collective-permute-start.1 = (bf16[64,3584]{1,0:T(8,128)(2,1)}, bf16[64,3584]{1,0:T(8,128)(2,1)S(1)}, u32[]{:S(2)}, u32[]{:S(2)}) collective-permute-start(bf16[64,3584]{1,0:T(8,128)(2,1)} %bitcast.34), channel_id=1, source_target_pairs={{0,2},{1,3},{2,0},{3,1},{4,6},{5,7},{6,4},{7,5},{8,10},{9,11},{10,... | collective-permute-start | bytes 1376264 | tf_op jit(solution)/shard_map/ppermute | solution.py:350
  9.5 14.2 %collective-permute-start = (bf16[64,3584]{1,0:T(8,128)(2,1)}, bf16[64,3584]{1,0:T(8,128)(2,1)S(1)}, u32[]{:S(2)}, u32[]{:S(2)}) collective-permute-start(bf16[64,3584]{1,0:T(8,128)(2,1)} %bitcast.35), channel_id=1, source_target_pairs={{0,1},{1,0},{2,3},{3,2},{4,5},{5,4},{6,7},{7,6},{8,9},{9,8},{10,11... | collective-permute-start | bytes 1376264 | tf_op jit(solution)/shard_map/ppermute | solution.py:350
  36.1 14.5 %collective-permute-start.4 = (bf16[64,3584]{1,0:T(8,128)(2,1)S(1)}, bf16[64,3584]{1,0:T(8,128)(2,1)S(1)}, u32[]{:S(2)}, u32[]{:S(2)}) collective-permute-start(bf16[64,3584]{1,0:T(8,128)(2,1)S(1)} %first_right.4), channel_id=1, source_target_pairs={{0,3},{1,2},{2,1},{3,0},{4,7},{5,6},{6,5},{7,4},{8,11},{9,10},{10,... | collective-permute-start | bytes 1376264 | tf_op jit(solution)/shard_map/ppermute | solution.py:350
  38.9 17.7 %collective-permute-start.5 = (bf16[64,3584]{1,0:T(8,128)(2,1)S(1)}, bf16[64,3584]{1,0:T(8,128)(2,1)S(1)}, u32[]{:S(2)}, u32[]{:S(2)}) collective-permute-start(bf16[64,3584]{1,0:T(8,128)(2,1)S(1)} %first_right.6), channel_id=1, source_target_pairs={{0,1},{1,0},{2,3},{3,2},{4,5},{5,4},{6,7},{7,6},{8,9},{9,8},{10,11... | collective-permute-start | bytes 1376264 | tf_op jit(solution)/shard_map/ppermute | solution.py:350
  39.4 18.0 %collective-permute-start.6 = (bf16[64,3584]{1,0:T(8,128)(2,1)S(1)}, bf16[64,3584]{1,0:T(8,128)(2,1)S(1)}, u32[]{:S(2)}, u32[]{:S(2)}) collective-permute-start(bf16[64,3584]{1,0:T(8,128)(2,1)S(1)} %first_right.5), channel_id=1, source_target_pairs={{0,2},{1,3},{2,0},{3,1},{4,6},{5,7},{6,4},{7,5},{8,10},{9,11},{10,... | collective-permute-start | bytes 1376264 | tf_op jit(solution)/shard_map/ppermute | solution.py:350
  57.6 12.5 %collective-permute-start.8 = (bf16[64,3584]{1,0:T(8,128)(2,1)S(1)}, bf16[64,3584]{1,0:T(8,128)(2,1)S(1)}, u32[]{:S(2)}, u32[]{:S(2)}) collective-permute-start(bf16[64,3584]{1,0:T(8,128)(2,1)S(1)} %add_convert_fusion.refs_0_), channel_id=1, source_target_pairs={{0,2},{1,3},{2,0},{3,1},{4,6},{5,7},{6,4},{7,5},{8,10},{9,11},{10,... | collective-permute-start | bytes 1376264 | tf_op jit(solution)/shard_map/ppermute | solution.py:350
  58.4 12.2 %collective-permute-start.7 = (bf16[64,3584]{1,0:T(8,128)(2,1)S(1)}, bf16[64,3584]{1,0:T(8,128)(2,1)S(1)}, u32[]{:S(2)}, u32[]{:S(2)}) collective-permute-start(bf16[64,3584]{1,0:T(8,128)(2,1)S(1)} %add_convert_fusion.refs_0_), channel_id=1, source_target_pairs={{0,1},{1,0},{2,3},{3,2},{4,5},{5,4},{6,7},{7,6},{8,9},{9,8},{10,11... | collective-permute-start | bytes 1376264 | tf_op jit(solution)/shard_map/ppermute | solution.py:350
  90.9 15.9 %collective-permute-start.14 = (bf16[8,64,512]{2,1,0:T(8,128)(2,1)S(1)}, bf16[8,64,512]{2,1,0:T(8,128)(2,1)S(1)}, u32[]{:S(2)}, u32[]{:S(2)}) collective-permute-start(bf16[8,64,512]{2,1,0:T(8,128)(2,1)S(1)} %second_right.3), channel_id=1, source_target_pairs={{0,3},{1,2},{2,1},{3,0},{4,7},{5,6},{6,5},{7,4},{8,11},{9,10},{10,... | collective-permute-start | bytes 1572872 | tf_op jit(solution)/shard_map/ppermute | solution.py:350
  95.5 18.5 %collective-permute-start.15 = (bf16[8,64,512]{2,1,0:T(8,128)(2,1)S(1)}, bf16[8,64,512]{2,1,0:T(8,128)(2,1)S(1)}, u32[]{:S(2)}, u32[]{:S(2)}) collective-permute-start(bf16[8,64,512]{2,1,0:T(8,128)(2,1)S(1)} %second_right.5), channel_id=1, source_target_pairs={{0,1},{1,0},{2,3},{3,2},{4,5},{5,4},{6,7},{7,6},{8,9},{9,8},{10,11... | collective-permute-start | bytes 1572872 | tf_op jit(solution)/shard_map/ppermute | solution.py:350
  97.0 17.6 %collective-permute-start.16 = (bf16[8,64,512]{2,1,0:T(8,128)(2,1)S(1)}, bf16[8,64,512]{2,1,0:T(8,128)(2,1)S(1)}, u32[]{:S(2)}, u32[]{:S(2)}) collective-permute-start(bf16[8,64,512]{2,1,0:T(8,128)(2,1)S(1)} %second_right.4), channel_id=1, source_target_pairs={{0,2},{1,3},{2,0},{3,1},{4,6},{5,7},{6,4},{7,5},{8,10},{9,11},{10,... | collective-permute-start | bytes 1572872 | tf_op jit(solution)/shard_map/ppermute | solution.py:350
  127.6 11.9 %collective-permute-start.21 = (bf16[64,640]{1,0:T(8,128)(2,1)S(1)}, bf16[64,640]{1,0:T(8,128)(2,1)S(1)}, u32[]{:S(2)}, u32[]{:S(2)}) collective-permute-start(bf16[64,640]{1,0:T(8,128)(2,1)S(1)} %get-tuple-element.132), channel_id=1, source_target_pairs={{0,8},{4,12},{8,0},{12,4},{16,24},{20,28},{24,16},{28,20},{1,9},{5... | collective-permute-start | bytes 245768 | tf_op jit(solution)/shard_map/ppermute | solution.py:350
  129.3 12.5 %collective-permute-start.22 = (bf16[64,640]{1,0:T(8,128)(2,1)S(1)}, bf16[64,640]{1,0:T(8,128)(2,1)S(1)}, u32[]{:S(2)}, u32[]{:S(2)}) collective-permute-start(bf16[64,640]{1,0:T(8,128)(2,1)S(1)} %get-tuple-element.133), channel_id=1, source_target_pairs={{0,12},{4,8},{8,4},{12,0},{16,28},{20,24},{24,20},{28,16},{1,13},{... | collective-permute-start | bytes 245768 | tf_op jit(solution)/shard_map/ppermute | solution.py:350
  129.5 12.3 %collective-permute-start.23 = (bf16[64,640]{1,0:T(8,128)(2,1)S(1)}, bf16[64,640]{1,0:T(8,128)(2,1)S(1)}, u32[]{:S(2)}, u32[]{:S(2)}) collective-permute-start(bf16[64,640]{1,0:T(8,128)(2,1)S(1)} %get-tuple-element.134), channel_id=1, source_target_pairs={{0,16},{4,20},{8,24},{12,28},{16,0},{20,4},{24,8},{28,12},{1,17},{... | collective-permute-start | bytes 245768 | tf_op jit(solution)/shard_map/ppermute | solution.py:350
  132.1 11.4 %collective-permute-start.25 = (bf16[64,640]{1,0:T(8,128)(2,1)S(1)}, bf16[64,640]{1,0:T(8,128)(2,1)S(1)}, u32[]{:S(2)}, u32[]{:S(2)}) collective-permute-start(bf16[64,640]{1,0:T(8,128)(2,1)S(1)} %get-tuple-element.136), channel_id=1, source_target_pairs={{0,24},{4,28},{8,16},{12,20},{16,8},{20,12},{24,0},{28,4},{1,25},{... | collective-permute-start | bytes 245768 | tf_op jit(solution)/shard_map/ppermute | solution.py:350
  150.6 16.6 %collective-permute-start.32 = (bf16[512,512]{1,0:T(8,128)(2,1)S(1)}, bf16[512,512]{1,0:T(8,128)(2,1)S(1)}, u32[]{:S(2)}, u32[]{:S(2)}) collective-permute-start(bf16[512,512]{1,0:T(8,128)(2,1)S(1)} %get-tuple-element.140.refs_4_), channel_id=1, source_target_pairs={{0,2},{1,3},{2,0},{3,1},{4,6},{5,7},{6,4},{7,5},{8,10},{9,11},{10,... | collective-permute-start | bytes 1572872 | tf_op jit(solution)/shard_map/ppermute | solution.py:350
  152.8 15.1 %collective-permute-start.31 = (bf16[512,512]{1,0:T(8,128)(2,1)S(1)}, bf16[512,512]{1,0:T(8,128)(2,1)S(1)}, u32[]{:S(2)}, u32[]{:S(2)}) collective-permute-start(bf16[512,512]{1,0:T(8,128)(2,1)S(1)} %get-tuple-element.140.refs_4_), channel_id=1, source_target_pairs={{0,1},{1,0},{2,3},{3,2},{4,5},{5,4},{6,7},{7,6},{8,9},{9,8},{10,11... | collective-permute-start | bytes 1572872 | tf_op jit(solution)/shard_map/ppermute | solution.py:350
  181.9 23.9 %collective-permute-start.46 = (bf16[256,512]{1,0:T(8,128)(2,1)S(1)}, bf16[256,512]{1,0:T(8,128)(2,1)S(1)}, u32[]{:S(2)}, u32[]{:S(2)}) collective-permute-start(bf16[256,512]{1,0:T(8,128)(2,1)S(1)} %slice.38), channel_id=1, source_target_pairs={{0,1},{1,0},{2,3},{3,2},{4,5},{5,4},{6,7},{7,6},{8,9},{9,8},{10,11... | collective-permute-start | bytes 786440 | tf_op jit(solution)/shard_map/ppermute | solution.py:350
  182.9 22.9 %collective-permute-start.47 = (bf16[256,512]{1,0:T(8,128)(2,1)S(1)}, bf16[256,512]{1,0:T(8,128)(2,1)S(1)}, u32[]{:S(2)}, u32[]{:S(2)}) collective-permute-start(bf16[256,512]{1,0:T(8,128)(2,1)S(1)} %slice.39), channel_id=1, source_target_pairs={{0,2},{1,3},{2,0},{3,1},{4,6},{5,7},{6,4},{7,5},{8,10},{9,11},{10,... | collective-permute-start | bytes 786440 | tf_op jit(solution)/shard_map/ppermute | solution.py:350
  183.5 10.5 %collective-permute-start.42 = (bf16[128,512]{1,0:T(8,128)(2,1)S(1)}, bf16[128,512]{1,0:T(8,128)(2,1)S(1)}, u32[]{:S(2)}, u32[]{:S(2)}) collective-permute-start(bf16[128,512]{1,0:T(8,128)(2,1)S(1)} %add_convert_fusion.2.refs_0_), channel_id=1, source_target_pairs={{0,3},{1,2},{2,1},{3,0},{4,7},{5,6},{6,5},{7,4},{8,11},{9,10},{10,... | collective-permute-start | bytes 393224 | tf_op jit(solution)/shard_map/ppermute | solution.py:350
  185.4 11.2 %collective-permute-start.41 = (bf16[128,512]{1,0:T(8,128)(2,1)S(1)}, bf16[128,512]{1,0:T(8,128)(2,1)S(1)}, u32[]{:S(2)}, u32[]{:S(2)}) collective-permute-start(bf16[128,512]{1,0:T(8,128)(2,1)S(1)} %add_convert_fusion.2.refs_0_), channel_id=1, source_target_pairs={{0,2},{1,3},{2,0},{3,1},{4,6},{5,7},{6,4},{7,5},{8,10},{9,11},{10,... | collective-permute-start | bytes 393224 | tf_op jit(solution)/shard_map/ppermute | solution.py:350
  186.0 13.9 %collective-permute-start.40 = (bf16[128,512]{1,0:T(8,128)(2,1)S(1)}, bf16[128,512]{1,0:T(8,128)(2,1)S(1)}, u32[]{:S(2)}, u32[]{:S(2)}) collective-permute-start(bf16[128,512]{1,0:T(8,128)(2,1)S(1)} %add_convert_fusion.2.refs_0_), channel_id=1, source_target_pairs={{0,1},{1,0},{2,3},{3,2},{4,5},{5,4},{6,7},{7,6},{8,9},{9,8},{10,11... | collective-permute-start | bytes 393224 | tf_op jit(solution)/shard_map/ppermute | solution.py:350
  194.0 11.9 %collective-permute-start.45 = (bf16[2,64,512]{2,1,0:T(8,128)(2,1)S(1)}, bf16[2,64,512]{2,1,0:T(8,128)(2,1)S(1)}, u32[]{:S(2)}, u32[]{:S(2)}) collective-permute-start(bf16[2,64,512]{2,1,0:T(8,128)(2,1)S(1)} %pad_maximum_fusion.3.refs_0_), channel_id=1, source_target_pairs={{0,24},{4,28},{8,16},{12,20},{16,8},{20,12},{24,0},{28,4},{1,25},{... | collective-permute-start | bytes 393224 | tf_op jit(solution)/shard_map/ppermute | solution.py:350
  196.6 11.6 %collective-permute-start.44 = (bf16[2,64,512]{2,1,0:T(8,128)(2,1)S(1)}, bf16[2,64,512]{2,1,0:T(8,128)(2,1)S(1)}, u32[]{:S(2)}, u32[]{:S(2)}) collective-permute-start(bf16[2,64,512]{2,1,0:T(8,128)(2,1)S(1)} %pad_maximum_fusion.3.refs_0_), channel_id=1, source_target_pairs={{0,16},{4,20},{8,24},{12,28},{16,0},{20,4},{24,8},{28,12},{1,17},{... | collective-permute-start | bytes 393224 | tf_op jit(solution)/shard_map/ppermute | solution.py:350
  (31 other events, 194.2 us)
Sparse Core Ops, SparseCore 0:
  114.8 27.5 all-gather.1
where the time goes:
time: 224 us
  waiting for transfers between devices  70.9 us (32%)
  Pallas kernels  64.4 us (29%)
  starting transfers between devices  60.3 us (27%)
  between operations  14.3 us (6%)
  local copies, waits for them, and re-layouts  12.9 us (6%)
    ppermute x48, waiting for transfers between devices, permute(): lax.ppermute(value, axis, [(source, source ^ gap) for source in range(cou...  70.9 us
    ppermute x48, starting transfers between devices, permute(): lax.ppermute(value, axis, [(source, source ^ gap) for source in range(cou...  60.3 us
    pallas_call x14, Pallas kernels, delta_call(): pl.pallas_call(kernel, in_specs=[pl.BlockSpec(memory_space=pltpu.SMEM)] +...  40.6 us
    pallas_call x4, Pallas kernels, small_call(): pl.pallas_call(kernel, in_specs=[spec(i) for i in range(len(args))], out_...  14.7 us
    unnamed x12, local copies, waits for them, and re-layouts  12.8 us
    pallas_call x1, Pallas kernels, body(): pl.pallas_call(functools.partial(merge_kernel, count, groups), grid=(rows...  9.1 us
  transfers between devices with their start and end apart: 49, of which 30 were waited for; matrix products, arithmetic and copies ran while one was open for 0% of the time, Pallas kernels for 18%

commit v1 on v0

--- a/solution.py
+++ b/solution.py
@@ -56,16 +56,14 @@
     work[:, :rank] = (lax.broadcasted_iota(jnp.int32, (rank, rank), 1) == index).astype(F32)
     work[:, rank:] = gram
     tiles = [work[at:at + 8, :] for at in range(0, rank, 8)]
-    below = lax.broadcasted_iota(jnp.int32, (8, 1), 0)
+    below = lax.broadcasted_iota(jnp.int32, (8, 2 * rank), 0)
     for k in range(rank - 1):
         at = rank + k
         first, inner = divmod(k, 8)
-        row = tiles[first][inner:inner + 1, :]
-        row = row * (1.0 / row[:, at:at + 1])
-        for number in range(first, len(tiles)):
-            column = tiles[number][:, at:at + 1]
-            if number == first:
-                column = jnp.where(below > inner, column, 0.0)
+        columns = [jnp.broadcast_to(tile[:, at:at + 1], tile.shape) for tile in tiles[first:]]
+        row = tiles[first][inner:inner + 1, :] * (1.0 / columns[0][inner:inner + 1, :])
+        columns[0] = jnp.where(below > inner, columns[0], 0.0)
+        for number, column in enumerate(columns, first):
             tiles[number] = tiles[number] - column * row
     table = jnp.concatenate(tiles, axis=0)
     pivots = jnp.sum(jnp.where(lane == index + rank, table, 0.0), axis=1, keepdims=True)
@@ -252,11 +250,9 @@
 
 
 def grams_kernel(groups, place_ref, left_stack, *refs):
-    pieces, (stack, middles, home, away, *slabs) = refs[:groups], refs[groups:]
-    left_rows = slabs[0].shape[0]
-    for gap, slab in enumerate(slabs):
-        at = pl.multiple_of((place_ref[1] ^ gap) * left_rows, left_rows)
-        slab[...] = dot(left_stack[pl.ds(at, left_rows), :], left_stack[...], NT).astype(BF16)
+    pieces, (stack, middles, home, away, left_rows) = refs[:groups], refs[groups:]
+    at = pl.multiple_of(place_ref[0] * left_rows.shape[0], left_rows.shape[0])
+    left_rows[...] = dot(left_stack[pl.ds(at, left_rows.shape[0]), :], left_stack[...], NT).astype(BF16)
     rank = pieces[0].shape[0]
     size = stack.shape[1]
     place = place_ref[0]
@@ -270,78 +266,72 @@
             out[number] = dot(stack[pl.ds(at, rank), :], stack[...], NT).astype(BF16)
 
 
-def fill_gram(place, pairs, gram):
-    rank = pairs[0].shape[1]
-    for number, pair in enumerate(pairs):
-        for side in range(2):
-            at = pl.multiple_of((place ^ (2 * number + side)) * rank, rank)
-            gram[pl.ds(at, rank), :] = pair[side].astype(F32)
-
-
-def polish(count, gram, product, spare, side):
-    size = gram.shape[0]
-    strip = min(512, size)
+def polish(count, sides):
+    size = sides[0][0].shape[0]
     eye = (
         lax.broadcasted_iota(jnp.int32, (size, size), 0) == lax.broadcasted_iota(jnp.int32, (size, size), 1)
     ).astype(F32)
     lead, tail = 1.5 / math.sqrt(count), -0.5 / (count * math.sqrt(count))
-    product[...] = lead * eye + tail * gram[...]
-
-    def multiply(a_ref, c_ref, lead, tail):
+    strip = min(512, size)
+    for gram, product, _, _ in sides:
+        product[...] = lead * eye + tail * gram[...]
+
+    def multiply(a_ref, c_ref, other, lead, tail):
         def one(index, _):
             rows = pl.ds(pl.multiple_of(index * strip, strip), strip)
             a = a_ref[rows, :]
-            c_ref[rows, :] = lead * a + tail * dot(a.astype(BF16), side[...])
+            c_ref[rows, :] = lead * a + tail * dot(a.astype(BF16), other[...])
             return 0
 
-        lax.fori_loop(0, size // strip, one, 0)
+        if strip == size:
+            c_ref[...] = lead * a_ref[...] + tail * dot(a_ref[...].astype(BF16), other[...])
+        else:
+            lax.fori_loop(0, size // strip, one, 0)
 
     def step(index, _):
         first = index == 1
         before = jnp.where(first, lead, 1.5)
         after = jnp.where(first, tail, -0.5)
-        side[...] = gram[...].astype(BF16)
-        multiply(gram, spare, before, after)
-        multiply(spare, gram, before, after)
-        side[...] = gram[...].astype(BF16)
-        multiply(product, product, 1.5, -0.5)
+        for gram, _, _, other in sides:
+            other[...] = gram[...].astype(BF16)
+        for gram, _, spare, other in sides:
+            multiply(gram, spare, other, before, after)
+        for gram, _, spare, other in sides:
+            multiply(spare, gram, other, before, after)
+        for gram, _, _, other in sides:
+            other[...] = gram[...].astype(BF16)
+        for _, product, _, other in sides:
+            multiply(product, product, other, 1.5, -0.5)
         return 0
 
     lax.fori_loop(1, NS_ITERS, step, 0)
 
 
-def left_mix_kernel(count, ckpt_count, place_ref, *refs):
-    slabs, (stack, middle, out, gram, product, spare, side) = refs[:count], refs[count:]
-    slab_rows = slabs[0].shape[0]
-    for gap, slab in enumerate(slabs):
-        at = pl.multiple_of((place_ref[0] ^ gap) * slab_rows, slab_rows)
-        gram[pl.ds(at, slab_rows), :] = slab[...].astype(F32)
-    polish(ckpt_count, gram, product, spare, side)
-    rank = middle.shape[1]
-    for index in range(ckpt_count):
-        rows = pl.ds(index * rank, rank)
-        spare[rows, :] = dot_wide(jnp.transpose(middle[index]), product[rows, :])
-    side[...] = spare[...].astype(BF16)
-    out[...] = dot(side[...], stack[...]).astype(BF16)
-
-
-def merge_kernel(count, ckpt_count, places_ref, mixed, *refs):
-    pairs, refs = refs[:ckpt_count // 2], refs[ckpt_count // 2:]
-    pieces, (out, gram, product, spare, side, wide) = refs[:count], refs[count:]
+def merge_kernel(count, ckpt_count, places_ref, stack, middle, *refs):
+    columns, pieces, refs = refs[:2], refs[2:2 + count], refs[2 + count:]
+    out, gram, product, spare, left_gram, left_product, left_spare, other, left_other, wide = refs
     real = out.shape[1]
 
     @pl.when(pl.program_id(0) == 0)
     def _():
-        fill_gram(places_ref[0], pairs, gram)
+        rank = middle.shape[1]
+        for number in range(ckpt_count // 2):
+            for side, column in enumerate(columns):
+                rows = pl.ds(pl.multiple_of((places_ref[0] ^ (2 * number + side)) * rank, rank), rank)
+                gram[rows, :] = column[number, :rank, :].astype(F32)
+                left_gram[rows, :] = column[number, rank:, :].astype(F32)
         size = pieces[0].shape[1]
         wide[...] = jnp.zeros_like(wide)
         for gap, piece in enumerate(pieces):
             start = pl.multiple_of(slot_start(places_ref[1] ^ gap, size, real), 128)
             wide[:, pl.ds(start, size)] += piece[...]
-        polish(ckpt_count, gram, product, spare, side)
-        side[...] = product[...].astype(BF16)
-
-    turned = jnp.transpose(dot(side[...], mixed[...])).astype(BF16)
+        polish(ckpt_count, [(gram, product, spare, other), (left_gram, left_product, left_spare, left_other)])
+        for index in range(ckpt_count):
+            rows = pl.ds(index * rank, rank)
+            left_spare[rows, :] = dot_wide(jnp.transpose(middle[index]), left_product[rows, :])
+        other[...] = dot_wide(product[...], left_spare[...]).astype(BF16)
+
+    turned = jnp.transpose(dot(other[...], stack[...])).astype(BF16)
     out[...] = dot(turned, wide[...]).astype(BF16)
 
 
@@ -452,48 +442,39 @@
     )
     pieces = swap(leaving, "ckpt")
     size = groups * rank
-    table = pltpu.VMEM((size, size), F32)
-    tables = [table, table, table, pltpu.VMEM((size, size), BF16)]
     slabs = shape((groups // 2, rank, size), BF16)
-    right_stack, middles, home, away, *left_slabs = small_call(
+    right_stack, middles, home, away, left_rows = small_call(
         functools.partial(grams_kernel, groups),
-        [shape((size, padded), BF16), shape((groups, rank, rank), F32), slabs, slabs]
-        + [shape((size // count, size), BF16)] * count,
-        [at_both, left_stack] + pieces, name="grams", scalars=1,
-    )
+        [shape((size, padded), BF16), shape((groups, rank, rank), F32), slabs, slabs, shape((rank, size), BF16)],
+        [at_ckpt, left_stack] + pieces, name="grams", scalars=1,
+    )
+    pair_sum = add_up([home, permute(away, "ckpt", 1)]).astype(BF16)
+    right_stack, pair_sum = together(right_stack, pair_sum)
+    own = add_up([pair_sum[0]] + [permute(pair_sum[n], "ckpt", 2 * n) for n in range(1, groups // 2)]).astype(BF16)
     near = [permute(right_stack, "rows", gap) for gap in range(1, count) if not gap & (gap - 1)]
-    pair_sum = add_up([home, permute(away, "ckpt", 1)]).astype(BF16)
-    own = add_up([pair_sum[0]] + [permute(pair_sum[n], "ckpt", 2 * n) for n in range(1, groups // 2)]).astype(BF16)
-    own, *held = together(own, *near, *left_slabs)
-    near, left_slabs = held[:len(near)], held[len(near):]
-    right_rows = add_up(spread(own, "rows")).astype(BF16)
-    left_slab = add_up(swap(left_slabs, "rows")).astype(BF16)
-    right_rows, left_slab = together(right_rows, left_slab)
-    pair = jnp.stack([right_rows, permute(right_rows, "ckpt", 1)])
-    pair, left_slab, *near = together(pair, left_slab, *near)
-    right_pairs = [pair] + [permute(pair, "ckpt", gap) for gap in range(2, groups, 2)]
-    left_slabs = spread(left_slab, "rows")
+    both = add_up(spread(jnp.concatenate([own, left_rows]), "rows")).astype(BF16)
+    both, *near = together(both, *near)
     right_all = [right_stack] + [None if gap & (gap - 1) else near.pop(0) for gap in range(1, count)]
     forward(right_all, "rows")
-
-    (mixed,) = small_call(
-        functools.partial(left_mix_kernel, count, groups), [shape((size, rows), BF16)],
-        [at_row] + left_slabs + [left_stack, middles], tables, "left_mix", scalars=1,
-    )
+    column = jnp.stack([both] + [permute(both, "ckpt", gap) for gap in range(2, groups, 2)])
+    column, *right_all = together(column, *right_all)
+    columns = [column, permute(column, "ckpt", 1)]
+
     step = min(512, rows)
     full = lambda value: pl.BlockSpec(value.shape, lambda i: (0,) * value.ndim)
     return pl.pallas_call(
         functools.partial(merge_kernel, count, groups),
         grid=(rows // step,),
         in_specs=[pl.BlockSpec(memory_space=pltpu.SMEM), pl.BlockSpec((size, step), lambda i: (0, i))]
-        + [full(value) for value in right_pairs + right_all],
+        + [full(value) for value in [middles] + columns + right_all],
         out_specs=pl.BlockSpec((step, block), lambda i: (i, 0)),
         out_shape=shape((rows, block), BF16),
-        scratch_shapes=tables + [pltpu.VMEM((size, block), BF16)],
-        compiler_params=pltpu.CompilerParams(vmem_limit_bytes=VMEM_BYTES),
+        scratch_shapes=[pltpu.VMEM((size, size), F32)] * 6 + [pltpu.VMEM((size, size), BF16)] * 2
+        + [pltpu.VMEM((size, block), BF16)],
+        compiler_params=pltpu.CompilerParams(vmem_limit_bytes=2 * VMEM_BYTES),
         name="merge",
         cost_estimate=SHORT,
-    )(at_both, mixed, *right_pairs, *right_all)
+    )(at_both, left_stack, middles, *columns, *right_all)
 
 
 def solution(mesh):

time: 224 us -> 217 us (0.969)
  starting transfers between devices: 60.3 us -> 55.5 us
    pallas_call x4 -> x3, Pallas kernels: 14.7 us -> 8.65 us  [small_call(): pl.pallas_call(kernel, in_specs=[spec(i) for i in range(len(args))], out_...]
    ppermute x48 -> x42, starting transfers between devices: 60.3 us -> 55.5 us  [permute(): lax.ppermute(value, axis, [(source, source ^ gap) for source in range(cou...]
    pallas_call x1, Pallas kernels: 9.1 us -> 13.1 us  [body(): pl.pallas_call(functools.partial(merge_kernel, count, groups), grid=(rows...]
    ppermute x48 -> x42, waiting for transfers between devices: 70.9 us -> 70.2 us  [permute(): lax.ppermute(value, axis, [(source, source ^ gap) for source in range(cou...]
  transfers between devices with their start and end apart: 49 -> 43, of which waited for: 30 -> 26; matrix products, arithmetic and copies ran while one was open for 0% -> 0% of each run, Pallas kernels for 18% -> 16%
where the time goes in v1:
time: 217 us
  waiting for transfers between devices  70.2 us (32%)
  Pallas kernels  62.4 us (29%)
  starting transfers between devices  55.5 us (26%)
  between operations  14.3 us (7%)
  local copies, waits for them, and re-layouts  12.9 us (6%)
    ppermute x42, waiting for transfers between devices, permute(): lax.ppermute(value, axis, [(source, source ^ gap) for source in range(cou...  70.2 us
    ppermute x42, starting transfers between devices, permute(): lax.ppermute(value, axis, [(source, source ^ gap) for source in range(cou...  55.5 us
    pallas_call x14, Pallas kernels, delta_call(): pl.pallas_call(kernel, in_specs=[pl.BlockSpec(memory_space=pltpu.SMEM)] +...  40.6 us
    pallas_call x1, Pallas kernels, body(): pl.pallas_call(functools.partial(merge_kernel, count, groups), grid=(rows...  13.1 us
    unnamed x12, local copies, waits for them, and re-layouts  12.8 us
    pallas_call x3, Pallas kernels, small_call(): pl.pallas_call(kernel, in_specs=[spec(i) for i in range(len(args))], out_...  8.65 us
  transfers between devices with their start and end apart: 43, of which 26 were waited for; matrix products, arithmetic and copies ran while one was open for 0% of the time, Pallas kernels for 16%

profile of v1, /device:TPU:0, one launch (start us, length us, event | category | flops | bytes accessed | tf_op | source)
XLA Modules:
  0.0 216.8 jit_solution(8580139514280831430)
XLA Ops:
  6.5 3.0 %collective-permute-start.1 = (bf16[64,3584]{1,0:T(8,128)(2,1)}, bf16[64,3584]{1,0:T(8,128)(2,1)S(1)}, u32[]{:S(2)}, u32[]{:S(2)}) collective-permute-start(bf16[64,3584]{1,0:T(8,128)(2,1)} %bitcast.34), channel_id=1, source_target_pairs={{0,2},{1,3},{2,0},{3,1},{4,6},{5,7},{6,4},{7,5},{8,10},{9,11},{10,... | collective-permute-start | bytes 1376264 | tf_op jit(solution)/shard_map/ppermute | solution.py:340
  11.0 9.3 %copy-done = bf16[1,1024,14336]{2,1,0:T(8,128)(2,1)S(1)} copy-done((bf16[1,1024,14336]{2,1,0:T(8,128)(2,1)S(1)}, bf16[1,1024,14336]{2,1,0:T(8,128)(2,1)}, u32[]{:S(2)}) %copy-start) | copy-done | bytes 29360152
  24.4 4.5 %first_left_part.3.refs_4_ = f32[64,1024]{1,0:T(8,128)S(1)} custom-call(s32[1]{0:T(128)} %bitcast.1.place_ref, bf16[1024,14336]{1,0:T(8,128)(2,1)S(1)} %bitcast.21, bf16[64,3584]{1,0:T(8,128)(2,1)S(1)} %collective-permute-done.refs_0_.refs_1_, bf16[64,3584]{1,0:T(8,128)(2,1)S(1)} %collective-permute-done.1.refs_1_.refs_2_, f32[64,1024]{1,0:T(8,128)S(1)} %first_left_part.2.refs_2_), custom_call_target="tpu_custom_call" | custom-call | flops 1024 | bytes 1024 | tf_op jit(solution)/shard_map/first_left_part/pallas_call | solution.py:134
  41.1 9.5 %collective-permute-done.4 = bf16[64,3584]{1,0:T(8,128)(2,1)S(1)} collective-permute-done((bf16[64,3584]{1,0:T(8,128)(2,1)S(1)}, bf16[64,3584]{1,0:T(8,128)(2,1)S(1)}, u32[]{:S(2)}, u32[]{:S(2)}) %collective-permute-start.4) | collective-permute-done | bytes 458784 | tf_op jit(solution)/shard_map/ppermute | solution.py:340
  51.9 4.8 %collective-permute-done.5 = bf16[64,3584]{1,0:T(8,128)(2,1)S(1)} collective-permute-done((bf16[64,3584]{1,0:T(8,128)(2,1)S(1)}, bf16[64,3584]{1,0:T(8,128)(2,1)S(1)}, u32[]{:S(2)}, u32[]{:S(2)}) %collective-permute-start.5) | collective-permute-done | bytes 458784 | tf_op jit(solution)/shard_map/ppermute | solution.py:340
  62.2 7.9 %collective-permute-done.8.refs_1_.refs_2_ = bf16[64,3584]{1,0:T(8,128)(2,1)S(1)} collective-permute-done((bf16[64,3584]{1,0:T(8,128)(2,1)S(1)}, bf16[64,3584]{1,0:T(8,128)(2,1)S(1)}, u32[]{:S(2)}, u32[]{:S(2)}) %collective-permute-start.8) | collective-permute-done | bytes 458784 | tf_op jit(solution)/shard_map/ppermute | solution.py:340
  73.4 4.7 %second_left_part.3.refs_4_ = f32[64,1024]{1,0:T(8,128)S(1)} custom-call(s32[1]{0:T(128)} %bitcast.1.place_ref, bf16[1024,14336]{1,0:T(8,128)(2,1)S(1)} %bitcast.28, bf16[64,3584]{1,0:T(8,128)(2,1)S(1)} %collective-permute-done.7.refs_0_.refs_1_, bf16[64,3584]{1,0:T(8,128)(2,1)S(1)} %collective-permute-done.8.refs_1_.refs_2_, ...), custom_call_target="tpu_custom_call" | custom-call | flops 1024 | bytes 1024 | tf_op jit(solution)/shard_map/second_left_part/pallas_call | solution.py:134
  78.3 7.6 %second_left.1 = (bf16[64,1024]{1,0:T(8,128)(2,1)S(1)}, f32[64,64]{1,0:T(8,128)S(1)}) custom-call(s32[1]{0:T(128)} %bitcast.1.place_ref, bf16[1024,14336]{1,0:T(8,128)(2,1)S(1)} %bitcast.29, bf16[64,3584]{1,0:T(8,128)(2,1)S(1)} %add_convert_fusion.refs_0_, bf16[64,3584]{1,0:T(8,128)(2,1)S(1)} %collective-permute-done.7.refs_0_.refs_1_, ...), custom_call_target="tpu_custom_call" | custom-call | flops 1024 | bytes 1024 | tf_op jit(solution)/shard_map/second_left/pallas_call | solution.py:134
  98.2 8.6 %collective-permute-done.14.refs_3_ = bf16[8,64,512]{2,1,0:T(8,128)(2,1)S(1)} collective-permute-done((bf16[8,64,512]{2,1,0:T(8,128)(2,1)S(1)}, bf16[8,64,512]{2,1,0:T(8,128)(2,1)S(1)}, u32[]{:S(2)}, u32[]{:S(2)}) %collective-permute-start.14) | collective-permute-done | bytes 524320 | tf_op jit(solution)/shard_map/ppermute | solution.py:340
  106.8 6.5 %second_own.1 = (bf16[8,64,512]{2,1,0:T(8,128)(2,1)S(1)}, bf16[64,1024]{1,0:T(8,128)(2,1)}, f32[64,64]{1,0:T(8,128)S(1)}) custom-call(s32[1]{0:T(128)} %bitcast.1.place_ref, bf16[1024,14336]{1,0:T(8,128)(2,1)S(1)} %bitcast.33, bf16[64,1024]{1,0:T(8,128)(2,1)S(1)} %get-tuple-element.107.left, f32[64,64]{1,0:T(8,128)S(1)} %get-tuple-element.108.refs_0_, ...), custom_call_target="tpu_custom_call" | custom-call | flops 1024 | bytes 1024 | tf_op jit(solution)/shard_map/second_own/pallas_call | solution.py:134
  121.4 6.4 %right_unit.1 = (bf16[64,640]{1,0:T(8,128)(2,1)S(1)}, bf16[64,640]{1,0:T(8,128)(2,1)S(1)}, bf16[64,640]{1,0:T(8,128)(2,1)S(1)}, bf16[64,640]{1,0:T(8,128)(2,1)S(...) custom-call(s32[1]{0:T(128)} %bitcast.place_ref, ...), custom_call_target="tpu_custom_call" | custom-call | flops 1024 | bytes 1024 | tf_op jit(solution)/shard_map/right_unit/pallas_call | solution.py:211
  129.7 2.6 %collective-permute-start.23 = (bf16[64,640]{1,0:T(8,128)(2,1)S(1)}, bf16[64,640]{1,0:T(8,128)(2,1)S(1)}, u32[]{:S(2)}, u32[]{:S(2)}) collective-permute-start(bf16[64,640]{1,0:T(8,128)(2,1)S(1)} %get-tuple-element.128), channel_id=1, source_target_pairs={{0,16},{4,20},{8,24},{12,28},{16,0},{20,4},{24,8},{28,12},{1,17},{... | collective-permute-start | bytes 245768 | tf_op jit(solution)/shard_map/ppermute | solution.py:340
  132.3 3.6 %collective-permute-start.25 = (bf16[64,640]{1,0:T(8,128)(2,1)S(1)}, bf16[64,640]{1,0:T(8,128)(2,1)S(1)}, u32[]{:S(2)}, u32[]{:S(2)}) collective-permute-start(bf16[64,640]{1,0:T(8,128)(2,1)S(1)} %get-tuple-element.130), channel_id=1, source_target_pairs={{0,24},{4,28},{8,16},{12,20},{16,8},{20,12},{24,0},{28,4},{1,25},{... | collective-permute-start | bytes 245768 | tf_op jit(solution)/shard_map/ppermute | solution.py:340
  135.9 3.9 %collective-permute-done.21.refs_2_ = bf16[64,640]{1,0:T(8,128)(2,1)S(1)} collective-permute-done((bf16[64,640]{1,0:T(8,128)(2,1)S(1)}, bf16[64,640]{1,0:T(8,128)(2,1)S(1)}, u32[]{:S(2)}, u32[]{:S(2)}) %collective-permute-start.21) | collective-permute-done | bytes 81952 | tf_op jit(solution)/shard_map/ppermute | solution.py:340
  143.7 2.7 %collective-permute-done.26.refs_7_ = bf16[64,640]{1,0:T(8,128)(2,1)S(1)} collective-permute-done((bf16[64,640]{1,0:T(8,128)(2,1)S(1)}, bf16[64,640]{1,0:T(8,128)(2,1)S(1)}, u32[]{:S(2)}, u32[]{:S(2)}) %collective-permute-start.26) | collective-permute-done | bytes 81952 | tf_op jit(solution)/shard_map/ppermute | solution.py:340
  151.0 3.1 %collective-permute-start.28 = (bf16[64,512]{1,0:T(8,128)(2,1)S(1)}, bf16[64,512]{1,0:T(8,128)(2,1)S(1)}, u32[]{:S(2)}, u32[]{:S(2)}) collective-permute-start(bf16[64,512]{1,0:T(8,128)(2,1)S(1)} %get-tuple-element.147), channel_id=1, source_target_pairs={{0,8},{4,12},{8,0},{12,4},{16,24},{20,28},{24,16},{28,20},{1,9},{5... | collective-permute-start | bytes 196616 | tf_op jit(solution)/shard_map/ppermute | solution.py:340
  154.1 2.5 %collective-permute-start.30 = (bf16[64,512]{1,0:T(8,128)(2,1)S(1)}, bf16[64,512]{1,0:T(8,128)(2,1)S(1)}, u32[]{:S(2)}, u32[]{:S(2)}) collective-permute-start(bf16[64,512]{1,0:T(8,128)(2,1)S(1)} %get-tuple-element.148), channel_id=1, source_target_pairs={{0,24},{4,28},{8,16},{12,20},{16,8},{20,12},{24,0},{28,4},{1,25},{... | collective-permute-start | bytes 196616 | tf_op jit(solution)/shard_map/ppermute | solution.py:340
  156.6 2.6 %collective-permute-start.35 = (bf16[512,512]{1,0:T(8,128)(2,1)S(1)}, bf16[512,512]{1,0:T(8,128)(2,1)S(1)}, u32[]{:S(2)}, u32[]{:S(2)}) collective-permute-start(bf16[512,512]{1,0:T(8,128)(2,1)S(1)} %get-tuple-element.143.refs_2_), channel_id=1, source_target_pairs={{0,2},{1,3},{2,0},{3,1},{4,6},{5,7},{6,4},{7,5},{8,10},{9,11},{10,... | collective-permute-start | bytes 1572872 | tf_op jit(solution)/shard_map/ppermute | solution.py:340
  163.1 2.7 %collective-permute-start.32 = (bf16[128,512]{1,0:T(8,128)(2,1)S(1)}, bf16[128,512]{1,0:T(8,128)(2,1)S(1)}, u32[]{:S(2)}, u32[]{:S(2)}) collective-permute-start(bf16[128,512]{1,0:T(8,128)(2,1)S(1)} %pad_maximum_fusion.4), channel_id=1, source_target_pairs={{0,2},{1,3},{2,0},{3,1},{4,6},{5,7},{6,4},{7,5},{8,10},{9,11},{10,... | collective-permute-start | bytes 393224 | tf_op jit(solution)/shard_map/ppermute | solution.py:340
  167.6 6.4 %collective-permute-done.32 = bf16[128,512]{1,0:T(8,128)(2,1)S(1)} collective-permute-done((bf16[128,512]{1,0:T(8,128)(2,1)S(1)}, bf16[128,512]{1,0:T(8,128)(2,1)S(1)}, u32[]{:S(2)}, u32[]{:S(2)}) %collective-permute-start.32) | collective-permute-done | bytes 131104 | tf_op jit(solution)/shard_map/ppermute | solution.py:340
  174.0 2.6 %collective-permute-done.31 = bf16[128,512]{1,0:T(8,128)(2,1)S(1)} collective-permute-done((bf16[128,512]{1,0:T(8,128)(2,1)S(1)}, bf16[128,512]{1,0:T(8,128)(2,1)S(1)}, u32[]{:S(2)}, u32[]{:S(2)}) %collective-permute-start.31) | collective-permute-done | bytes 131104 | tf_op jit(solution)/shard_map/ppermute | solution.py:340
  185.8 3.3 %collective-permute-done.38 = bf16[128,512]{1,0:T(8,128)(2,1)S(1)} collective-permute-done((bf16[128,512]{1,0:T(8,128)(2,1)S(1)}, bf16[128,512]{1,0:T(8,128)(2,1)S(1)}, u32[]{:S(2)}, u32[]{:S(2)}) %collective-permute-start.38) | collective-permute-done | bytes 131104 | tf_op jit(solution)/shard_map/ppermute | solution.py:340
  189.1 4.3 %collective-permute-done.37 = bf16[128,512]{1,0:T(8,128)(2,1)S(1)} collective-permute-done((bf16[128,512]{1,0:T(8,128)(2,1)S(1)}, bf16[128,512]{1,0:T(8,128)(2,1)S(1)}, u32[]{:S(2)}, u32[]{:S(2)}) %collective-permute-start.37) | collective-permute-done | bytes 131104 | tf_op jit(solution)/shard_map/ppermute | solution.py:340
  196.8 13.1 %merge.1 = bf16[1024,1792]{1,0:T(8,128)(2,1)} custom-call(s32[2]{0:T(128)S(1)} %pad_add_fusion.places_ref, bf16[512,1024]{1,0:T(8,128)(2,1)S(1)} %copy-done.2, f32[8,64,64]{2,1,0:T(8,128)S(1)} %get-tuple-element.132.middle, bf16[4,128,512]{2,1,0:T(8,128)(2,1)S(1)} %pad_maximum_fusion.refs_0_, bf16[4,128,512]{2,1,0:T(8,128)(2,1)S(1)} %collective-permute-done.41.refs_1_, ...), custom_call_target="tpu_custom_call" | custom-call | flops 1024 | bytes 1024 | tf_op jit(solution)/shard_map/merge/pallas_call | solution.py:465
  (111 shorter events, 76.2 us)
Async XLA Ops:
  6.5 139.9 %all-gather.2.cloned.1.call-start = ((), (), s32[]{:S(2)}) async-start(), calls=%async_computation | async-start | bytes 1179648 | tf_op jit(solution)/shard_map/all_gather | solution.py:432
  6.5 17.2 %collective-permute-start.1 = (bf16[64,3584]{1,0:T(8,128)(2,1)}, bf16[64,3584]{1,0:T(8,128)(2,1)S(1)}, u32[]{:S(2)}, u32[]{:S(2)}) collective-permute-start(bf16[64,3584]{1,0:T(8,128)(2,1)} %bitcast.34), channel_id=1, source_target_pairs={{0,2},{1,3},{2,0},{3,1},{4,6},{5,7},{6,4},{7,5},{8,10},{9,11},{10,... | collective-permute-start | bytes 1376264 | tf_op jit(solution)/shard_map/ppermute | solution.py:340
  9.5 14.2 %collective-permute-start = (bf16[64,3584]{1,0:T(8,128)(2,1)}, bf16[64,3584]{1,0:T(8,128)(2,1)S(1)}, u32[]{:S(2)}, u32[]{:S(2)}) collective-permute-start(bf16[64,3584]{1,0:T(8,128)(2,1)} %bitcast.35), channel_id=1, source_target_pairs={{0,1},{1,0},{2,3},{3,2},{4,5},{5,4},{6,7},{7,6},{8,9},{9,8},{10,11... | collective-permute-start | bytes 1376264 | tf_op jit(solution)/shard_map/ppermute | solution.py:340
  36.1 14.5 %collective-permute-start.4 = (bf16[64,3584]{1,0:T(8,128)(2,1)S(1)}, bf16[64,3584]{1,0:T(8,128)(2,1)S(1)}, u32[]{:S(2)}, u32[]{:S(2)}) collective-permute-start(bf16[64,3584]{1,0:T(8,128)(2,1)S(1)} %first_right.4), channel_id=1, source_target_pairs={{0,3},{1,2},{2,1},{3,0},{4,7},{5,6},{6,5},{7,4},{8,11},{9,10},{10,... | collective-permute-start | bytes 1376264 | tf_op jit(solution)/shard_map/ppermute | solution.py:340
  38.9 17.7 %collective-permute-start.5 = (bf16[64,3584]{1,0:T(8,128)(2,1)S(1)}, bf16[64,3584]{1,0:T(8,128)(2,1)S(1)}, u32[]{:S(2)}, u32[]{:S(2)}) collective-permute-start(bf16[64,3584]{1,0:T(8,128)(2,1)S(1)} %first_right.6), channel_id=1, source_target_pairs={{0,1},{1,0},{2,3},{3,2},{4,5},{5,4},{6,7},{7,6},{8,9},{9,8},{10,11... | collective-permute-start | bytes 1376264 | tf_op jit(solution)/shard_map/ppermute | solution.py:340
  39.4 18.0 %collective-permute-start.6 = (bf16[64,3584]{1,0:T(8,128)(2,1)S(1)}, bf16[64,3584]{1,0:T(8,128)(2,1)S(1)}, u32[]{:S(2)}, u32[]{:S(2)}) collective-permute-start(bf16[64,3584]{1,0:T(8,128)(2,1)S(1)} %first_right.5), channel_id=1, source_target_pairs={{0,2},{1,3},{2,0},{3,1},{4,6},{5,7},{6,4},{7,5},{8,10},{9,11},{10,... | collective-permute-start | bytes 1376264 | tf_op jit(solution)/shard_map/ppermute | solution.py:340
  57.6 12.5 %collective-permute-start.8 = (bf16[64,3584]{1,0:T(8,128)(2,1)S(1)}, bf16[64,3584]{1,0:T(8,128)(2,1)S(1)}, u32[]{:S(2)}, u32[]{:S(2)}) collective-permute-start(bf16[64,3584]{1,0:T(8,128)(2,1)S(1)} %add_convert_fusion.refs_0_), channel_id=1, source_target_pairs={{0,2},{1,3},{2,0},{3,1},{4,6},{5,7},{6,4},{7,5},{8,10},{9,11},{10,... | collective-permute-start | bytes 1376264 | tf_op jit(solution)/shard_map/ppermute | solution.py:340
  58.4 12.2 %collective-permute-start.7 = (bf16[64,3584]{1,0:T(8,128)(2,1)S(1)}, bf16[64,3584]{1,0:T(8,128)(2,1)S(1)}, u32[]{:S(2)}, u32[]{:S(2)}) collective-permute-start(bf16[64,3584]{1,0:T(8,128)(2,1)S(1)} %add_convert_fusion.refs_0_), channel_id=1, source_target_pairs={{0,1},{1,0},{2,3},{3,2},{4,5},{5,4},{6,7},{7,6},{8,9},{9,8},{10,11... | collective-permute-start | bytes 1376264 | tf_op jit(solution)/shard_map/ppermute | solution.py:340
  90.9 15.9 %collective-permute-start.14 = (bf16[8,64,512]{2,1,0:T(8,128)(2,1)S(1)}, bf16[8,64,512]{2,1,0:T(8,128)(2,1)S(1)}, u32[]{:S(2)}, u32[]{:S(2)}) collective-permute-start(bf16[8,64,512]{2,1,0:T(8,128)(2,1)S(1)} %second_right.3), channel_id=1, source_target_pairs={{0,3},{1,2},{2,1},{3,0},{4,7},{5,6},{6,5},{7,4},{8,11},{9,10},{10,... | collective-permute-start | bytes 1572872 | tf_op jit(solution)/shard_map/ppermute | solution.py:340
  95.5 18.5 %collective-permute-start.15 = (bf16[8,64,512]{2,1,0:T(8,128)(2,1)S(1)}, bf16[8,64,512]{2,1,0:T(8,128)(2,1)S(1)}, u32[]{:S(2)}, u32[]{:S(2)}) collective-permute-start(bf16[8,64,512]{2,1,0:T(8,128)(2,1)S(1)} %second_right.5), channel_id=1, source_target_pairs={{0,1},{1,0},{2,3},{3,2},{4,5},{5,4},{6,7},{7,6},{8,9},{9,8},{10,11... | collective-permute-start | bytes 1572872 | tf_op jit(solution)/shard_map/ppermute | solution.py:340
  97.0 17.7 %collective-permute-start.16 = (bf16[8,64,512]{2,1,0:T(8,128)(2,1)S(1)}, bf16[8,64,512]{2,1,0:T(8,128)(2,1)S(1)}, u32[]{:S(2)}, u32[]{:S(2)}) collective-permute-start(bf16[8,64,512]{2,1,0:T(8,128)(2,1)S(1)} %second_right.4), channel_id=1, source_target_pairs={{0,2},{1,3},{2,0},{3,1},{4,6},{5,7},{6,4},{7,5},{8,10},{9,11},{10,... | collective-permute-start | bytes 1572872 | tf_op jit(solution)/shard_map/ppermute | solution.py:340
  127.8 12.0 %collective-permute-start.21 = (bf16[64,640]{1,0:T(8,128)(2,1)S(1)}, bf16[64,640]{1,0:T(8,128)(2,1)S(1)}, u32[]{:S(2)}, u32[]{:S(2)}) collective-permute-start(bf16[64,640]{1,0:T(8,128)(2,1)S(1)} %get-tuple-element.126), channel_id=1, source_target_pairs={{0,8},{4,12},{8,0},{12,4},{16,24},{20,28},{24,16},{28,20},{1,9},{5... | collective-permute-start | bytes 245768 | tf_op jit(solution)/shard_map/ppermute | solution.py:340
  129.4 12.0 %collective-permute-start.22 = (bf16[64,640]{1,0:T(8,128)(2,1)S(1)}, bf16[64,640]{1,0:T(8,128)(2,1)S(1)}, u32[]{:S(2)}, u32[]{:S(2)}) collective-permute-start(bf16[64,640]{1,0:T(8,128)(2,1)S(1)} %get-tuple-element.127), channel_id=1, source_target_pairs={{0,12},{4,8},{8,4},{12,0},{16,28},{20,24},{24,20},{28,16},{1,13},{... | collective-permute-start | bytes 245768 | tf_op jit(solution)/shard_map/ppermute | solution.py:340
  129.7 11.8 %collective-permute-start.23 = (bf16[64,640]{1,0:T(8,128)(2,1)S(1)}, bf16[64,640]{1,0:T(8,128)(2,1)S(1)}, u32[]{:S(2)}, u32[]{:S(2)}) collective-permute-start(bf16[64,640]{1,0:T(8,128)(2,1)S(1)} %get-tuple-element.128), channel_id=1, source_target_pairs={{0,16},{4,20},{8,24},{12,28},{16,0},{20,4},{24,8},{28,12},{1,17},{... | collective-permute-start | bytes 245768 | tf_op jit(solution)/shard_map/ppermute | solution.py:340
  132.3 11.4 %collective-permute-start.25 = (bf16[64,640]{1,0:T(8,128)(2,1)S(1)}, bf16[64,640]{1,0:T(8,128)(2,1)S(1)}, u32[]{:S(2)}, u32[]{:S(2)}) collective-permute-start(bf16[64,640]{1,0:T(8,128)(2,1)S(1)} %get-tuple-element.130), channel_id=1, source_target_pairs={{0,24},{4,28},{8,16},{12,20},{16,8},{20,12},{24,0},{28,4},{1,25},{... | collective-permute-start | bytes 245768 | tf_op jit(solution)/shard_map/ppermute | solution.py:340
  151.0 10.0 %collective-permute-start.28 = (bf16[64,512]{1,0:T(8,128)(2,1)S(1)}, bf16[64,512]{1,0:T(8,128)(2,1)S(1)}, u32[]{:S(2)}, u32[]{:S(2)}) collective-permute-start(bf16[64,512]{1,0:T(8,128)(2,1)S(1)} %get-tuple-element.147), channel_id=1, source_target_pairs={{0,8},{4,12},{8,0},{12,4},{16,24},{20,28},{24,16},{28,20},{1,9},{5... | collective-permute-start | bytes 196616 | tf_op jit(solution)/shard_map/ppermute | solution.py:340
  156.6 21.2 %collective-permute-start.35 = (bf16[512,512]{1,0:T(8,128)(2,1)S(1)}, bf16[512,512]{1,0:T(8,128)(2,1)S(1)}, u32[]{:S(2)}, u32[]{:S(2)}) collective-permute-start(bf16[512,512]{1,0:T(8,128)(2,1)S(1)} %get-tuple-element.143.refs_2_), channel_id=1, source_target_pairs={{0,2},{1,3},{2,0},{3,1},{4,6},{5,7},{6,4},{7,5},{8,10},{9,11},{10,... | collective-permute-start | bytes 1572872 | tf_op jit(solution)/shard_map/ppermute | solution.py:340
  159.2 18.5 %collective-permute-start.34 = (bf16[512,512]{1,0:T(8,128)(2,1)S(1)}, bf16[512,512]{1,0:T(8,128)(2,1)S(1)}, u32[]{:S(2)}, u32[]{:S(2)}) collective-permute-start(bf16[512,512]{1,0:T(8,128)(2,1)S(1)} %get-tuple-element.143.refs_2_), channel_id=1, source_target_pairs={{0,1},{1,0},{2,3},{3,2},{4,5},{5,4},{6,7},{7,6},{8,9},{9,8},{10,11... | collective-permute-start | bytes 1572872 | tf_op jit(solution)/shard_map/ppermute | solution.py:340
  163.1 10.9 %collective-permute-start.32 = (bf16[128,512]{1,0:T(8,128)(2,1)S(1)}, bf16[128,512]{1,0:T(8,128)(2,1)S(1)}, u32[]{:S(2)}, u32[]{:S(2)}) collective-permute-start(bf16[128,512]{1,0:T(8,128)(2,1)S(1)} %pad_maximum_fusion.4), channel_id=1, source_target_pairs={{0,2},{1,3},{2,0},{3,1},{4,6},{5,7},{6,4},{7,5},{8,10},{9,11},{10,... | collective-permute-start | bytes 393224 | tf_op jit(solution)/shard_map/ppermute | solution.py:340
  165.8 10.8 %collective-permute-start.31 = (bf16[128,512]{1,0:T(8,128)(2,1)S(1)}, bf16[128,512]{1,0:T(8,128)(2,1)S(1)}, u32[]{:S(2)}, u32[]{:S(2)}) collective-permute-start(bf16[128,512]{1,0:T(8,128)(2,1)S(1)} %pad_maximum_fusion.4), channel_id=1, source_target_pairs={{0,1},{1,0},{2,3},{3,2},{4,5},{5,4},{6,7},{7,6},{8,9},{9,8},{10,11... | collective-permute-start | bytes 393224 | tf_op jit(solution)/shard_map/ppermute | solution.py:340
  167.6 10.1 %collective-permute-start.33 = (bf16[128,512]{1,0:T(8,128)(2,1)S(1)}, bf16[128,512]{1,0:T(8,128)(2,1)S(1)}, u32[]{:S(2)}, u32[]{:S(2)}) collective-permute-start(bf16[128,512]{1,0:T(8,128)(2,1)S(1)} %pad_maximum_fusion.4), channel_id=1, source_target_pairs={{0,3},{1,2},{2,1},{3,0},{4,7},{5,6},{6,5},{7,4},{8,11},{9,10},{10,... | collective-permute-start | bytes 393224 | tf_op jit(solution)/shard_map/ppermute | solution.py:340
  177.9 15.7 %collective-permute-start.39 = (bf16[256,512]{1,0:T(8,128)(2,1)S(1)}, bf16[256,512]{1,0:T(8,128)(2,1)S(1)}, u32[]{:S(2)}, u32[]{:S(2)}) collective-permute-start(bf16[256,512]{1,0:T(8,128)(2,1)S(1)} %slice.38), channel_id=1, source_target_pairs={{0,1},{1,0},{2,3},{3,2},{4,5},{5,4},{6,7},{7,6},{8,9},{9,8},{10,11... | collective-permute-start | bytes 786440 | tf_op jit(solution)/shard_map/ppermute | solution.py:340
  179.7 13.9 %collective-permute-start.40 = (bf16[256,512]{1,0:T(8,128)(2,1)S(1)}, bf16[256,512]{1,0:T(8,128)(2,1)S(1)}, u32[]{:S(2)}, u32[]{:S(2)}) collective-permute-start(bf16[256,512]{1,0:T(8,128)(2,1)S(1)} %slice.39), channel_id=1, source_target_pairs={{0,2},{1,3},{2,0},{3,1},{4,6},{5,7},{6,4},{7,5},{8,10},{9,11},{10,... | collective-permute-start | bytes 786440 | tf_op jit(solution)/shard_map/ppermute | solution.py:340
  182.9 10.5 %collective-permute-start.37 = (bf16[128,512]{1,0:T(8,128)(2,1)S(1)}, bf16[128,512]{1,0:T(8,128)(2,1)S(1)}, u32[]{:S(2)}, u32[]{:S(2)}) collective-permute-start(bf16[128,512]{1,0:T(8,128)(2,1)S(1)} %add_convert_fusion.2), channel_id=1, source_target_pairs={{0,16},{4,20},{8,24},{12,28},{16,0},{20,4},{24,8},{28,12},{1,17},{... | collective-permute-start | bytes 393224 | tf_op jit(solution)/shard_map/ppermute | solution.py:340
  (25 other events, 157.6 us)
Sparse Core Ops, SparseCore 0:
  114.8 27.0 all-gather.1

commit v2 on v1

--- a/solution.py
+++ b/solution.py
@@ -206,8 +206,9 @@
     return jnp.minimum(slot * size, real - size)
 
 
-def small_call(kernel, out_shape, args, scratch=(), name=None, scalars=0):
-    spec = lambda i: pl.BlockSpec(memory_space=pltpu.SMEM if i < scalars else pltpu.VMEM)
+def small_call(kernel, out_shape, args, scratch=(), name=None, scalars=0, hbm=0):
+    spaces = [pltpu.SMEM] * scalars + [pltpu.HBM] * hbm + [pltpu.VMEM] * (len(args) - scalars - hbm)
+    spec = lambda i: pl.BlockSpec(memory_space=spaces[i])
     return pl.pallas_call(
         kernel,
         in_specs=[spec(i) for i in range(len(args))],
@@ -249,10 +250,10 @@
         out[:, size + rank:] = middle_low
 
 
-def grams_kernel(groups, place_ref, left_stack, *refs):
-    pieces, (stack, middles, home, away, left_rows) = refs[:groups], refs[groups:]
-    at = pl.multiple_of(place_ref[0] * left_rows.shape[0], left_rows.shape[0])
-    left_rows[...] = dot(left_stack[pl.ds(at, left_rows.shape[0]), :], left_stack[...], NT).astype(BF16)
+def grams_kernel(groups, place_ref, left_hbm, *refs):
+    pieces, (stack, middles, home, away, left_rows, left_stack, sem) = refs[:groups], refs[groups:]
+    copy = pltpu.make_async_copy(left_hbm, left_stack, sem)
+    copy.start()
     rank = pieces[0].shape[0]
     size = stack.shape[1]
     place = place_ref[0]
@@ -264,6 +265,9 @@
         for out, gap in ((home, 2 * number), (away, 2 * number + 1)):
             at = pl.multiple_of((place ^ gap) * rank, rank)
             out[number] = dot(stack[pl.ds(at, rank), :], stack[...], NT).astype(BF16)
+    copy.wait()
+    at = pl.multiple_of(place * rank, rank)
+    left_rows[...] = dot(left_stack[pl.ds(at, rank), :], left_stack[...], NT).astype(BF16)
 
 
 def polish(count, sides):
@@ -307,32 +311,40 @@
     lax.fori_loop(1, NS_ITERS, step, 0)
 
 
-def merge_kernel(count, ckpt_count, places_ref, stack, middle, *refs):
+def merge_kernel(count, ckpt_count, places_ref, left_hbm, middle, *refs):
     columns, pieces, refs = refs[:2], refs[2:2 + count], refs[2 + count:]
-    out, gram, product, spare, left_gram, left_product, left_spare, other, left_other, wide = refs
+    out, gram, product, spare, left_gram, left_product, left_spare, other, left_other, wide, strips, stack, sem, sems = refs
     real = out.shape[1]
-
-    @pl.when(pl.program_id(0) == 0)
-    def _():
-        rank = middle.shape[1]
-        for number in range(ckpt_count // 2):
-            for side, column in enumerate(columns):
-                rows = pl.ds(pl.multiple_of((places_ref[0] ^ (2 * number + side)) * rank, rank), rank)
-                gram[rows, :] = column[number, :rank, :].astype(F32)
-                left_gram[rows, :] = column[number, rank:, :].astype(F32)
-        size = pieces[0].shape[1]
-        wide[...] = jnp.zeros_like(wide)
-        for gap, piece in enumerate(pieces):
-            start = pl.multiple_of(slot_start(places_ref[1] ^ gap, size, real), 128)
-            wide[:, pl.ds(start, size)] += piece[...]
-        polish(ckpt_count, [(gram, product, spare, other), (left_gram, left_product, left_spare, left_other)])
-        for index in range(ckpt_count):
-            rows = pl.ds(index * rank, rank)
-            left_spare[rows, :] = dot_wide(jnp.transpose(middle[index]), left_product[rows, :])
-        other[...] = dot_wide(product[...], left_spare[...]).astype(BF16)
-
-    turned = jnp.transpose(dot(other[...], stack[...])).astype(BF16)
-    out[...] = dot(turned, wide[...]).astype(BF16)
+    load = pltpu.make_async_copy(left_hbm, stack, sem)
+    load.start()
+    rank = middle.shape[1]
+    for number in range(ckpt_count // 2):
+        for side, column in enumerate(columns):
+            rows = pl.ds(pl.multiple_of((places_ref[0] ^ (2 * number + side)) * rank, rank), rank)
+            gram[rows, :] = column[number, :rank, :].astype(F32)
+            left_gram[rows, :] = column[number, rank:, :].astype(F32)
+    size = pieces[0].shape[1]
+    wide[...] = jnp.zeros_like(wide)
+    for gap, piece in enumerate(pieces):
+        start = pl.multiple_of(slot_start(places_ref[1] ^ gap, size, real), 128)
+        wide[:, pl.ds(start, size)] += piece[...]
+    polish(ckpt_count, [(gram, product, spare, other), (left_gram, left_product, left_spare, left_other)])
+    for index in range(ckpt_count):
+        rows = pl.ds(index * rank, rank)
+        left_spare[rows, :] = dot_wide(jnp.transpose(middle[index]), left_product[rows, :])
+    other[...] = dot_wide(product[...], left_spare[...]).astype(BF16)
+
+    load.wait()
+    copies = []
+    for number in range(strips.shape[0]):
+        span = slice(number * strips.shape[1], (number + 1) * strips.shape[1])
+        turned = jnp.transpose(dot(other[...], stack[:, span])).astype(BF16)
+        strips[number] = dot(turned, wide[...]).astype(BF16)
+        copy = pltpu.make_async_copy(strips.at[number], out.at[pl.ds(span.start, strips.shape[1]), :], sems.at[number])
+        copy.start()
+        copies.append(copy)
+    for copy in copies:
+        copy.wait()
 
 
 def permute(value, axis, gap):
@@ -443,10 +455,12 @@
     pieces = swap(leaving, "ckpt")
     size = groups * rank
     slabs = shape((groups // 2, rank, size), BF16)
+    in_hbm = pltpu.with_memory_space_constraint(left_stack, pltpu.HBM)
     right_stack, middles, home, away, left_rows = small_call(
         functools.partial(grams_kernel, groups),
         [shape((size, padded), BF16), shape((groups, rank, rank), F32), slabs, slabs, shape((rank, size), BF16)],
-        [at_ckpt, left_stack] + pieces, name="grams", scalars=1,
+        [at_ckpt, in_hbm] + pieces, [pltpu.VMEM(left_stack.shape, BF16), pltpu.SemaphoreType.DMA(())],
+        name="grams", scalars=1, hbm=1,
     )
     pair_sum = add_up([home, permute(away, "ckpt", 1)]).astype(BF16)
     right_stack, pair_sum = together(right_stack, pair_sum)
@@ -460,21 +474,21 @@
     column, *right_all = together(column, *right_all)
     columns = [column, permute(column, "ckpt", 1)]
 
-    step = min(512, rows)
-    full = lambda value: pl.BlockSpec(value.shape, lambda i: (0,) * value.ndim)
+    step = min(256, rows)
+    vmem = pl.BlockSpec(memory_space=pltpu.VMEM)
+    args = [in_hbm, middles, *columns, *right_all]
     return pl.pallas_call(
         functools.partial(merge_kernel, count, groups),
-        grid=(rows // step,),
-        in_specs=[pl.BlockSpec(memory_space=pltpu.SMEM), pl.BlockSpec((size, step), lambda i: (0, i))]
-        + [full(value) for value in [middles] + columns + right_all],
-        out_specs=pl.BlockSpec((step, block), lambda i: (i, 0)),
+        in_specs=[pl.BlockSpec(memory_space=pltpu.SMEM), pl.BlockSpec(memory_space=pltpu.HBM)] + [vmem] * (len(args) - 1),
+        out_specs=pl.BlockSpec(memory_space=pl.ANY),
         out_shape=shape((rows, block), BF16),
         scratch_shapes=[pltpu.VMEM((size, size), F32)] * 6 + [pltpu.VMEM((size, size), BF16)] * 2
-        + [pltpu.VMEM((size, block), BF16)],
+        + [pltpu.VMEM((size, block), BF16), pltpu.VMEM((rows // step, step, block), BF16),
+           pltpu.VMEM(left_stack.shape, BF16), pltpu.SemaphoreType.DMA(()), pltpu.SemaphoreType.DMA((rows // step,))],
         compiler_params=pltpu.CompilerParams(vmem_limit_bytes=2 * VMEM_BYTES),
         name="merge",
         cost_estimate=SHORT,
-    )(at_both, left_stack, middles, *columns, *right_all)
+    )(at_both, *args)
 
 
 def solution(mesh):

time: 217 us -> 216 us (level)
  local copies, waits for them, and re-layouts: 12.9 us -> 10.5 us
    unnamed x12 -> x8, local copies, waits for them, and re-layouts: 12.8 us -> 10.4 us
where the time goes in v2:
time: 216 us
  waiting for transfers between devices  70.2 us (32%)
  Pallas kernels  63.7 us (29%)
  starting transfers between devices  55.6 us (26%)
  between operations  14.4 us (7%)
  local copies, waits for them, and re-layouts  10.5 us (5%)
    ppermute x42, waiting for transfers between devices, permute(): lax.ppermute(value, axis, [(source, source ^ gap) for source in range(cou...  70.2 us
    ppermute x42, starting transfers between devices, permute(): lax.ppermute(value, axis, [(source, source ^ gap) for source in range(cou...  55.6 us
    pallas_call x14, Pallas kernels, delta_call(): pl.pallas_call(kernel, in_specs=[pl.BlockSpec(memory_space=pltpu.SMEM)] +...  40.6 us
    pallas_call x1, Pallas kernels, body(): pl.pallas_call(functools.partial(merge_kernel, count, groups), in_specs=[...  13.2 us
    unnamed x8, local copies, waits for them, and re-layouts  10.4 us
    pallas_call x3, Pallas kernels, small_call(): pl.pallas_call(kernel, in_specs=[spec(i) for i in range(len(args))], out_...  9.91 us
  transfers between devices with their start and end apart: 43, of which 26 were waited for; matrix products, arithmetic and copies ran while one was open for 0% of the time, Pallas kernels for 16%

profile of v2, /device:TPU:0, one launch (start us, length us, event | category | flops | bytes accessed | tf_op | source)
XLA Modules:
  0.0 215.7 jit_solution(13279163665133224718)
XLA Ops:
  6.5 3.0 %collective-permute-start.1 = (bf16[64,3584]{1,0:T(8,128)(2,1)}, bf16[64,3584]{1,0:T(8,128)(2,1)S(1)}, u32[]{:S(2)}, u32[]{:S(2)}) collective-permute-start(bf16[64,3584]{1,0:T(8,128)(2,1)} %bitcast.34), channel_id=1, source_target_pairs={{0,2},{1,3},{2,0},{3,1},{4,6},{5,7},{6,4},{7,5},{8,10},{9,11},{10,... | collective-permute-start | bytes 1376264 | tf_op jit(solution)/shard_map/ppermute | solution.py:352
  11.0 9.3 %copy-done = bf16[1,1024,14336]{2,1,0:T(8,128)(2,1)S(1)} copy-done((bf16[1,1024,14336]{2,1,0:T(8,128)(2,1)S(1)}, bf16[1,1024,14336]{2,1,0:T(8,128)(2,1)}, u32[]{:S(2)}) %copy-start) | copy-done | bytes 29360152
  24.4 4.5 %first_left_part.3.refs_4_ = f32[64,1024]{1,0:T(8,128)S(1)} custom-call(s32[1]{0:T(128)} %bitcast.1.place_ref, bf16[1024,14336]{1,0:T(8,128)(2,1)S(1)} %bitcast.21, bf16[64,3584]{1,0:T(8,128)(2,1)S(1)} %collective-permute-done.refs_0_.refs_1_, bf16[64,3584]{1,0:T(8,128)(2,1)S(1)} %collective-permute-done.1.refs_1_.refs_2_, f32[64,1024]{1,0:T(8,128)S(1)} %first_left_part.2.refs_2_), custom_call_target="tpu_custom_call" | custom-call | flops 1024 | bytes 1024 | tf_op jit(solution)/shard_map/first_left_part/pallas_call | solution.py:134
  41.1 9.5 %collective-permute-done.4 = bf16[64,3584]{1,0:T(8,128)(2,1)S(1)} collective-permute-done((bf16[64,3584]{1,0:T(8,128)(2,1)S(1)}, bf16[64,3584]{1,0:T(8,128)(2,1)S(1)}, u32[]{:S(2)}, u32[]{:S(2)}) %collective-permute-start.4) | collective-permute-done | bytes 458784 | tf_op jit(solution)/shard_map/ppermute | solution.py:352
  51.9 4.8 %collective-permute-done.5 = bf16[64,3584]{1,0:T(8,128)(2,1)S(1)} collective-permute-done((bf16[64,3584]{1,0:T(8,128)(2,1)S(1)}, bf16[64,3584]{1,0:T(8,128)(2,1)S(1)}, u32[]{:S(2)}, u32[]{:S(2)}) %collective-permute-start.5) | collective-permute-done | bytes 458784 | tf_op jit(solution)/shard_map/ppermute | solution.py:352
  62.2 7.9 %collective-permute-done.8.refs_1_.refs_2_ = bf16[64,3584]{1,0:T(8,128)(2,1)S(1)} collective-permute-done((bf16[64,3584]{1,0:T(8,128)(2,1)S(1)}, bf16[64,3584]{1,0:T(8,128)(2,1)S(1)}, u32[]{:S(2)}, u32[]{:S(2)}) %collective-permute-start.8) | collective-permute-done | bytes 458784 | tf_op jit(solution)/shard_map/ppermute | solution.py:352
  73.4 4.7 %second_left_part.3.refs_4_ = f32[64,1024]{1,0:T(8,128)S(1)} custom-call(s32[1]{0:T(128)} %bitcast.1.place_ref, bf16[1024,14336]{1,0:T(8,128)(2,1)S(1)} %bitcast.28, bf16[64,3584]{1,0:T(8,128)(2,1)S(1)} %collective-permute-done.7.refs_0_.refs_1_, bf16[64,3584]{1,0:T(8,128)(2,1)S(1)} %collective-permute-done.8.refs_1_.refs_2_, ...), custom_call_target="tpu_custom_call" | custom-call | flops 1024 | bytes 1024 | tf_op jit(solution)/shard_map/second_left_part/pallas_call | solution.py:134
  78.3 7.6 %second_left.1 = (bf16[64,1024]{1,0:T(8,128)(2,1)S(1)}, f32[64,64]{1,0:T(8,128)S(1)}) custom-call(s32[1]{0:T(128)} %bitcast.1.place_ref, bf16[1024,14336]{1,0:T(8,128)(2,1)S(1)} %bitcast.29, bf16[64,3584]{1,0:T(8,128)(2,1)S(1)} %add_convert_fusion.refs_0_, bf16[64,3584]{1,0:T(8,128)(2,1)S(1)} %collective-permute-done.7.refs_0_.refs_1_, ...), custom_call_target="tpu_custom_call" | custom-call | flops 1024 | bytes 1024 | tf_op jit(solution)/shard_map/second_left/pallas_call | solution.py:134
  98.2 8.6 %collective-permute-done.14.refs_3_ = bf16[8,64,512]{2,1,0:T(8,128)(2,1)S(1)} collective-permute-done((bf16[8,64,512]{2,1,0:T(8,128)(2,1)S(1)}, bf16[8,64,512]{2,1,0:T(8,128)(2,1)S(1)}, u32[]{:S(2)}, u32[]{:S(2)}) %collective-permute-start.14) | collective-permute-done | bytes 524320 | tf_op jit(solution)/shard_map/ppermute | solution.py:352
  106.8 6.5 %second_own.1 = (bf16[8,64,512]{2,1,0:T(8,128)(2,1)S(1)}, bf16[64,1024]{1,0:T(8,128)(2,1)}, f32[64,64]{1,0:T(8,128)S(1)}) custom-call(s32[1]{0:T(128)} %bitcast.1.place_ref, bf16[1024,14336]{1,0:T(8,128)(2,1)S(1)} %bitcast.33, bf16[64,1024]{1,0:T(8,128)(2,1)S(1)} %get-tuple-element.107.left, f32[64,64]{1,0:T(8,128)S(1)} %get-tuple-element.108.refs_0_, ...), custom_call_target="tpu_custom_call" | custom-call | flops 1024 | bytes 1024 | tf_op jit(solution)/shard_map/second_own/pallas_call | solution.py:134
  121.4 6.4 %right_unit.1 = (bf16[64,640]{1,0:T(8,128)(2,1)S(1)}, bf16[64,640]{1,0:T(8,128)(2,1)S(1)}, bf16[64,640]{1,0:T(8,128)(2,1)S(1)}, bf16[64,640]{1,0:T(8,128)(2,1)S(...) custom-call(s32[1]{0:T(128)} %bitcast.place_ref, ...), custom_call_target="tpu_custom_call" | custom-call | flops 1024 | bytes 1024 | tf_op jit(solution)/shard_map/right_unit/pallas_call | solution.py:212
  129.7 2.6 %collective-permute-start.23 = (bf16[64,640]{1,0:T(8,128)(2,1)S(1)}, bf16[64,640]{1,0:T(8,128)(2,1)S(1)}, u32[]{:S(2)}, u32[]{:S(2)}) collective-permute-start(bf16[64,640]{1,0:T(8,128)(2,1)S(1)} %get-tuple-element.128), channel_id=1, source_target_pairs={{0,16},{4,20},{8,24},{12,28},{16,0},{20,4},{24,8},{28,12},{1,17},{... | collective-permute-start | bytes 245768 | tf_op jit(solution)/shard_map/ppermute | solution.py:352
  132.3 3.6 %collective-permute-start.25 = (bf16[64,640]{1,0:T(8,128)(2,1)S(1)}, bf16[64,640]{1,0:T(8,128)(2,1)S(1)}, u32[]{:S(2)}, u32[]{:S(2)}) collective-permute-start(bf16[64,640]{1,0:T(8,128)(2,1)S(1)} %get-tuple-element.130), channel_id=1, source_target_pairs={{0,24},{4,28},{8,16},{12,20},{16,8},{20,12},{24,0},{28,4},{1,25},{... | collective-permute-start | bytes 245768 | tf_op jit(solution)/shard_map/ppermute | solution.py:352
  135.9 3.9 %collective-permute-done.21.refs_2_ = bf16[64,640]{1,0:T(8,128)(2,1)S(1)} collective-permute-done((bf16[64,640]{1,0:T(8,128)(2,1)S(1)}, bf16[64,640]{1,0:T(8,128)(2,1)S(1)}, u32[]{:S(2)}, u32[]{:S(2)}) %collective-permute-start.21) | collective-permute-done | bytes 81952 | tf_op jit(solution)/shard_map/ppermute | solution.py:352
  143.7 2.7 %collective-permute-done.26.refs_7_ = bf16[64,640]{1,0:T(8,128)(2,1)S(1)} collective-permute-done((bf16[64,640]{1,0:T(8,128)(2,1)S(1)}, bf16[64,640]{1,0:T(8,128)(2,1)S(1)}, u32[]{:S(2)}, u32[]{:S(2)}) %collective-permute-start.26) | collective-permute-done | bytes 81952 | tf_op jit(solution)/shard_map/ppermute | solution.py:352
  146.4 3.0 %grams.1 = (bf16[512,512]{1,0:T(8,128)(2,1)S(1)}, f32[8,64,64]{2,1,0:T(8,128)S(1)}, bf16[4,64,512]{2,1,0:T(8,128)(2,1)S(1)}, bf16[4,64,512]{2,1,0:T(8,128)(2,1)S(1)}, bf16[64,512]{1,0:T(8,128)(2,1)S(1)}) custom-call(s32[1]{0:T(128)} %bitcast.place_ref, bf16[512,1024]{1,0:T(8,128)(2,1)} %all-gather.2.cloned.1.call-done.left_hbm, ...), custom_call_target="tpu_custom_call" | custom-call | flops 1024 | bytes 1024 | tf_op jit(solution)/shard_map/grams/pallas_call | solution.py:212
  151.1 3.1 %collective-permute-start.28 = (bf16[64,512]{1,0:T(8,128)(2,1)S(1)}, bf16[64,512]{1,0:T(8,128)(2,1)S(1)}, u32[]{:S(2)}, u32[]{:S(2)}) collective-permute-start(bf16[64,512]{1,0:T(8,128)(2,1)S(1)} %get-tuple-element.147), channel_id=1, source_target_pairs={{0,8},{4,12},{8,0},{12,4},{16,24},{20,28},{24,16},{28,20},{1,9},{5... | collective-permute-start | bytes 196616 | tf_op jit(solution)/shard_map/ppermute | solution.py:352
  156.7 2.6 %collective-permute-start.35 = (bf16[512,512]{1,0:T(8,128)(2,1)S(1)}, bf16[512,512]{1,0:T(8,128)(2,1)S(1)}, u32[]{:S(2)}, u32[]{:S(2)}) collective-permute-start(bf16[512,512]{1,0:T(8,128)(2,1)S(1)} %get-tuple-element.143.refs_2_), channel_id=1, source_target_pairs={{0,2},{1,3},{2,0},{3,1},{4,6},{5,7},{6,4},{7,5},{8,10},{9,11},{10,... | collective-permute-start | bytes 1572872 | tf_op jit(solution)/shard_map/ppermute | solution.py:352
  163.2 2.7 %collective-permute-start.32 = (bf16[128,512]{1,0:T(8,128)(2,1)S(1)}, bf16[128,512]{1,0:T(8,128)(2,1)S(1)}, u32[]{:S(2)}, u32[]{:S(2)}) collective-permute-start(bf16[128,512]{1,0:T(8,128)(2,1)S(1)} %pad_maximum_fusion.4), channel_id=1, source_target_pairs={{0,2},{1,3},{2,0},{3,1},{4,6},{5,7},{6,4},{7,5},{8,10},{9,11},{10,... | collective-permute-start | bytes 393224 | tf_op jit(solution)/shard_map/ppermute | solution.py:352
  167.6 6.4 %collective-permute-done.32 = bf16[128,512]{1,0:T(8,128)(2,1)S(1)} collective-permute-done((bf16[128,512]{1,0:T(8,128)(2,1)S(1)}, bf16[128,512]{1,0:T(8,128)(2,1)S(1)}, u32[]{:S(2)}, u32[]{:S(2)}) %collective-permute-start.32) | collective-permute-done | bytes 131104 | tf_op jit(solution)/shard_map/ppermute | solution.py:352
  174.0 2.6 %collective-permute-done.31 = bf16[128,512]{1,0:T(8,128)(2,1)S(1)} collective-permute-done((bf16[128,512]{1,0:T(8,128)(2,1)S(1)}, bf16[128,512]{1,0:T(8,128)(2,1)S(1)}, u32[]{:S(2)}, u32[]{:S(2)}) %collective-permute-start.31) | collective-permute-done | bytes 131104 | tf_op jit(solution)/shard_map/ppermute | solution.py:352
  185.8 3.3 %collective-permute-done.38 = bf16[128,512]{1,0:T(8,128)(2,1)S(1)} collective-permute-done((bf16[128,512]{1,0:T(8,128)(2,1)S(1)}, bf16[128,512]{1,0:T(8,128)(2,1)S(1)}, u32[]{:S(2)}, u32[]{:S(2)}) %collective-permute-start.38) | collective-permute-done | bytes 131104 | tf_op jit(solution)/shard_map/ppermute | solution.py:352
  189.2 4.3 %collective-permute-done.37 = bf16[128,512]{1,0:T(8,128)(2,1)S(1)} collective-permute-done((bf16[128,512]{1,0:T(8,128)(2,1)S(1)}, bf16[128,512]{1,0:T(8,128)(2,1)S(1)}, u32[]{:S(2)}, u32[]{:S(2)}) %collective-permute-start.37) | collective-permute-done | bytes 131104 | tf_op jit(solution)/shard_map/ppermute | solution.py:352
  195.6 13.2 %merge.1 = bf16[1024,1792]{1,0:T(8,128)(2,1)} custom-call(s32[2]{0:T(128)S(1)} %pad_add_fusion.places_ref, bf16[512,1024]{1,0:T(8,128)(2,1)} %all-gather.2.cloned.1.call-done.left_hbm, f32[8,64,64]{2,1,0:T(8,128)S(1)} %get-tuple-element.132.middle, bf16[4,128,512]{2,1,0:T(8,128)(2,1)S(1)} %pad_maximum_fusion.refs_0_, ...), custom_call_target="tpu_custom_call" | custom-call | flops 1024 | bytes 1024 | tf_op jit(solution)/shard_map/merge/pallas_call | solution.py:480
  (107 shorter events, 74.6 us)
Async XLA Ops:
  6.5 139.9 %all-gather.2.cloned.1.call-start = ((), (), s32[]{:S(2)}) async-start(), calls=%async_computation | async-start | bytes 1179648 | tf_op jit(solution)/shard_map/all_gather | solution.py:444
  6.5 17.2 %collective-permute-start.1 = (bf16[64,3584]{1,0:T(8,128)(2,1)}, bf16[64,3584]{1,0:T(8,128)(2,1)S(1)}, u32[]{:S(2)}, u32[]{:S(2)}) collective-permute-start(bf16[64,3584]{1,0:T(8,128)(2,1)} %bitcast.34), channel_id=1, source_target_pairs={{0,2},{1,3},{2,0},{3,1},{4,6},{5,7},{6,4},{7,5},{8,10},{9,11},{10,... | collective-permute-start | bytes 1376264 | tf_op jit(solution)/shard_map/ppermute | solution.py:352
  9.5 14.2 %collective-permute-start = (bf16[64,3584]{1,0:T(8,128)(2,1)}, bf16[64,3584]{1,0:T(8,128)(2,1)S(1)}, u32[]{:S(2)}, u32[]{:S(2)}) collective-permute-start(bf16[64,3584]{1,0:T(8,128)(2,1)} %bitcast.35), channel_id=1, source_target_pairs={{0,1},{1,0},{2,3},{3,2},{4,5},{5,4},{6,7},{7,6},{8,9},{9,8},{10,11... | collective-permute-start | bytes 1376264 | tf_op jit(solution)/shard_map/ppermute | solution.py:352
  36.1 14.5 %collective-permute-start.4 = (bf16[64,3584]{1,0:T(8,128)(2,1)S(1)}, bf16[64,3584]{1,0:T(8,128)(2,1)S(1)}, u32[]{:S(2)}, u32[]{:S(2)}) collective-permute-start(bf16[64,3584]{1,0:T(8,128)(2,1)S(1)} %first_right.4), channel_id=1, source_target_pairs={{0,3},{1,2},{2,1},{3,0},{4,7},{5,6},{6,5},{7,4},{8,11},{9,10},{10,... | collective-permute-start | bytes 1376264 | tf_op jit(solution)/shard_map/ppermute | solution.py:352
  38.9 17.7 %collective-permute-start.5 = (bf16[64,3584]{1,0:T(8,128)(2,1)S(1)}, bf16[64,3584]{1,0:T(8,128)(2,1)S(1)}, u32[]{:S(2)}, u32[]{:S(2)}) collective-permute-start(bf16[64,3584]{1,0:T(8,128)(2,1)S(1)} %first_right.6), channel_id=1, source_target_pairs={{0,1},{1,0},{2,3},{3,2},{4,5},{5,4},{6,7},{7,6},{8,9},{9,8},{10,11... | collective-permute-start | bytes 1376264 | tf_op jit(solution)/shard_map/ppermute | solution.py:352
  39.4 18.0 %collective-permute-start.6 = (bf16[64,3584]{1,0:T(8,128)(2,1)S(1)}, bf16[64,3584]{1,0:T(8,128)(2,1)S(1)}, u32[]{:S(2)}, u32[]{:S(2)}) collective-permute-start(bf16[64,3584]{1,0:T(8,128)(2,1)S(1)} %first_right.5), channel_id=1, source_target_pairs={{0,2},{1,3},{2,0},{3,1},{4,6},{5,7},{6,4},{7,5},{8,10},{9,11},{10,... | collective-permute-start | bytes 1376264 | tf_op jit(solution)/shard_map/ppermute | solution.py:352
  57.6 12.5 %collective-permute-start.8 = (bf16[64,3584]{1,0:T(8,128)(2,1)S(1)}, bf16[64,3584]{1,0:T(8,128)(2,1)S(1)}, u32[]{:S(2)}, u32[]{:S(2)}) collective-permute-start(bf16[64,3584]{1,0:T(8,128)(2,1)S(1)} %add_convert_fusion.refs_0_), channel_id=1, source_target_pairs={{0,2},{1,3},{2,0},{3,1},{4,6},{5,7},{6,4},{7,5},{8,10},{9,11},{10,... | collective-permute-start | bytes 1376264 | tf_op jit(solution)/shard_map/ppermute | solution.py:352
  58.4 12.2 %collective-permute-start.7 = (bf16[64,3584]{1,0:T(8,128)(2,1)S(1)}, bf16[64,3584]{1,0:T(8,128)(2,1)S(1)}, u32[]{:S(2)}, u32[]{:S(2)}) collective-permute-start(bf16[64,3584]{1,0:T(8,128)(2,1)S(1)} %add_convert_fusion.refs_0_), channel_id=1, source_target_pairs={{0,1},{1,0},{2,3},{3,2},{4,5},{5,4},{6,7},{7,6},{8,9},{9,8},{10,11... | collective-permute-start | bytes 1376264 | tf_op jit(solution)/shard_map/ppermute | solution.py:352
  90.9 15.9 %collective-permute-start.14 = (bf16[8,64,512]{2,1,0:T(8,128)(2,1)S(1)}, bf16[8,64,512]{2,1,0:T(8,128)(2,1)S(1)}, u32[]{:S(2)}, u32[]{:S(2)}) collective-permute-start(bf16[8,64,512]{2,1,0:T(8,128)(2,1)S(1)} %second_right.3), channel_id=1, source_target_pairs={{0,3},{1,2},{2,1},{3,0},{4,7},{5,6},{6,5},{7,4},{8,11},{9,10},{10,... | collective-permute-start | bytes 1572872 | tf_op jit(solution)/shard_map/ppermute | solution.py:352
  95.5 18.5 %collective-permute-start.15 = (bf16[8,64,512]{2,1,0:T(8,128)(2,1)S(1)}, bf16[8,64,512]{2,1,0:T(8,128)(2,1)S(1)}, u32[]{:S(2)}, u32[]{:S(2)}) collective-permute-start(bf16[8,64,512]{2,1,0:T(8,128)(2,1)S(1)} %second_right.5), channel_id=1, source_target_pairs={{0,1},{1,0},{2,3},{3,2},{4,5},{5,4},{6,7},{7,6},{8,9},{9,8},{10,11... | collective-permute-start | bytes 1572872 | tf_op jit(solution)/shard_map/ppermute | solution.py:352
  97.0 17.7 %collective-permute-start.16 = (bf16[8,64,512]{2,1,0:T(8,128)(2,1)S(1)}, bf16[8,64,512]{2,1,0:T(8,128)(2,1)S(1)}, u32[]{:S(2)}, u32[]{:S(2)}) collective-permute-start(bf16[8,64,512]{2,1,0:T(8,128)(2,1)S(1)} %second_right.4), channel_id=1, source_target_pairs={{0,2},{1,3},{2,0},{3,1},{4,6},{5,7},{6,4},{7,5},{8,10},{9,11},{10,... | collective-permute-start | bytes 1572872 | tf_op jit(solution)/shard_map/ppermute | solution.py:352
  127.8 12.0 %collective-permute-start.21 = (bf16[64,640]{1,0:T(8,128)(2,1)S(1)}, bf16[64,640]{1,0:T(8,128)(2,1)S(1)}, u32[]{:S(2)}, u32[]{:S(2)}) collective-permute-start(bf16[64,640]{1,0:T(8,128)(2,1)S(1)} %get-tuple-element.126), channel_id=1, source_target_pairs={{0,8},{4,12},{8,0},{12,4},{16,24},{20,28},{24,16},{28,20},{1,9},{5... | collective-permute-start | bytes 245768 | tf_op jit(solution)/shard_map/ppermute | solution.py:352
  129.4 12.0 %collective-permute-start.22 = (bf16[64,640]{1,0:T(8,128)(2,1)S(1)}, bf16[64,640]{1,0:T(8,128)(2,1)S(1)}, u32[]{:S(2)}, u32[]{:S(2)}) collective-permute-start(bf16[64,640]{1,0:T(8,128)(2,1)S(1)} %get-tuple-element.127), channel_id=1, source_target_pairs={{0,12},{4,8},{8,4},{12,0},{16,28},{20,24},{24,20},{28,16},{1,13},{... | collective-permute-start | bytes 245768 | tf_op jit(solution)/shard_map/ppermute | solution.py:352
  129.7 11.8 %collective-permute-start.23 = (bf16[64,640]{1,0:T(8,128)(2,1)S(1)}, bf16[64,640]{1,0:T(8,128)(2,1)S(1)}, u32[]{:S(2)}, u32[]{:S(2)}) collective-permute-start(bf16[64,640]{1,0:T(8,128)(2,1)S(1)} %get-tuple-element.128), channel_id=1, source_target_pairs={{0,16},{4,20},{8,24},{12,28},{16,0},{20,4},{24,8},{28,12},{1,17},{... | collective-permute-start | bytes 245768 | tf_op jit(solution)/shard_map/ppermute | solution.py:352
  132.3 11.4 %collective-permute-start.25 = (bf16[64,640]{1,0:T(8,128)(2,1)S(1)}, bf16[64,640]{1,0:T(8,128)(2,1)S(1)}, u32[]{:S(2)}, u32[]{:S(2)}) collective-permute-start(bf16[64,640]{1,0:T(8,128)(2,1)S(1)} %get-tuple-element.130), channel_id=1, source_target_pairs={{0,24},{4,28},{8,16},{12,20},{16,8},{20,12},{24,0},{28,4},{1,25},{... | collective-permute-start | bytes 245768 | tf_op jit(solution)/shard_map/ppermute | solution.py:352
  151.1 10.0 %collective-permute-start.28 = (bf16[64,512]{1,0:T(8,128)(2,1)S(1)}, bf16[64,512]{1,0:T(8,128)(2,1)S(1)}, u32[]{:S(2)}, u32[]{:S(2)}) collective-permute-start(bf16[64,512]{1,0:T(8,128)(2,1)S(1)} %get-tuple-element.147), channel_id=1, source_target_pairs={{0,8},{4,12},{8,0},{12,4},{16,24},{20,28},{24,16},{28,20},{1,9},{5... | collective-permute-start | bytes 196616 | tf_op jit(solution)/shard_map/ppermute | solution.py:352
  156.7 21.2 %collective-permute-start.35 = (bf16[512,512]{1,0:T(8,128)(2,1)S(1)}, bf16[512,512]{1,0:T(8,128)(2,1)S(1)}, u32[]{:S(2)}, u32[]{:S(2)}) collective-permute-start(bf16[512,512]{1,0:T(8,128)(2,1)S(1)} %get-tuple-element.143.refs_2_), channel_id=1, source_target_pairs={{0,2},{1,3},{2,0},{3,1},{4,6},{5,7},{6,4},{7,5},{8,10},{9,11},{10,... | collective-permute-start | bytes 1572872 | tf_op jit(solution)/shard_map/ppermute | solution.py:352
  159.3 18.5 %collective-permute-start.34 = (bf16[512,512]{1,0:T(8,128)(2,1)S(1)}, bf16[512,512]{1,0:T(8,128)(2,1)S(1)}, u32[]{:S(2)}, u32[]{:S(2)}) collective-permute-start(bf16[512,512]{1,0:T(8,128)(2,1)S(1)} %get-tuple-element.143.refs_2_), channel_id=1, source_target_pairs={{0,1},{1,0},{2,3},{3,2},{4,5},{5,4},{6,7},{7,6},{8,9},{9,8},{10,11... | collective-permute-start | bytes 1572872 | tf_op jit(solution)/shard_map/ppermute | solution.py:352
  163.2 10.9 %collective-permute-start.32 = (bf16[128,512]{1,0:T(8,128)(2,1)S(1)}, bf16[128,512]{1,0:T(8,128)(2,1)S(1)}, u32[]{:S(2)}, u32[]{:S(2)}) collective-permute-start(bf16[128,512]{1,0:T(8,128)(2,1)S(1)} %pad_maximum_fusion.4), channel_id=1, source_target_pairs={{0,2},{1,3},{2,0},{3,1},{4,6},{5,7},{6,4},{7,5},{8,10},{9,11},{10,... | collective-permute-start | bytes 393224 | tf_op jit(solution)/shard_map/ppermute | solution.py:352
  165.9 10.8 %collective-permute-start.31 = (bf16[128,512]{1,0:T(8,128)(2,1)S(1)}, bf16[128,512]{1,0:T(8,128)(2,1)S(1)}, u32[]{:S(2)}, u32[]{:S(2)}) collective-permute-start(bf16[128,512]{1,0:T(8,128)(2,1)S(1)} %pad_maximum_fusion.4), channel_id=1, source_target_pairs={{0,1},{1,0},{2,3},{3,2},{4,5},{5,4},{6,7},{7,6},{8,9},{9,8},{10,11... | collective-permute-start | bytes 393224 | tf_op jit(solution)/shard_map/ppermute | solution.py:352
  167.6 10.1 %collective-permute-start.33 = (bf16[128,512]{1,0:T(8,128)(2,1)S(1)}, bf16[128,512]{1,0:T(8,128)(2,1)S(1)}, u32[]{:S(2)}, u32[]{:S(2)}) collective-permute-start(bf16[128,512]{1,0:T(8,128)(2,1)S(1)} %pad_maximum_fusion.4), channel_id=1, source_target_pairs={{0,3},{1,2},{2,1},{3,0},{4,7},{5,6},{6,5},{7,4},{8,11},{9,10},{10,... | collective-permute-start | bytes 393224 | tf_op jit(solution)/shard_map/ppermute | solution.py:352
  177.9 15.7 %collective-permute-start.39 = (bf16[256,512]{1,0:T(8,128)(2,1)S(1)}, bf16[256,512]{1,0:T(8,128)(2,1)S(1)}, u32[]{:S(2)}, u32[]{:S(2)}) collective-permute-start(bf16[256,512]{1,0:T(8,128)(2,1)S(1)} %slice.38), channel_id=1, source_target_pairs={{0,1},{1,0},{2,3},{3,2},{4,5},{5,4},{6,7},{7,6},{8,9},{9,8},{10,11... | collective-permute-start | bytes 786440 | tf_op jit(solution)/shard_map/ppermute | solution.py:352
  179.7 13.9 %collective-permute-start.40 = (bf16[256,512]{1,0:T(8,128)(2,1)S(1)}, bf16[256,512]{1,0:T(8,128)(2,1)S(1)}, u32[]{:S(2)}, u32[]{:S(2)}) collective-permute-start(bf16[256,512]{1,0:T(8,128)(2,1)S(1)} %slice.39), channel_id=1, source_target_pairs={{0,2},{1,3},{2,0},{3,1},{4,6},{5,7},{6,4},{7,5},{8,10},{9,11},{10,... | collective-permute-start | bytes 786440 | tf_op jit(solution)/shard_map/ppermute | solution.py:352
  183.0 10.5 %collective-permute-start.37 = (bf16[128,512]{1,0:T(8,128)(2,1)S(1)}, bf16[128,512]{1,0:T(8,128)(2,1)S(1)}, u32[]{:S(2)}, u32[]{:S(2)}) collective-permute-start(bf16[128,512]{1,0:T(8,128)(2,1)S(1)} %add_convert_fusion.2), channel_id=1, source_target_pairs={{0,16},{4,20},{8,24},{12,28},{16,0},{20,4},{24,8},{28,12},{1,17},{... | collective-permute-start | bytes 393224 | tf_op jit(solution)/shard_map/ppermute | solution.py:352
  (23 other events, 155.2 us)
Sparse Core Ops, SparseCore 0:
  114.8 27.0 all-gather.1

commit v3 on v2

--- a/solution.py
+++ b/solution.py
@@ -312,7 +312,7 @@
 
 
 def merge_kernel(count, ckpt_count, places_ref, left_hbm, middle, *refs):
-    columns, pieces, refs = refs[:2], refs[2:2 + count], refs[2 + count:]
+    columns, pieces, refs = refs[:2], refs[2], refs[3:]
     out, gram, product, spare, left_gram, left_product, left_spare, other, left_other, wide, strips, stack, sem, sems = refs
     real = out.shape[1]
     load = pltpu.make_async_copy(left_hbm, stack, sem)
@@ -323,11 +323,11 @@
             rows = pl.ds(pl.multiple_of((places_ref[0] ^ (2 * number + side)) * rank, rank), rank)
             gram[rows, :] = column[number, :rank, :].astype(F32)
             left_gram[rows, :] = column[number, rank:, :].astype(F32)
-    size = pieces[0].shape[1]
+    size = pieces.shape[2]
     wide[...] = jnp.zeros_like(wide)
-    for gap, piece in enumerate(pieces):
-        start = pl.multiple_of(slot_start(places_ref[1] ^ gap, size, real), 128)
-        wide[:, pl.ds(start, size)] += piece[...]
+    for slot in range(count):
+        start = min(slot * size, real - size)
+        wide[:, start:start + size] += pieces[slot]
     polish(ckpt_count, [(gram, product, spare, other), (left_gram, left_product, left_spare, left_other)])
     for index in range(ckpt_count):
         rows = pl.ds(index * rank, rank)
@@ -463,20 +463,15 @@
         name="grams", scalars=1, hbm=1,
     )
     pair_sum = add_up([home, permute(away, "ckpt", 1)]).astype(BF16)
-    right_stack, pair_sum = together(right_stack, pair_sum)
+    gathered = lax.all_gather(right_stack, "rows", axis=0)
     own = add_up([pair_sum[0]] + [permute(pair_sum[n], "ckpt", 2 * n) for n in range(1, groups // 2)]).astype(BF16)
-    near = [permute(right_stack, "rows", gap) for gap in range(1, count) if not gap & (gap - 1)]
     both = add_up(spread(jnp.concatenate([own, left_rows]), "rows")).astype(BF16)
-    both, *near = together(both, *near)
-    right_all = [right_stack] + [None if gap & (gap - 1) else near.pop(0) for gap in range(1, count)]
-    forward(right_all, "rows")
     column = jnp.stack([both] + [permute(both, "ckpt", gap) for gap in range(2, groups, 2)])
-    column, *right_all = together(column, *right_all)
     columns = [column, permute(column, "ckpt", 1)]
 
     step = min(256, rows)
     vmem = pl.BlockSpec(memory_space=pltpu.VMEM)
-    args = [in_hbm, middles, *columns, *right_all]
+    args = [in_hbm, middles, *columns, gathered]
     return pl.pallas_call(
         functools.partial(merge_kernel, count, groups),
         in_specs=[pl.BlockSpec(memory_space=pltpu.SMEM), pl.BlockSpec(memory_space=pltpu.HBM)] + [vmem] * (len(args) - 1),

time: 216 us -> 216 us (level)
  starting transfers between devices: 55.6 us -> 49.7 us
  waiting for transfers between devices: 70.2 us -> 74.2 us
    ppermute x42 -> x38, starting transfers between devices: 55.6 us -> 49.5 us  [permute(): lax.ppermute(value, axis, [(source, source ^ gap) for source in range(cou...]
    ppermute x42 -> x38, waiting for transfers between devices: 70.2 us -> 72.3 us  [permute(): lax.ppermute(value, axis, [(source, source ^ gap) for source in range(cou...]
    unnamed x8 -> x10, local copies, waits for them, and re-layouts: 10.4 us -> 12 us
  transfers between devices with their start and end apart: 43 -> 40, of which waited for: 26 -> 28; matrix products, arithmetic and copies ran while one was open for 0% -> 0% of each run, Pallas kernels for 16% -> 16%
where the time goes in v3:
time: 216 us; the launch traced here: 215 us
  waiting for transfers between devices  74.2 us (34%)
  Pallas kernels  63.7 us (29%)
  starting transfers between devices  49.7 us (23%)
  between operations  14.3 us (7%)
  local copies, waits for them, and re-layouts  12.1 us (6%)
    ppermute x38, waiting for transfers between devices, permute(): lax.ppermute(value, axis, [(source, source ^ gap) for source in range(cou...  72.3 us
    ppermute x38, starting transfers between devices, permute(): lax.ppermute(value, axis, [(source, source ^ gap) for source in range(cou...  49.5 us
    pallas_call x14, Pallas kernels, delta_call(): pl.pallas_call(kernel, in_specs=[pl.BlockSpec(memory_space=pltpu.SMEM)] +...  40.6 us
    pallas_call x1, Pallas kernels, body(): pl.pallas_call(functools.partial(merge_kernel, count, groups), in_specs=[...  13.1 us
    unnamed x10, local copies, waits for them, and re-layouts  12 us
    pallas_call x3, Pallas kernels, small_call(): pl.pallas_call(kernel, in_specs=[spec(i) for i in range(len(args))], out_...  10 us
  transfers between devices with their start and end apart: 40, of which 28 were waited for; matrix products, arithmetic and copies ran while one was open for 0% of the time, Pallas kernels for 16%

profile of v3, /device:TPU:0, one launch (start us, length us, event | category | flops | bytes accessed | tf_op | source)
XLA Modules:
  0.0 215.2 jit_solution(624190602654813288)
XLA Ops:
  6.5 3.0 %collective-permute-start.1 = (bf16[64,3584]{1,0:T(8,128)(2,1)}, bf16[64,3584]{1,0:T(8,128)(2,1)S(1)}, u32[]{:S(2)}, u32[]{:S(2)}) collective-permute-start(bf16[64,3584]{1,0:T(8,128)(2,1)} %bitcast.38), channel_id=1, source_target_pairs={{0,2},{1,3},{2,0},{3,1},{4,6},{5,7},{6,4},{7,5},{8,10},{9,11},{10,... | collective-permute-start | bytes 1376264 | tf_op jit(solution)/shard_map/ppermute | solution.py:352
  11.0 9.3 %copy-done = bf16[1,1024,14336]{2,1,0:T(8,128)(2,1)S(1)} copy-done((bf16[1,1024,14336]{2,1,0:T(8,128)(2,1)S(1)}, bf16[1,1024,14336]{2,1,0:T(8,128)(2,1)}, u32[]{:S(2)}) %copy-start) | copy-done | bytes 29360152
  24.4 4.6 %first_left_part.3.refs_4_ = f32[64,1024]{1,0:T(8,128)S(1)} custom-call(s32[1]{0:T(128)} %bitcast.1.place_ref, bf16[1024,14336]{1,0:T(8,128)(2,1)S(1)} %bitcast.24, bf16[64,3584]{1,0:T(8,128)(2,1)S(1)} %collective-permute-done.refs_0_.refs_1_, bf16[64,3584]{1,0:T(8,128)(2,1)S(1)} %collective-permute-done.1.refs_1_.refs_2_, f32[64,1024]{1,0:T(8,128)S(1)} %first_left_part.2.refs_2_), custom_call_target="tpu_custom_call" | custom-call | flops 1024 | bytes 1024 | tf_op jit(solution)/shard_map/first_left_part/pallas_call | solution.py:134
  41.1 9.5 %collective-permute-done.4 = bf16[64,3584]{1,0:T(8,128)(2,1)S(1)} collective-permute-done((bf16[64,3584]{1,0:T(8,128)(2,1)S(1)}, bf16[64,3584]{1,0:T(8,128)(2,1)S(1)}, u32[]{:S(2)}, u32[]{:S(2)}) %collective-permute-start.4) | collective-permute-done | bytes 458784 | tf_op jit(solution)/shard_map/ppermute | solution.py:352
  51.9 4.8 %collective-permute-done.5 = bf16[64,3584]{1,0:T(8,128)(2,1)S(1)} collective-permute-done((bf16[64,3584]{1,0:T(8,128)(2,1)S(1)}, bf16[64,3584]{1,0:T(8,128)(2,1)S(1)}, u32[]{:S(2)}, u32[]{:S(2)}) %collective-permute-start.5) | collective-permute-done | bytes 458784 | tf_op jit(solution)/shard_map/ppermute | solution.py:352
  62.2 7.9 %collective-permute-done.8.refs_1_.refs_2_ = bf16[64,3584]{1,0:T(8,128)(2,1)S(1)} collective-permute-done((bf16[64,3584]{1,0:T(8,128)(2,1)S(1)}, bf16[64,3584]{1,0:T(8,128)(2,1)S(1)}, u32[]{:S(2)}, u32[]{:S(2)}) %collective-permute-start.8) | collective-permute-done | bytes 458784 | tf_op jit(solution)/shard_map/ppermute | solution.py:352
  73.4 4.7 %second_left_part.3.refs_4_ = f32[64,1024]{1,0:T(8,128)S(1)} custom-call(s32[1]{0:T(128)} %bitcast.1.place_ref, bf16[1024,14336]{1,0:T(8,128)(2,1)S(1)} %bitcast.31, bf16[64,3584]{1,0:T(8,128)(2,1)S(1)} %collective-permute-done.7.refs_0_.refs_1_, bf16[64,3584]{1,0:T(8,128)(2,1)S(1)} %collective-permute-done.8.refs_1_.refs_2_, ...), custom_call_target="tpu_custom_call" | custom-call | flops 1024 | bytes 1024 | tf_op jit(solution)/shard_map/second_left_part/pallas_call | solution.py:134
  78.3 7.6 %second_left.1 = (bf16[64,1024]{1,0:T(8,128)(2,1)S(1)}, f32[64,64]{1,0:T(8,128)S(1)}) custom-call(s32[1]{0:T(128)} %bitcast.1.place_ref, bf16[1024,14336]{1,0:T(8,128)(2,1)S(1)} %bitcast.32, bf16[64,3584]{1,0:T(8,128)(2,1)S(1)} %add_convert_fusion.refs_0_, bf16[64,3584]{1,0:T(8,128)(2,1)S(1)} %collective-permute-done.7.refs_0_.refs_1_, ...), custom_call_target="tpu_custom_call" | custom-call | flops 1024 | bytes 1024 | tf_op jit(solution)/shard_map/second_left/pallas_call | solution.py:134
  98.2 8.6 %collective-permute-done.14.refs_3_ = bf16[8,64,512]{2,1,0:T(8,128)(2,1)S(1)} collective-permute-done((bf16[8,64,512]{2,1,0:T(8,128)(2,1)S(1)}, bf16[8,64,512]{2,1,0:T(8,128)(2,1)S(1)}, u32[]{:S(2)}, u32[]{:S(2)}) %collective-permute-start.14) | collective-permute-done | bytes 524320 | tf_op jit(solution)/shard_map/ppermute | solution.py:352
  106.8 6.5 %second_own.1 = (bf16[8,64,512]{2,1,0:T(8,128)(2,1)S(1)}, bf16[64,1024]{1,0:T(8,128)(2,1)}, f32[64,64]{1,0:T(8,128)S(1)}) custom-call(s32[1]{0:T(128)} %bitcast.1.place_ref, bf16[1024,14336]{1,0:T(8,128)(2,1)S(1)} %bitcast.36, bf16[64,1024]{1,0:T(8,128)(2,1)S(1)} %get-tuple-element.97.left, f32[64,64]{1,0:T(8,128)S(1)} %get-tuple-element.98.refs_0_, ...), custom_call_target="tpu_custom_call" | custom-call | flops 1024 | bytes 1024 | tf_op jit(solution)/shard_map/second_own/pallas_call | solution.py:134
  121.6 6.1 %right_unit.1 = (bf16[64,640]{1,0:T(8,128)(2,1)S(1)}, bf16[64,640]{1,0:T(8,128)(2,1)S(1)}, bf16[64,640]{1,0:T(8,128)(2,1)S(1)}, bf16[64,640]{1,0:T(8,128)(2,1)S(...) custom-call(s32[1]{0:T(128)} %bitcast.place_ref, ...), custom_call_target="tpu_custom_call" | custom-call | flops 1024 | bytes 1024 | tf_op jit(solution)/shard_map/right_unit/pallas_call | solution.py:212
  129.7 2.6 %collective-permute-start.23 = (bf16[64,640]{1,0:T(8,128)(2,1)S(1)}, bf16[64,640]{1,0:T(8,128)(2,1)S(1)}, u32[]{:S(2)}, u32[]{:S(2)}) collective-permute-start(bf16[64,640]{1,0:T(8,128)(2,1)S(1)} %get-tuple-element.118), channel_id=1, source_target_pairs={{0,16},{4,20},{8,24},{12,28},{16,0},{20,4},{24,8},{28,12},{1,17},{... | collective-permute-start | bytes 245768 | tf_op jit(solution)/shard_map/ppermute | solution.py:352
  132.3 3.6 %collective-permute-start.25 = (bf16[64,640]{1,0:T(8,128)(2,1)S(1)}, bf16[64,640]{1,0:T(8,128)(2,1)S(1)}, u32[]{:S(2)}, u32[]{:S(2)}) collective-permute-start(bf16[64,640]{1,0:T(8,128)(2,1)S(1)} %get-tuple-element.120), channel_id=1, source_target_pairs={{0,24},{4,28},{8,16},{12,20},{16,8},{20,12},{24,0},{28,4},{1,25},{... | collective-permute-start | bytes 245768 | tf_op jit(solution)/shard_map/ppermute | solution.py:352
  135.9 3.4 %collective-permute-done.21.refs_2_ = bf16[64,640]{1,0:T(8,128)(2,1)S(1)} collective-permute-done((bf16[64,640]{1,0:T(8,128)(2,1)S(1)}, bf16[64,640]{1,0:T(8,128)(2,1)S(1)}, u32[]{:S(2)}, u32[]{:S(2)}) %collective-permute-start.21) | collective-permute-done | bytes 81952 | tf_op jit(solution)/shard_map/ppermute | solution.py:352
  141.5 2.4 %collective-permute-done.24.refs_5_ = bf16[64,640]{1,0:T(8,128)(2,1)S(1)} collective-permute-done((bf16[64,640]{1,0:T(8,128)(2,1)S(1)}, bf16[64,640]{1,0:T(8,128)(2,1)S(1)}, u32[]{:S(2)}, u32[]{:S(2)}) %collective-permute-start.24) | collective-permute-done | bytes 81952 | tf_op jit(solution)/shard_map/ppermute | solution.py:352
  145.6 3.3 %grams.1 = (bf16[512,512]{1,0:T(8,128)(2,1)}, f32[8,64,64]{2,1,0:T(8,128)S(1)}, bf16[4,64,512]{2,1,0:T(8,128)(2,1)S(1)}, bf16[4,64,512]{2,1,0:T(8,128)(2,1)S(1)}, bf16[64,512]{1,0:T(8,128)(2,1)S(1)}) custom-call(s32[1]{0:T(128)} %bitcast.place_ref, bf16[512,1024]{1,0:T(8,128)(2,1)} %all-gather.4.cloned.1.call-done.left_hbm, ...), custom_call_target="tpu_custom_call" | custom-call | flops 1024 | bytes 1024 | tf_op jit(solution)/shard_map/grams/pallas_call | solution.py:212
  150.7 4.1 %collective-permute-start.28 = (bf16[64,512]{1,0:T(8,128)(2,1)S(1)}, bf16[64,512]{1,0:T(8,128)(2,1)S(1)}, u32[]{:S(2)}, u32[]{:S(2)}) collective-permute-start(bf16[64,512]{1,0:T(8,128)(2,1)S(1)} %get-tuple-element.127), channel_id=1, source_target_pairs={{0,8},{4,12},{8,0},{12,4},{16,24},{20,28},{24,16},{28,20},{1,9},{5... | collective-permute-start | bytes 196616 | tf_op jit(solution)/shard_map/ppermute | solution.py:352
  157.2 4.4 %collective-permute-done.30 = bf16[64,512]{1,0:T(8,128)(2,1)S(1)} collective-permute-done((bf16[64,512]{1,0:T(8,128)(2,1)S(1)}, bf16[64,512]{1,0:T(8,128)(2,1)S(1)}, u32[]{:S(2)}, u32[]{:S(2)}) %collective-permute-start.30) | collective-permute-done | bytes 65568 | tf_op jit(solution)/shard_map/ppermute | solution.py:352
  163.7 2.9 %collective-permute-start.32 = (bf16[128,512]{1,0:T(8,128)(2,1)S(1)}, bf16[128,512]{1,0:T(8,128)(2,1)S(1)}, u32[]{:S(2)}, u32[]{:S(2)}) collective-permute-start(bf16[128,512]{1,0:T(8,128)(2,1)S(1)} %pad_maximum_fusion.3), channel_id=1, source_target_pairs={{0,2},{1,3},{2,0},{3,1},{4,6},{5,7},{6,4},{7,5},{8,10},{9,11},{10,... | collective-permute-start | bytes 393224 | tf_op jit(solution)/shard_map/ppermute | solution.py:352
  168.1 3.6 %collective-permute-done.32 = bf16[128,512]{1,0:T(8,128)(2,1)S(1)} collective-permute-done((bf16[128,512]{1,0:T(8,128)(2,1)S(1)}, bf16[128,512]{1,0:T(8,128)(2,1)S(1)}, u32[]{:S(2)}, u32[]{:S(2)}) %collective-permute-start.32) | collective-permute-done | bytes 131104 | tf_op jit(solution)/shard_map/ppermute | solution.py:352
  175.2 3.4 %collective-permute-start.36 = (bf16[128,512]{1,0:T(8,128)(2,1)S(1)}, bf16[128,512]{1,0:T(8,128)(2,1)S(1)}, u32[]{:S(2)}, u32[]{:S(2)}) collective-permute-start(bf16[128,512]{1,0:T(8,128)(2,1)S(1)} %add_convert_fusion.2), channel_id=1, source_target_pairs={{0,24},{4,28},{8,16},{12,20},{16,8},{20,12},{24,0},{28,4},{1,25},{... | collective-permute-start | bytes 393224 | tf_op jit(solution)/shard_map/ppermute | solution.py:352
  179.7 3.9 %collective-permute-done.36 = bf16[128,512]{1,0:T(8,128)(2,1)S(1)} collective-permute-done((bf16[128,512]{1,0:T(8,128)(2,1)S(1)}, bf16[128,512]{1,0:T(8,128)(2,1)S(1)}, u32[]{:S(2)}, u32[]{:S(2)}) %collective-permute-start.36) | collective-permute-done | bytes 131104 | tf_op jit(solution)/shard_map/ppermute | solution.py:352
  183.5 6.3 %collective-permute-done.35 = bf16[128,512]{1,0:T(8,128)(2,1)S(1)} collective-permute-done((bf16[128,512]{1,0:T(8,128)(2,1)S(1)}, bf16[128,512]{1,0:T(8,128)(2,1)S(1)}, u32[]{:S(2)}, u32[]{:S(2)}) %collective-permute-start.35) | collective-permute-done | bytes 131104 | tf_op jit(solution)/shard_map/ppermute | solution.py:352
  195.3 13.1 %merge.1 = bf16[1024,1792]{1,0:T(8,128)(2,1)} custom-call(s32[2]{0:T(128)S(1)} %pad_add_fusion.places_ref, bf16[512,1024]{1,0:T(8,128)(2,1)} %all-gather.4.cloned.1.call-done.left_hbm, f32[8,64,64]{2,1,0:T(8,128)S(1)} %get-tuple-element.122.middle, bf16[4,128,512]{2,1,0:T(8,128)(2,1)S(1)} %pad_maximum_fusion.refs_0_, ...), custom_call_target="tpu_custom_call" | custom-call | flops 1024 | bytes 1024 | tf_op jit(solution)/shard_map/merge/pallas_call | solution.py:475
  (101 shorter events, 71.5 us)
Async XLA Ops:
  6.5 139.1 %all-gather.4.cloned.1.call-start = ((), (), s32[]{:S(2)}) async-start(), calls=%async_computation | async-start | bytes 1179648 | tf_op jit(solution)/shard_map/all_gather | solution.py:444
  6.5 17.2 %collective-permute-start.1 = (bf16[64,3584]{1,0:T(8,128)(2,1)}, bf16[64,3584]{1,0:T(8,128)(2,1)S(1)}, u32[]{:S(2)}, u32[]{:S(2)}) collective-permute-start(bf16[64,3584]{1,0:T(8,128)(2,1)} %bitcast.38), channel_id=1, source_target_pairs={{0,2},{1,3},{2,0},{3,1},{4,6},{5,7},{6,4},{7,5},{8,10},{9,11},{10,... | collective-permute-start | bytes 1376264 | tf_op jit(solution)/shard_map/ppermute | solution.py:352
  9.5 14.2 %collective-permute-start = (bf16[64,3584]{1,0:T(8,128)(2,1)}, bf16[64,3584]{1,0:T(8,128)(2,1)S(1)}, u32[]{:S(2)}, u32[]{:S(2)}) collective-permute-start(bf16[64,3584]{1,0:T(8,128)(2,1)} %bitcast.39), channel_id=1, source_target_pairs={{0,1},{1,0},{2,3},{3,2},{4,5},{5,4},{6,7},{7,6},{8,9},{9,8},{10,11... | collective-permute-start | bytes 1376264 | tf_op jit(solution)/shard_map/ppermute | solution.py:352
  23.8 6.8 %collective-permute-start.2 = (bf16[32,3584]{1,0:T(8,128)(2,1)S(1)}, bf16[32,3584]{1,0:T(8,128)(2,1)S(1)}, u32[]{:S(2)}, u32[]{:S(2)}) collective-permute-start(bf16[32,3584]{1,0:T(8,128)(2,1)S(1)} %slice.24), channel_id=1, source_target_pairs={{0,1},{1,0},{2,3},{3,2},{4,5},{5,4},{6,7},{7,6},{8,9},{9,8},{10,11... | collective-permute-start | bytes 688136 | tf_op jit(solution)/shard_map/ppermute | solution.py:352
  36.1 14.5 %collective-permute-start.4 = (bf16[64,3584]{1,0:T(8,128)(2,1)S(1)}, bf16[64,3584]{1,0:T(8,128)(2,1)S(1)}, u32[]{:S(2)}, u32[]{:S(2)}) collective-permute-start(bf16[64,3584]{1,0:T(8,128)(2,1)S(1)} %first_right.4), channel_id=1, source_target_pairs={{0,3},{1,2},{2,1},{3,0},{4,7},{5,6},{6,5},{7,4},{8,11},{9,10},{10,... | collective-permute-start | bytes 1376264 | tf_op jit(solution)/shard_map/ppermute | solution.py:352
  39.0 17.7 %collective-permute-start.5 = (bf16[64,3584]{1,0:T(8,128)(2,1)S(1)}, bf16[64,3584]{1,0:T(8,128)(2,1)S(1)}, u32[]{:S(2)}, u32[]{:S(2)}) collective-permute-start(bf16[64,3584]{1,0:T(8,128)(2,1)S(1)} %first_right.6), channel_id=1, source_target_pairs={{0,1},{1,0},{2,3},{3,2},{4,5},{5,4},{6,7},{7,6},{8,9},{9,8},{10,11... | collective-permute-start | bytes 1376264 | tf_op jit(solution)/shard_map/ppermute | solution.py:352
  39.4 18.0 %collective-permute-start.6 = (bf16[64,3584]{1,0:T(8,128)(2,1)S(1)}, bf16[64,3584]{1,0:T(8,128)(2,1)S(1)}, u32[]{:S(2)}, u32[]{:S(2)}) collective-permute-start(bf16[64,3584]{1,0:T(8,128)(2,1)S(1)} %first_right.5), channel_id=1, source_target_pairs={{0,2},{1,3},{2,0},{3,1},{4,6},{5,7},{6,4},{7,5},{8,10},{9,11},{10,... | collective-permute-start | bytes 1376264 | tf_op jit(solution)/shard_map/ppermute | solution.py:352
  57.6 12.5 %collective-permute-start.8 = (bf16[64,3584]{1,0:T(8,128)(2,1)S(1)}, bf16[64,3584]{1,0:T(8,128)(2,1)S(1)}, u32[]{:S(2)}, u32[]{:S(2)}) collective-permute-start(bf16[64,3584]{1,0:T(8,128)(2,1)S(1)} %add_convert_fusion.refs_0_), channel_id=1, source_target_pairs={{0,2},{1,3},{2,0},{3,1},{4,6},{5,7},{6,4},{7,5},{8,10},{9,11},{10,... | collective-permute-start | bytes 1376264 | tf_op jit(solution)/shard_map/ppermute | solution.py:352
  58.4 12.2 %collective-permute-start.7 = (bf16[64,3584]{1,0:T(8,128)(2,1)S(1)}, bf16[64,3584]{1,0:T(8,128)(2,1)S(1)}, u32[]{:S(2)}, u32[]{:S(2)}) collective-permute-start(bf16[64,3584]{1,0:T(8,128)(2,1)S(1)} %add_convert_fusion.refs_0_), channel_id=1, source_target_pairs={{0,1},{1,0},{2,3},{3,2},{4,5},{5,4},{6,7},{7,6},{8,9},{9,8},{10,11... | collective-permute-start | bytes 1376264 | tf_op jit(solution)/shard_map/ppermute | solution.py:352
  70.6 7.5 %collective-permute-start.9 = (bf16[32,3584]{1,0:T(8,128)(2,1)S(1)}, bf16[32,3584]{1,0:T(8,128)(2,1)S(1)}, u32[]{:S(2)}, u32[]{:S(2)}) collective-permute-start(bf16[32,3584]{1,0:T(8,128)(2,1)S(1)} %slice.26), channel_id=1, source_target_pairs={{0,1},{1,0},{2,3},{3,2},{4,5},{5,4},{6,7},{7,6},{8,9},{9,8},{10,11... | collective-permute-start | bytes 688136 | tf_op jit(solution)/shard_map/ppermute | solution.py:352
  90.9 15.9 %collective-permute-start.14 = (bf16[8,64,512]{2,1,0:T(8,128)(2,1)S(1)}, bf16[8,64,512]{2,1,0:T(8,128)(2,1)S(1)}, u32[]{:S(2)}, u32[]{:S(2)}) collective-permute-start(bf16[8,64,512]{2,1,0:T(8,128)(2,1)S(1)} %second_right.3), channel_id=1, source_target_pairs={{0,3},{1,2},{2,1},{3,0},{4,7},{5,6},{6,5},{7,4},{8,11},{9,10},{10,... | collective-permute-start | bytes 1572872 | tf_op jit(solution)/shard_map/ppermute | solution.py:352
  95.5 18.5 %collective-permute-start.15 = (bf16[8,64,512]{2,1,0:T(8,128)(2,1)S(1)}, bf16[8,64,512]{2,1,0:T(8,128)(2,1)S(1)}, u32[]{:S(2)}, u32[]{:S(2)}) collective-permute-start(bf16[8,64,512]{2,1,0:T(8,128)(2,1)S(1)} %second_right.5), channel_id=1, source_target_pairs={{0,1},{1,0},{2,3},{3,2},{4,5},{5,4},{6,7},{7,6},{8,9},{9,8},{10,11... | collective-permute-start | bytes 1572872 | tf_op jit(solution)/shard_map/ppermute | solution.py:352
  97.0 17.7 %collective-permute-start.16 = (bf16[8,64,512]{2,1,0:T(8,128)(2,1)S(1)}, bf16[8,64,512]{2,1,0:T(8,128)(2,1)S(1)}, u32[]{:S(2)}, u32[]{:S(2)}) collective-permute-start(bf16[8,64,512]{2,1,0:T(8,128)(2,1)S(1)} %second_right.4), channel_id=1, source_target_pairs={{0,2},{1,3},{2,0},{3,1},{4,6},{5,7},{6,4},{7,5},{8,10},{9,11},{10,... | collective-permute-start | bytes 1572872 | tf_op jit(solution)/shard_map/ppermute | solution.py:352
  114.7 79.0 %all-gather.6.cloned.1.call-start = ((), (), s32[]{:S(2)}) async-start(), calls=%async_computation.1 | async-start | bytes 2621440 | tf_op jit(solution)/shard_map/all_gather | solution.py:466
  127.8 11.5 %collective-permute-start.21 = (bf16[64,640]{1,0:T(8,128)(2,1)S(1)}, bf16[64,640]{1,0:T(8,128)(2,1)S(1)}, u32[]{:S(2)}, u32[]{:S(2)}) collective-permute-start(bf16[64,640]{1,0:T(8,128)(2,1)S(1)} %get-tuple-element.116), channel_id=1, source_target_pairs={{0,8},{4,12},{8,0},{12,4},{16,24},{20,28},{24,16},{28,20},{1,9},{5... | collective-permute-start | bytes 245768 | tf_op jit(solution)/shard_map/ppermute | solution.py:352
  129.5 12.0 %collective-permute-start.22 = (bf16[64,640]{1,0:T(8,128)(2,1)S(1)}, bf16[64,640]{1,0:T(8,128)(2,1)S(1)}, u32[]{:S(2)}, u32[]{:S(2)}) collective-permute-start(bf16[64,640]{1,0:T(8,128)(2,1)S(1)} %get-tuple-element.117), channel_id=1, source_target_pairs={{0,12},{4,8},{8,4},{12,0},{16,28},{20,24},{24,20},{28,16},{1,13},{... | collective-permute-start | bytes 245768 | tf_op jit(solution)/shard_map/ppermute | solution.py:352
  129.7 11.8 %collective-permute-start.23 = (bf16[64,640]{1,0:T(8,128)(2,1)S(1)}, bf16[64,640]{1,0:T(8,128)(2,1)S(1)}, u32[]{:S(2)}, u32[]{:S(2)}) collective-permute-start(bf16[64,640]{1,0:T(8,128)(2,1)S(1)} %get-tuple-element.118), channel_id=1, source_target_pairs={{0,16},{4,20},{8,24},{12,28},{16,0},{20,4},{24,8},{28,12},{1,17},{... | collective-permute-start | bytes 245768 | tf_op jit(solution)/shard_map/ppermute | solution.py:352
  132.3 11.6 %collective-permute-start.24 = (bf16[64,640]{1,0:T(8,128)(2,1)S(1)}, bf16[64,640]{1,0:T(8,128)(2,1)S(1)}, u32[]{:S(2)}, u32[]{:S(2)}) collective-permute-start(bf16[64,640]{1,0:T(8,128)(2,1)S(1)} %get-tuple-element.119), channel_id=1, source_target_pairs={{0,20},{4,16},{8,28},{12,24},{16,4},{20,0},{24,12},{28,8},{1,21},{... | collective-permute-start | bytes 245768 | tf_op jit(solution)/shard_map/ppermute | solution.py:352
  132.3 11.6 %collective-permute-start.25 = (bf16[64,640]{1,0:T(8,128)(2,1)S(1)}, bf16[64,640]{1,0:T(8,128)(2,1)S(1)}, u32[]{:S(2)}, u32[]{:S(2)}) collective-permute-start(bf16[64,640]{1,0:T(8,128)(2,1)S(1)} %get-tuple-element.120), channel_id=1, source_target_pairs={{0,24},{4,28},{8,16},{12,20},{16,8},{20,12},{24,0},{28,4},{1,25},{... | collective-permute-start | bytes 245768 | tf_op jit(solution)/shard_map/ppermute | solution.py:352
  163.7 8.0 %collective-permute-start.32 = (bf16[128,512]{1,0:T(8,128)(2,1)S(1)}, bf16[128,512]{1,0:T(8,128)(2,1)S(1)}, u32[]{:S(2)}, u32[]{:S(2)}) collective-permute-start(bf16[128,512]{1,0:T(8,128)(2,1)S(1)} %pad_maximum_fusion.3), channel_id=1, source_target_pairs={{0,2},{1,3},{2,0},{3,1},{4,6},{5,7},{6,4},{7,5},{8,10},{9,11},{10,... | collective-permute-start | bytes 393224 | tf_op jit(solution)/shard_map/ppermute | solution.py:352
  167.8 7.3 %collective-permute-start.33 = (bf16[128,512]{1,0:T(8,128)(2,1)S(1)}, bf16[128,512]{1,0:T(8,128)(2,1)S(1)}, u32[]{:S(2)}, u32[]{:S(2)}) collective-permute-start(bf16[128,512]{1,0:T(8,128)(2,1)S(1)} %pad_maximum_fusion.3), channel_id=1, source_target_pairs={{0,3},{1,2},{2,1},{3,0},{4,7},{5,6},{6,5},{7,4},{8,11},{9,10},{10,... | collective-permute-start | bytes 393224 | tf_op jit(solution)/shard_map/ppermute | solution.py:352
  175.2 8.3 %collective-permute-start.36 = (bf16[128,512]{1,0:T(8,128)(2,1)S(1)}, bf16[128,512]{1,0:T(8,128)(2,1)S(1)}, u32[]{:S(2)}, u32[]{:S(2)}) collective-permute-start(bf16[128,512]{1,0:T(8,128)(2,1)S(1)} %add_convert_fusion.2), channel_id=1, source_target_pairs={{0,24},{4,28},{8,16},{12,20},{16,8},{20,12},{24,0},{28,4},{1,25},{... | collective-permute-start | bytes 393224 | tf_op jit(solution)/shard_map/ppermute | solution.py:352
  178.6 11.2 %collective-permute-start.35 = (bf16[128,512]{1,0:T(8,128)(2,1)S(1)}, bf16[128,512]{1,0:T(8,128)(2,1)S(1)}, u32[]{:S(2)}, u32[]{:S(2)}) collective-permute-start(bf16[128,512]{1,0:T(8,128)(2,1)S(1)} %add_convert_fusion.2), channel_id=1, source_target_pairs={{0,16},{4,20},{8,24},{12,28},{16,0},{20,4},{24,8},{28,12},{1,17},{... | collective-permute-start | bytes 393224 | tf_op jit(solution)/shard_map/ppermute | solution.py:352
  178.6 11.2 %collective-permute-start.34 = (bf16[128,512]{1,0:T(8,128)(2,1)S(1)}, bf16[128,512]{1,0:T(8,128)(2,1)S(1)}, u32[]{:S(2)}, u32[]{:S(2)}) collective-permute-start(bf16[128,512]{1,0:T(8,128)(2,1)S(1)} %add_convert_fusion.2), channel_id=1, source_target_pairs={{0,8},{4,12},{8,0},{12,4},{16,24},{20,28},{24,16},{28,20},{1,9},{5... | collective-permute-start | bytes 393224 | tf_op jit(solution)/shard_map/ppermute | solution.py:352
  (21 other events, 125.3 us)
Sparse Core Ops, SparseCore 0:
  114.8 27.2 all-gather.3
  149.1 44.6 all-gather.5

commit v4 on v3

--- a/solution.py
+++ b/solution.py
@@ -311,29 +311,32 @@
     lax.fori_loop(1, NS_ITERS, step, 0)
 
 
-def merge_kernel(count, ckpt_count, places_ref, left_hbm, middle, *refs):
-    columns, pieces, refs = refs[:2], refs[2], refs[3:]
-    out, gram, product, spare, left_gram, left_product, left_spare, other, left_other, wide, strips, stack, sem, sems = refs
+def merge_kernel(count, ckpt_count, places_ref, left_hbm, right_hbm, middle, *refs):
+    columns, refs = refs[:2], refs[2:]
+    out, gram, product, spare, left_gram, left_product, left_spare, other, left_other, wide, strips, stack, sem, sems, pieces, right_sem = refs
     real = out.shape[1]
     load = pltpu.make_async_copy(left_hbm, stack, sem)
     load.start()
+    right_load = pltpu.make_async_copy(right_hbm, pieces, right_sem)
+    right_load.start()
     rank = middle.shape[1]
     for number in range(ckpt_count // 2):
         for side, column in enumerate(columns):
             rows = pl.ds(pl.multiple_of((places_ref[0] ^ (2 * number + side)) * rank, rank), rank)
             gram[rows, :] = column[number, :rank, :].astype(F32)
             left_gram[rows, :] = column[number, rank:, :].astype(F32)
+    polish(ckpt_count, [(gram, product, spare, other), (left_gram, left_product, left_spare, left_other)])
+    for index in range(ckpt_count):
+        rows = pl.ds(index * rank, rank)
+        left_spare[rows, :] = dot_wide(jnp.transpose(middle[index]), left_product[rows, :])
+    other[...] = dot_wide(product[...], left_spare[...]).astype(BF16)
+
+    right_load.wait()
     size = pieces.shape[2]
     wide[...] = jnp.zeros_like(wide)
     for slot in range(count):
         start = min(slot * size, real - size)
         wide[:, start:start + size] += pieces[slot]
-    polish(ckpt_count, [(gram, product, spare, other), (left_gram, left_product, left_spare, left_other)])
-    for index in range(ckpt_count):
-        rows = pl.ds(index * rank, rank)
-        left_spare[rows, :] = dot_wide(jnp.transpose(middle[index]), left_product[rows, :])
-    other[...] = dot_wide(product[...], left_spare[...]).astype(BF16)
-
     load.wait()
     copies = []
     for number in range(strips.shape[0]):
@@ -471,15 +474,17 @@
 
     step = min(256, rows)
     vmem = pl.BlockSpec(memory_space=pltpu.VMEM)
-    args = [in_hbm, middles, *columns, gathered]
+    args = [in_hbm, pltpu.with_memory_space_constraint(gathered, pltpu.HBM), middles, *columns]
     return pl.pallas_call(
         functools.partial(merge_kernel, count, groups),
-        in_specs=[pl.BlockSpec(memory_space=pltpu.SMEM), pl.BlockSpec(memory_space=pltpu.HBM)] + [vmem] * (len(args) - 1),
+        in_specs=[pl.BlockSpec(memory_space=pltpu.SMEM)] + [pl.BlockSpec(memory_space=pltpu.HBM)] * 2
+        + [vmem] * (len(args) - 2),
         out_specs=pl.BlockSpec(memory_space=pl.ANY),
         out_shape=shape((rows, block), BF16),
         scratch_shapes=[pltpu.VMEM((size, size), F32)] * 6 + [pltpu.VMEM((size, size), BF16)] * 2
         + [pltpu.VMEM((size, block), BF16), pltpu.VMEM((rows // step, step, block), BF16),
-           pltpu.VMEM(left_stack.shape, BF16), pltpu.SemaphoreType.DMA(()), pltpu.SemaphoreType.DMA((rows // step,))],
+           pltpu.VMEM(left_stack.shape, BF16), pltpu.SemaphoreType.DMA(()), pltpu.SemaphoreType.DMA((rows // step,)),
+           pltpu.VMEM(gathered.shape, BF16), pltpu.SemaphoreType.DMA(())],
         compiler_params=pltpu.CompilerParams(vmem_limit_bytes=2 * VMEM_BYTES),
         name="merge",
         cost_estimate=SHORT,

time: 216 us -> 214 us (level)
    unnamed x10 -> x8, local copies, waits for them, and re-layouts: 12 us -> 10.4 us
where the time goes in v4:
time: 214 us
  waiting for transfers between devices  74.2 us (35%)
  Pallas kernels  63.6 us (30%)
  starting transfers between devices  49.7 us (23%)
  between operations  14.3 us (7%)
  local copies, waits for them, and re-layouts  10.5 us (5%)
    ppermute x38, waiting for transfers between devices, permute(): lax.ppermute(value, axis, [(source, source ^ gap) for source in range(cou...  72.3 us
    ppermute x38, starting transfers between devices, permute(): lax.ppermute(value, axis, [(source, source ^ gap) for source in range(cou...  49.5 us
    pallas_call x14, Pallas kernels, delta_call(): pl.pallas_call(kernel, in_specs=[pl.BlockSpec(memory_space=pltpu.SMEM)] +...  40.6 us
    pallas_call x1, Pallas kernels, body(): pl.pallas_call(functools.partial(merge_kernel, count, groups), in_specs=[...  13 us
    unnamed x8, local copies, waits for them, and re-layouts  10.4 us
    pallas_call x3, Pallas kernels, small_call(): pl.pallas_call(kernel, in_specs=[spec(i) for i in range(len(args))], out_...  10 us
  transfers between devices with their start and end apart: 40, of which 28 were waited for; matrix products, arithmetic and copies ran while one was open for 0% of the time, Pallas kernels for 16%

profile of v4, /device:TPU:0, one launch (start us, length us, event | category | flops | bytes accessed | tf_op | source)
XLA Modules:
  0.0 213.6 jit_solution(14032824552306519121)
XLA Ops:
  6.5 3.0 %collective-permute-start.1 = (bf16[64,3584]{1,0:T(8,128)(2,1)}, bf16[64,3584]{1,0:T(8,128)(2,1)S(1)}, u32[]{:S(2)}, u32[]{:S(2)}) collective-permute-start(bf16[64,3584]{1,0:T(8,128)(2,1)} %bitcast.37), channel_id=1, source_target_pairs={{0,2},{1,3},{2,0},{3,1},{4,6},{5,7},{6,4},{7,5},{8,10},{9,11},{10,... | collective-permute-start | bytes 1376264 | tf_op jit(solution)/shard_map/ppermute | solution.py:355
  11.0 9.3 %copy-done = bf16[1,1024,14336]{2,1,0:T(8,128)(2,1)S(1)} copy-done((bf16[1,1024,14336]{2,1,0:T(8,128)(2,1)S(1)}, bf16[1,1024,14336]{2,1,0:T(8,128)(2,1)}, u32[]{:S(2)}) %copy-start) | copy-done | bytes 29360152
  24.4 4.6 %first_left_part.3.refs_4_ = f32[64,1024]{1,0:T(8,128)S(1)} custom-call(s32[1]{0:T(128)} %bitcast.1.place_ref, bf16[1024,14336]{1,0:T(8,128)(2,1)S(1)} %bitcast.24, bf16[64,3584]{1,0:T(8,128)(2,1)S(1)} %collective-permute-done.refs_0_.refs_1_, bf16[64,3584]{1,0:T(8,128)(2,1)S(1)} %collective-permute-done.1.refs_1_.refs_2_, f32[64,1024]{1,0:T(8,128)S(1)} %first_left_part.2.refs_2_), custom_call_target="tpu_custom_call" | custom-call | flops 1024 | bytes 1024 | tf_op jit(solution)/shard_map/first_left_part/pallas_call | solution.py:134
  41.1 9.5 %collective-permute-done.4 = bf16[64,3584]{1,0:T(8,128)(2,1)S(1)} collective-permute-done((bf16[64,3584]{1,0:T(8,128)(2,1)S(1)}, bf16[64,3584]{1,0:T(8,128)(2,1)S(1)}, u32[]{:S(2)}, u32[]{:S(2)}) %collective-permute-start.4) | collective-permute-done | bytes 458784 | tf_op jit(solution)/shard_map/ppermute | solution.py:355
  51.9 4.8 %collective-permute-done.5 = bf16[64,3584]{1,0:T(8,128)(2,1)S(1)} collective-permute-done((bf16[64,3584]{1,0:T(8,128)(2,1)S(1)}, bf16[64,3584]{1,0:T(8,128)(2,1)S(1)}, u32[]{:S(2)}, u32[]{:S(2)}) %collective-permute-start.5) | collective-permute-done | bytes 458784 | tf_op jit(solution)/shard_map/ppermute | solution.py:355
  62.2 7.9 %collective-permute-done.8.refs_1_.refs_2_ = bf16[64,3584]{1,0:T(8,128)(2,1)S(1)} collective-permute-done((bf16[64,3584]{1,0:T(8,128)(2,1)S(1)}, bf16[64,3584]{1,0:T(8,128)(2,1)S(1)}, u32[]{:S(2)}, u32[]{:S(2)}) %collective-permute-start.8) | collective-permute-done | bytes 458784 | tf_op jit(solution)/shard_map/ppermute | solution.py:355
  73.4 4.7 %second_left_part.3.refs_4_ = f32[64,1024]{1,0:T(8,128)S(1)} custom-call(s32[1]{0:T(128)} %bitcast.1.place_ref, bf16[1024,14336]{1,0:T(8,128)(2,1)S(1)} %bitcast.31, bf16[64,3584]{1,0:T(8,128)(2,1)S(1)} %collective-permute-done.7.refs_0_.refs_1_, bf16[64,3584]{1,0:T(8,128)(2,1)S(1)} %collective-permute-done.8.refs_1_.refs_2_, ...), custom_call_target="tpu_custom_call" | custom-call | flops 1024 | bytes 1024 | tf_op jit(solution)/shard_map/second_left_part/pallas_call | solution.py:134
  78.3 7.6 %second_left.1 = (bf16[64,1024]{1,0:T(8,128)(2,1)S(1)}, f32[64,64]{1,0:T(8,128)S(1)}) custom-call(s32[1]{0:T(128)} %bitcast.1.place_ref, bf16[1024,14336]{1,0:T(8,128)(2,1)S(1)} %bitcast.32, bf16[64,3584]{1,0:T(8,128)(2,1)S(1)} %add_convert_fusion.refs_0_, bf16[64,3584]{1,0:T(8,128)(2,1)S(1)} %collective-permute-done.7.refs_0_.refs_1_, ...), custom_call_target="tpu_custom_call" | custom-call | flops 1024 | bytes 1024 | tf_op jit(solution)/shard_map/second_left/pallas_call | solution.py:134
  98.2 8.6 %collective-permute-done.14.refs_3_ = bf16[8,64,512]{2,1,0:T(8,128)(2,1)S(1)} collective-permute-done((bf16[8,64,512]{2,1,0:T(8,128)(2,1)S(1)}, bf16[8,64,512]{2,1,0:T(8,128)(2,1)S(1)}, u32[]{:S(2)}, u32[]{:S(2)}) %collective-permute-start.14) | collective-permute-done | bytes 524320 | tf_op jit(solution)/shard_map/ppermute | solution.py:355
  106.8 6.5 %second_own.1 = (bf16[8,64,512]{2,1,0:T(8,128)(2,1)S(1)}, bf16[64,1024]{1,0:T(8,128)(2,1)}, f32[64,64]{1,0:T(8,128)S(1)}) custom-call(s32[1]{0:T(128)} %bitcast.1.place_ref, bf16[1024,14336]{1,0:T(8,128)(2,1)S(1)} %bitcast.36, bf16[64,1024]{1,0:T(8,128)(2,1)S(1)} %get-tuple-element.97.left, f32[64,64]{1,0:T(8,128)S(1)} %get-tuple-element.98.refs_0_, ...), custom_call_target="tpu_custom_call" | custom-call | flops 1024 | bytes 1024 | tf_op jit(solution)/shard_map/second_own/pallas_call | solution.py:134
  121.6 6.1 %right_unit.1 = (bf16[64,640]{1,0:T(8,128)(2,1)S(1)}, bf16[64,640]{1,0:T(8,128)(2,1)S(1)}, bf16[64,640]{1,0:T(8,128)(2,1)S(1)}, bf16[64,640]{1,0:T(8,128)(2,1)S(...) custom-call(s32[1]{0:T(128)} %bitcast.place_ref, ...), custom_call_target="tpu_custom_call" | custom-call | flops 1024 | bytes 1024 | tf_op jit(solution)/shard_map/right_unit/pallas_call | solution.py:212
  129.7 2.6 %collective-permute-start.23 = (bf16[64,640]{1,0:T(8,128)(2,1)S(1)}, bf16[64,640]{1,0:T(8,128)(2,1)S(1)}, u32[]{:S(2)}, u32[]{:S(2)}) collective-permute-start(bf16[64,640]{1,0:T(8,128)(2,1)S(1)} %get-tuple-element.118), channel_id=1, source_target_pairs={{0,16},{4,20},{8,24},{12,28},{16,0},{20,4},{24,8},{28,12},{1,17},{... | collective-permute-start | bytes 245768 | tf_op jit(solution)/shard_map/ppermute | solution.py:355
  132.3 3.6 %collective-permute-start.25 = (bf16[64,640]{1,0:T(8,128)(2,1)S(1)}, bf16[64,640]{1,0:T(8,128)(2,1)S(1)}, u32[]{:S(2)}, u32[]{:S(2)}) collective-permute-start(bf16[64,640]{1,0:T(8,128)(2,1)S(1)} %get-tuple-element.120), channel_id=1, source_target_pairs={{0,24},{4,28},{8,16},{12,20},{16,8},{20,12},{24,0},{28,4},{1,25},{... | collective-permute-start | bytes 245768 | tf_op jit(solution)/shard_map/ppermute | solution.py:355
  135.9 3.4 %collective-permute-done.21.refs_2_ = bf16[64,640]{1,0:T(8,128)(2,1)S(1)} collective-permute-done((bf16[64,640]{1,0:T(8,128)(2,1)S(1)}, bf16[64,640]{1,0:T(8,128)(2,1)S(1)}, u32[]{:S(2)}, u32[]{:S(2)}) %collective-permute-start.21) | collective-permute-done | bytes 81952 | tf_op jit(solution)/shard_map/ppermute | solution.py:355
  141.5 2.4 %collective-permute-done.24.refs_5_ = bf16[64,640]{1,0:T(8,128)(2,1)S(1)} collective-permute-done((bf16[64,640]{1,0:T(8,128)(2,1)S(1)}, bf16[64,640]{1,0:T(8,128)(2,1)S(1)}, u32[]{:S(2)}, u32[]{:S(2)}) %collective-permute-start.24) | collective-permute-done | bytes 81952 | tf_op jit(solution)/shard_map/ppermute | solution.py:355
  145.6 3.3 %grams.1 = (bf16[512,512]{1,0:T(8,128)(2,1)}, f32[8,64,64]{2,1,0:T(8,128)S(1)}, bf16[4,64,512]{2,1,0:T(8,128)(2,1)S(1)}, bf16[4,64,512]{2,1,0:T(8,128)(2,1)S(1)}, bf16[64,512]{1,0:T(8,128)(2,1)S(1)}) custom-call(s32[1]{0:T(128)} %bitcast.place_ref, bf16[512,1024]{1,0:T(8,128)(2,1)} %all-gather.4.cloned.1.call-done.left_hbm, ...), custom_call_target="tpu_custom_call" | custom-call | flops 1024 | bytes 1024 | tf_op jit(solution)/shard_map/grams/pallas_call | solution.py:212
  150.7 4.1 %collective-permute-start.28 = (bf16[64,512]{1,0:T(8,128)(2,1)S(1)}, bf16[64,512]{1,0:T(8,128)(2,1)S(1)}, u32[]{:S(2)}, u32[]{:S(2)}) collective-permute-start(bf16[64,512]{1,0:T(8,128)(2,1)S(1)} %get-tuple-element.127), channel_id=1, source_target_pairs={{0,8},{4,12},{8,0},{12,4},{16,24},{20,28},{24,16},{28,20},{1,9},{5... | collective-permute-start | bytes 196616 | tf_op jit(solution)/shard_map/ppermute | solution.py:355
  157.2 4.4 %collective-permute-done.30 = bf16[64,512]{1,0:T(8,128)(2,1)S(1)} collective-permute-done((bf16[64,512]{1,0:T(8,128)(2,1)S(1)}, bf16[64,512]{1,0:T(8,128)(2,1)S(1)}, u32[]{:S(2)}, u32[]{:S(2)}) %collective-permute-start.30) | collective-permute-done | bytes 65568 | tf_op jit(solution)/shard_map/ppermute | solution.py:355
  163.7 2.9 %collective-permute-start.32 = (bf16[128,512]{1,0:T(8,128)(2,1)S(1)}, bf16[128,512]{1,0:T(8,128)(2,1)S(1)}, u32[]{:S(2)}, u32[]{:S(2)}) collective-permute-start(bf16[128,512]{1,0:T(8,128)(2,1)S(1)} %pad_maximum_fusion.3), channel_id=1, source_target_pairs={{0,2},{1,3},{2,0},{3,1},{4,6},{5,7},{6,4},{7,5},{8,10},{9,11},{10,... | collective-permute-start | bytes 393224 | tf_op jit(solution)/shard_map/ppermute | solution.py:355
  168.1 3.6 %collective-permute-done.32 = bf16[128,512]{1,0:T(8,128)(2,1)S(1)} collective-permute-done((bf16[128,512]{1,0:T(8,128)(2,1)S(1)}, bf16[128,512]{1,0:T(8,128)(2,1)S(1)}, u32[]{:S(2)}, u32[]{:S(2)}) %collective-permute-start.32) | collective-permute-done | bytes 131104 | tf_op jit(solution)/shard_map/ppermute | solution.py:355
  175.2 3.4 %collective-permute-start.36 = (bf16[128,512]{1,0:T(8,128)(2,1)S(1)}, bf16[128,512]{1,0:T(8,128)(2,1)S(1)}, u32[]{:S(2)}, u32[]{:S(2)}) collective-permute-start(bf16[128,512]{1,0:T(8,128)(2,1)S(1)} %add_convert_fusion.2), channel_id=1, source_target_pairs={{0,24},{4,28},{8,16},{12,20},{16,8},{20,12},{24,0},{28,4},{1,25},{... | collective-permute-start | bytes 393224 | tf_op jit(solution)/shard_map/ppermute | solution.py:355
  179.7 3.9 %collective-permute-done.36 = bf16[128,512]{1,0:T(8,128)(2,1)S(1)} collective-permute-done((bf16[128,512]{1,0:T(8,128)(2,1)S(1)}, bf16[128,512]{1,0:T(8,128)(2,1)S(1)}, u32[]{:S(2)}, u32[]{:S(2)}) %collective-permute-start.36) | collective-permute-done | bytes 131104 | tf_op jit(solution)/shard_map/ppermute | solution.py:355
  183.5 6.3 %collective-permute-done.35 = bf16[128,512]{1,0:T(8,128)(2,1)S(1)} collective-permute-done((bf16[128,512]{1,0:T(8,128)(2,1)S(1)}, bf16[128,512]{1,0:T(8,128)(2,1)S(1)}, u32[]{:S(2)}, u32[]{:S(2)}) %collective-permute-start.35) | collective-permute-done | bytes 131104 | tf_op jit(solution)/shard_map/ppermute | solution.py:355
  193.7 13.0 %merge.1 = bf16[1024,1792]{1,0:T(8,128)(2,1)} custom-call(s32[2]{0:T(128)S(1)} %pad_add_fusion.places_ref, bf16[512,1024]{1,0:T(8,128)(2,1)} %all-gather.4.cloned.1.call-done.left_hbm, bf16[4,512,512]{2,1,0:T(8,128)(2,1)} %bitcast.41, f32[8,64,64]{2,1,0:T(8,128)S(1)} %get-tuple-element.123.middle, bf16[4,128,512]{2,1,0:T(8,128)(2,1)S(1)} %pad_maximum_fusion.refs_0_, ...), custom_call_target="tpu_custom_call" | custom-call | flops 1024 | bytes 1024 | tf_op jit(solution)/shard_map/merge/pallas_call | solution.py:478
  (99 shorter events, 69.9 us)
Async XLA Ops:
  6.5 139.1 %all-gather.4.cloned.1.call-start = ((), (), s32[]{:S(2)}) async-start(), calls=%async_computation | async-start | bytes 1179648 | tf_op jit(solution)/shard_map/all_gather | solution.py:447
  6.5 17.2 %collective-permute-start.1 = (bf16[64,3584]{1,0:T(8,128)(2,1)}, bf16[64,3584]{1,0:T(8,128)(2,1)S(1)}, u32[]{:S(2)}, u32[]{:S(2)}) collective-permute-start(bf16[64,3584]{1,0:T(8,128)(2,1)} %bitcast.37), channel_id=1, source_target_pairs={{0,2},{1,3},{2,0},{3,1},{4,6},{5,7},{6,4},{7,5},{8,10},{9,11},{10,... | collective-permute-start | bytes 1376264 | tf_op jit(solution)/shard_map/ppermute | solution.py:355
  9.5 14.2 %collective-permute-start = (bf16[64,3584]{1,0:T(8,128)(2,1)}, bf16[64,3584]{1,0:T(8,128)(2,1)S(1)}, u32[]{:S(2)}, u32[]{:S(2)}) collective-permute-start(bf16[64,3584]{1,0:T(8,128)(2,1)} %bitcast.38), channel_id=1, source_target_pairs={{0,1},{1,0},{2,3},{3,2},{4,5},{5,4},{6,7},{7,6},{8,9},{9,8},{10,11... | collective-permute-start | bytes 1376264 | tf_op jit(solution)/shard_map/ppermute | solution.py:355
  23.8 6.8 %collective-permute-start.2 = (bf16[32,3584]{1,0:T(8,128)(2,1)S(1)}, bf16[32,3584]{1,0:T(8,128)(2,1)S(1)}, u32[]{:S(2)}, u32[]{:S(2)}) collective-permute-start(bf16[32,3584]{1,0:T(8,128)(2,1)S(1)} %slice.24), channel_id=1, source_target_pairs={{0,1},{1,0},{2,3},{3,2},{4,5},{5,4},{6,7},{7,6},{8,9},{9,8},{10,11... | collective-permute-start | bytes 688136 | tf_op jit(solution)/shard_map/ppermute | solution.py:355
  36.1 14.5 %collective-permute-start.4 = (bf16[64,3584]{1,0:T(8,128)(2,1)S(1)}, bf16[64,3584]{1,0:T(8,128)(2,1)S(1)}, u32[]{:S(2)}, u32[]{:S(2)}) collective-permute-start(bf16[64,3584]{1,0:T(8,128)(2,1)S(1)} %first_right.4), channel_id=1, source_target_pairs={{0,3},{1,2},{2,1},{3,0},{4,7},{5,6},{6,5},{7,4},{8,11},{9,10},{10,... | collective-permute-start | bytes 1376264 | tf_op jit(solution)/shard_map/ppermute | solution.py:355
  39.0 17.7 %collective-permute-start.5 = (bf16[64,3584]{1,0:T(8,128)(2,1)S(1)}, bf16[64,3584]{1,0:T(8,128)(2,1)S(1)}, u32[]{:S(2)}, u32[]{:S(2)}) collective-permute-start(bf16[64,3584]{1,0:T(8,128)(2,1)S(1)} %first_right.6), channel_id=1, source_target_pairs={{0,1},{1,0},{2,3},{3,2},{4,5},{5,4},{6,7},{7,6},{8,9},{9,8},{10,11... | collective-permute-start | bytes 1376264 | tf_op jit(solution)/shard_map/ppermute | solution.py:355
  39.4 18.0 %collective-permute-start.6 = (bf16[64,3584]{1,0:T(8,128)(2,1)S(1)}, bf16[64,3584]{1,0:T(8,128)(2,1)S(1)}, u32[]{:S(2)}, u32[]{:S(2)}) collective-permute-start(bf16[64,3584]{1,0:T(8,128)(2,1)S(1)} %first_right.5), channel_id=1, source_target_pairs={{0,2},{1,3},{2,0},{3,1},{4,6},{5,7},{6,4},{7,5},{8,10},{9,11},{10,... | collective-permute-start | bytes 1376264 | tf_op jit(solution)/shard_map/ppermute | solution.py:355
  57.6 12.5 %collective-permute-start.8 = (bf16[64,3584]{1,0:T(8,128)(2,1)S(1)}, bf16[64,3584]{1,0:T(8,128)(2,1)S(1)}, u32[]{:S(2)}, u32[]{:S(2)}) collective-permute-start(bf16[64,3584]{1,0:T(8,128)(2,1)S(1)} %add_convert_fusion.refs_0_), channel_id=1, source_target_pairs={{0,2},{1,3},{2,0},{3,1},{4,6},{5,7},{6,4},{7,5},{8,10},{9,11},{10,... | collective-permute-start | bytes 1376264 | tf_op jit(solution)/shard_map/ppermute | solution.py:355
  58.4 12.2 %collective-permute-start.7 = (bf16[64,3584]{1,0:T(8,128)(2,1)S(1)}, bf16[64,3584]{1,0:T(8,128)(2,1)S(1)}, u32[]{:S(2)}, u32[]{:S(2)}) collective-permute-start(bf16[64,3584]{1,0:T(8,128)(2,1)S(1)} %add_convert_fusion.refs_0_), channel_id=1, source_target_pairs={{0,1},{1,0},{2,3},{3,2},{4,5},{5,4},{6,7},{7,6},{8,9},{9,8},{10,11... | collective-permute-start | bytes 1376264 | tf_op jit(solution)/shard_map/ppermute | solution.py:355
  70.6 7.5 %collective-permute-start.9 = (bf16[32,3584]{1,0:T(8,128)(2,1)S(1)}, bf16[32,3584]{1,0:T(8,128)(2,1)S(1)}, u32[]{:S(2)}, u32[]{:S(2)}) collective-permute-start(bf16[32,3584]{1,0:T(8,128)(2,1)S(1)} %slice.26), channel_id=1, source_target_pairs={{0,1},{1,0},{2,3},{3,2},{4,5},{5,4},{6,7},{7,6},{8,9},{9,8},{10,11... | collective-permute-start | bytes 688136 | tf_op jit(solution)/shard_map/ppermute | solution.py:355
  90.9 15.9 %collective-permute-start.14 = (bf16[8,64,512]{2,1,0:T(8,128)(2,1)S(1)}, bf16[8,64,512]{2,1,0:T(8,128)(2,1)S(1)}, u32[]{:S(2)}, u32[]{:S(2)}) collective-permute-start(bf16[8,64,512]{2,1,0:T(8,128)(2,1)S(1)} %second_right.3), channel_id=1, source_target_pairs={{0,3},{1,2},{2,1},{3,0},{4,7},{5,6},{6,5},{7,4},{8,11},{9,10},{10,... | collective-permute-start | bytes 1572872 | tf_op jit(solution)/shard_map/ppermute | solution.py:355
  95.5 18.5 %collective-permute-start.15 = (bf16[8,64,512]{2,1,0:T(8,128)(2,1)S(1)}, bf16[8,64,512]{2,1,0:T(8,128)(2,1)S(1)}, u32[]{:S(2)}, u32[]{:S(2)}) collective-permute-start(bf16[8,64,512]{2,1,0:T(8,128)(2,1)S(1)} %second_right.5), channel_id=1, source_target_pairs={{0,1},{1,0},{2,3},{3,2},{4,5},{5,4},{6,7},{7,6},{8,9},{9,8},{10,11... | collective-permute-start | bytes 1572872 | tf_op jit(solution)/shard_map/ppermute | solution.py:355
  97.0 17.7 %collective-permute-start.16 = (bf16[8,64,512]{2,1,0:T(8,128)(2,1)S(1)}, bf16[8,64,512]{2,1,0:T(8,128)(2,1)S(1)}, u32[]{:S(2)}, u32[]{:S(2)}) collective-permute-start(bf16[8,64,512]{2,1,0:T(8,128)(2,1)S(1)} %second_right.4), channel_id=1, source_target_pairs={{0,2},{1,3},{2,0},{3,1},{4,6},{5,7},{6,4},{7,5},{8,10},{9,11},{10,... | collective-permute-start | bytes 1572872 | tf_op jit(solution)/shard_map/ppermute | solution.py:355
  114.7 79.0 %all-gather.6.cloned.1.call-start = ((), (), s32[]{:S(2)}) async-start(), calls=%async_computation.1 | async-start | bytes 2621440 | tf_op jit(solution)/shard_map/all_gather | solution.py:469
  127.8 11.5 %collective-permute-start.21 = (bf16[64,640]{1,0:T(8,128)(2,1)S(1)}, bf16[64,640]{1,0:T(8,128)(2,1)S(1)}, u32[]{:S(2)}, u32[]{:S(2)}) collective-permute-start(bf16[64,640]{1,0:T(8,128)(2,1)S(1)} %get-tuple-element.116), channel_id=1, source_target_pairs={{0,8},{4,12},{8,0},{12,4},{16,24},{20,28},{24,16},{28,20},{1,9},{5... | collective-permute-start | bytes 245768 | tf_op jit(solution)/shard_map/ppermute | solution.py:355
  129.5 12.0 %collective-permute-start.22 = (bf16[64,640]{1,0:T(8,128)(2,1)S(1)}, bf16[64,640]{1,0:T(8,128)(2,1)S(1)}, u32[]{:S(2)}, u32[]{:S(2)}) collective-permute-start(bf16[64,640]{1,0:T(8,128)(2,1)S(1)} %get-tuple-element.117), channel_id=1, source_target_pairs={{0,12},{4,8},{8,4},{12,0},{16,28},{20,24},{24,20},{28,16},{1,13},{... | collective-permute-start | bytes 245768 | tf_op jit(solution)/shard_map/ppermute | solution.py:355
  129.7 11.8 %collective-permute-start.23 = (bf16[64,640]{1,0:T(8,128)(2,1)S(1)}, bf16[64,640]{1,0:T(8,128)(2,1)S(1)}, u32[]{:S(2)}, u32[]{:S(2)}) collective-permute-start(bf16[64,640]{1,0:T(8,128)(2,1)S(1)} %get-tuple-element.118), channel_id=1, source_target_pairs={{0,16},{4,20},{8,24},{12,28},{16,0},{20,4},{24,8},{28,12},{1,17},{... | collective-permute-start | bytes 245768 | tf_op jit(solution)/shard_map/ppermute | solution.py:355
  132.3 11.6 %collective-permute-start.24 = (bf16[64,640]{1,0:T(8,128)(2,1)S(1)}, bf16[64,640]{1,0:T(8,128)(2,1)S(1)}, u32[]{:S(2)}, u32[]{:S(2)}) collective-permute-start(bf16[64,640]{1,0:T(8,128)(2,1)S(1)} %get-tuple-element.119), channel_id=1, source_target_pairs={{0,20},{4,16},{8,28},{12,24},{16,4},{20,0},{24,12},{28,8},{1,21},{... | collective-permute-start | bytes 245768 | tf_op jit(solution)/shard_map/ppermute | solution.py:355
  132.3 11.6 %collective-permute-start.25 = (bf16[64,640]{1,0:T(8,128)(2,1)S(1)}, bf16[64,640]{1,0:T(8,128)(2,1)S(1)}, u32[]{:S(2)}, u32[]{:S(2)}) collective-permute-start(bf16[64,640]{1,0:T(8,128)(2,1)S(1)} %get-tuple-element.120), channel_id=1, source_target_pairs={{0,24},{4,28},{8,16},{12,20},{16,8},{20,12},{24,0},{28,4},{1,25},{... | collective-permute-start | bytes 245768 | tf_op jit(solution)/shard_map/ppermute | solution.py:355
  163.7 8.0 %collective-permute-start.32 = (bf16[128,512]{1,0:T(8,128)(2,1)S(1)}, bf16[128,512]{1,0:T(8,128)(2,1)S(1)}, u32[]{:S(2)}, u32[]{:S(2)}) collective-permute-start(bf16[128,512]{1,0:T(8,128)(2,1)S(1)} %pad_maximum_fusion.3), channel_id=1, source_target_pairs={{0,2},{1,3},{2,0},{3,1},{4,6},{5,7},{6,4},{7,5},{8,10},{9,11},{10,... | collective-permute-start | bytes 393224 | tf_op jit(solution)/shard_map/ppermute | solution.py:355
  167.8 7.3 %collective-permute-start.33 = (bf16[128,512]{1,0:T(8,128)(2,1)S(1)}, bf16[128,512]{1,0:T(8,128)(2,1)S(1)}, u32[]{:S(2)}, u32[]{:S(2)}) collective-permute-start(bf16[128,512]{1,0:T(8,128)(2,1)S(1)} %pad_maximum_fusion.3), channel_id=1, source_target_pairs={{0,3},{1,2},{2,1},{3,0},{4,7},{5,6},{6,5},{7,4},{8,11},{9,10},{10,... | collective-permute-start | bytes 393224 | tf_op jit(solution)/shard_map/ppermute | solution.py:355
  175.2 8.3 %collective-permute-start.36 = (bf16[128,512]{1,0:T(8,128)(2,1)S(1)}, bf16[128,512]{1,0:T(8,128)(2,1)S(1)}, u32[]{:S(2)}, u32[]{:S(2)}) collective-permute-start(bf16[128,512]{1,0:T(8,128)(2,1)S(1)} %add_convert_fusion.2), channel_id=1, source_target_pairs={{0,24},{4,28},{8,16},{12,20},{16,8},{20,12},{24,0},{28,4},{1,25},{... | collective-permute-start | bytes 393224 | tf_op jit(solution)/shard_map/ppermute | solution.py:355
  178.6 11.2 %collective-permute-start.35 = (bf16[128,512]{1,0:T(8,128)(2,1)S(1)}, bf16[128,512]{1,0:T(8,128)(2,1)S(1)}, u32[]{:S(2)}, u32[]{:S(2)}) collective-permute-start(bf16[128,512]{1,0:T(8,128)(2,1)S(1)} %add_convert_fusion.2), channel_id=1, source_target_pairs={{0,16},{4,20},{8,24},{12,28},{16,0},{20,4},{24,8},{28,12},{1,17},{... | collective-permute-start | bytes 393224 | tf_op jit(solution)/shard_map/ppermute | solution.py:355
  178.6 11.2 %collective-permute-start.34 = (bf16[128,512]{1,0:T(8,128)(2,1)S(1)}, bf16[128,512]{1,0:T(8,128)(2,1)S(1)}, u32[]{:S(2)}, u32[]{:S(2)}) collective-permute-start(bf16[128,512]{1,0:T(8,128)(2,1)S(1)} %add_convert_fusion.2), channel_id=1, source_target_pairs={{0,8},{4,12},{8,0},{12,4},{16,24},{20,28},{24,16},{28,20},{1,9},{5... | collective-permute-start | bytes 393224 | tf_op jit(solution)/shard_map/ppermute | solution.py:355
  (20 other events, 123.7 us)
Sparse Core Ops, SparseCore 0:
  114.8 27.2 all-gather.3
  149.1 44.6 all-gather.5
